TPU v7x, 32 devices: a whole 2x2x4 slice. The times are simulated.
32 devices in a mesh: res: 16 (over z, y, x), half: 2 (over core).
Axes of the slice: x: 2, y: 2, z: 4, core: 2. Of those that a mesh axis runs over, the one named last changes fastest.
Arguments:
- nodes: bfloat16 [1536, 512], P('res'), may hold values from -6 to 6
- edges: bfloat16 [1536, 60, 192], P('res'), may hold values from -6 to 6
- neighbours: int32 [1536, 60], P('res'), may hold values from 0 to 1535, as said below
- counts: int32 [1536], P('res'), may hold values from 30 to 60, as said below
- message_first: bfloat16 [1216, 512], replicated, may hold values from -0.15625 to 0.15625
- message_first_bias: bfloat16 [512], replicated, may hold values from -3 to 3
- message_second: bfloat16 [512, 512], replicated, may hold values from -0.25 to 0.25
- message_second_bias: bfloat16 [512], replicated, may hold values from -3 to 3
- message_third: bfloat16 [512, 512], replicated, may hold values from -0.75 to 0.75
- message_third_bias: bfloat16 [512], replicated, may hold values from -2 to 2
- node_norm_gain: bfloat16 [512], replicated, may hold values from 0.5 to 1.5
- node_norm_shift: bfloat16 [512], replicated, may hold values from -2 to 2
- expand_weight: bfloat16 [512, 2048], replicated, may hold values from -0.25 to 0.25
- expand_bias: bfloat16 [2048], replicated, may hold values from -3 to 3
- reduce_weight: bfloat16 [2048, 512], replicated, may hold values from -0.25 to 0.25
- reduce_bias: bfloat16 [512], replicated, may hold values from -2 to 2
- output_norm_gain: bfloat16 [512], replicated, may hold values from 0.5 to 1.5
- output_norm_shift: bfloat16 [512], replicated, may hold values from -2 to 2
- edge_first: bfloat16 [1216, 192], replicated, may hold values from -0.15625 to 0.15625
- edge_first_bias: bfloat16 [192], replicated, may hold values from -3 to 3
- edge_second: bfloat16 [192, 192], replicated, may hold values from -0.4375 to 0.4375
- edge_second_bias: bfloat16 [192], replicated, may hold values from -3 to 3
- edge_third: bfloat16 [192, 192], replicated, may hold values from -0.875 to 0.875
- edge_third_bias: bfloat16 [192], replicated, may hold values from -2 to 2
- edge_norm_gain: bfloat16 [192], replicated, may hold values from 0.5 to 1.5
- edge_norm_shift: bfloat16 [192], replicated, may hold values from -2 to 2
- cot_nodes: bfloat16 [1536, 512], P('res'), may hold values from -6 to 6
- cot_edges: bfloat16 [1536, 60, 192], P('res'), may hold values from -6 to 6
Outputs:
- nodes_out: bfloat16 [1536, 512], P('res', 'half')
- edges_out: bfloat16 [1536, 60, 192], P('res', 'half')
- fed_grad: float32 [1536, 512], P('res', 'half')
- edges_grad: float32 [1536, 60, 192], P('res', 'half')
- message_first_grad: float32 [1216, 512], P('half')
- message_first_bias_grad: float32 [512], P('half')
- message_second_grad: float32 [512, 512], P('half')
- message_second_bias_grad: float32 [512], P('half')
- message_third_grad: float32 [512, 512], P('half')
- message_third_bias_grad: float32 [512], P('half')
- node_norm_gain_grad: float32 [512], P('half')
- node_norm_shift_grad: float32 [512], P('half')
- expand_weight_grad: float32 [512, 2048], P('half')
- expand_bias_grad: float32 [2048], P('half')
- reduce_weight_grad: float32 [2048, 512], P('half')
- reduce_bias_grad: float32 [512], P('half')
- output_norm_gain_grad: float32 [512], P('half')
- output_norm_shift_grad: float32 [512], P('half')
- edge_first_grad: float32 [1216, 192], P('half')
- edge_first_bias_grad: float32 [192], P('half')
- edge_second_grad: float32 [192, 192], P('half')
- edge_second_bias_grad: float32 [192], P('half')
- edge_third_grad: float32 [192, 192], P('half')
- edge_third_bias_grad: float32 [192], P('half')
- edge_norm_gain_grad: float32 [192], P('half')
- edge_norm_shift_grad: float32 [192], P('half')
Inputs may be any that keep to these rules, and one draw needn't show every extreme that they name: `neighbours`: residues form contiguous proteins of 256 to 1024 residues (the last one may be shorter); the first begins at residue 0 and every other begins at a residue whose index is 96 // 2 modulo 96. Every slot names a residue of the same protein at most 64 positions away from residue i; only the first counts[i] slots of residue i are used. Residue i uses slots 0 to counts[i] - 1.
All inputs are finite; a program needn't handle non-finite values.
Results may differ from a plain program's by a relative error of at most 0.025.
Values may be sent and summed in bfloat16 or wider, within the bound.
A program may use at most 320 MiB of HBM per device.

v0:
```python
import jax
import jax.numpy as jnp
from jax import lax
from jax.sharding import PartitionSpec as P

EPSILON = 1e-05
PRECISE = lax.Precision.HIGHEST


def with_halo(block, sides, width):
    for axis, dim in sides:
        count = lax.axis_size(axis)
        forward = [(i, i + 1) for i in range(count - 1)]
        backward = [(target, source) for source, target in forward]
        low = lax.ppermute(
            lax.slice_in_dim(block, block.shape[dim] - width, None, axis=dim), axis, forward
        )
        high = lax.ppermute(lax.slice_in_dim(block, 0, width, axis=dim), axis, backward)
        block = jnp.concatenate([low, block, high], axis=dim)
    return block


def from_behind(block, axis, distance):
    devices = range(lax.axis_size(axis))
    route = [(i - distance, i) for i in devices if i - distance in devices]
    return lax.ppermute(block, axis, route)


def broadcast(block, axis, source):
    block = jnp.where(lax.axis_index(axis) == source, block, jnp.zeros_like(block))
    return lax.psum(block, axis)


def activation(values):
    return jax.nn.gelu(values, approximate=True)


def layer_norm(values, norm_gain, norm_shift):
    centered = values - jnp.mean(values, -1, keepdims=True)
    variance = jnp.mean(centered * centered, -1, keepdims=True)
    return centered * lax.rsqrt(variance + EPSILON) * norm_gain + norm_shift


def as_float(values):
    return values.astype(jnp.float32)


def row_sum(values):
    return jnp.sum(as_float(values).reshape(-1, values.shape[-1]), 0)


def slot_apply(left, weight):
    return jnp.einsum("rkc,ch->rkh", left, weight, preferred_element_type=jnp.float32)


def slot_product(left, right):
    return jnp.einsum("rkc,rkh->ch", left, right, preferred_element_type=jnp.float32)


def slot_back(grad_in, weight):
    return jnp.einsum("rkh,ch->rkc", grad_in, weight, preferred_element_type=jnp.float32)


def fetch_rows(values):
    return with_halo(values, (("res", 0),), values.shape[0])


def return_rows(far_table, rows_dev):
    total = far_table[rows_dev : 2 * rows_dev]
    for offset, piece in ((-1, far_table[:rows_dev]), (1, far_table[2 * rows_dev :])):
        total = total + from_behind(piece, "res", offset)
    return total


def three_layers(table, own_low, edges, neighbours, weights):
    w_first, b_first, w_second, b_second, w_third, b_third = weights
    width = own_low.shape[1]
    far_rows = table[neighbours]
    near_term = jnp.dot(own_low, w_first[:width], preferred_element_type=jnp.float32) + as_float(
        b_first
    )
    pre_one = (
        near_term[:, None, :]
        + slot_apply(far_rows, w_first[width : 2 * width])
        + slot_apply(edges, w_first[2 * width :])
    )
    act_one = activation(pre_one).astype(jnp.bfloat16)
    pre_two = slot_apply(act_one, w_second) + as_float(b_second)
    act_two = activation(pre_two).astype(jnp.bfloat16)
    update = slot_apply(act_two, w_third) + as_float(b_third)
    return (update, far_rows, pre_one, pre_two)


def three_back(
    d_update, pre_one, pre_two, far_rows, own_low, edges, neighbours, weights, total_rows
):
    w_first, b_first, w_second, b_second, w_third, b_third = weights
    width = own_low.shape[1]
    act_two_f, back_two = jax.vjp(activation, pre_two)
    act_two = act_two_f.astype(jnp.bfloat16)
    g_third = slot_product(act_two, d_update)
    d_pre_two = back_two(slot_back(d_update, w_third))[0].astype(jnp.bfloat16)
    act_one_f, back_one = jax.vjp(activation, pre_one)
    act_one = act_one_f.astype(jnp.bfloat16)
    g_second = slot_product(act_one, d_pre_two)
    d_pre_one = back_one(slot_back(d_pre_two, w_second))[0].astype(jnp.bfloat16)
    d_pre_sum = jnp.sum(as_float(d_pre_one), 1)
    g_first = jnp.concatenate(
        [
            jnp.dot(as_float(own_low).T, d_pre_sum, precision=PRECISE),
            slot_product(far_rows, d_pre_one),
            slot_product(edges, d_pre_one),
        ],
        0,
    )
    d_own = jnp.dot(d_pre_sum, as_float(w_first[:width]).T, precision=PRECISE)
    d_far = slot_back(d_pre_one, w_first[width : 2 * width])
    d_edges = slot_back(d_pre_one, w_first[2 * width :])
    far_table = (
        jnp.zeros((total_rows, width), jnp.float32)
        .at[neighbours.reshape(-1)]
        .add(d_far.reshape(-1, width))
    )
    grads = (g_first, row_sum(d_pre_one), g_second, row_sum(d_pre_two), g_third, row_sum(d_update))
    return (grads, d_own, far_table, d_edges)


def node_forward(table, own_low, edges, neighbours, live_mask, counts_f, node_weights):
    g_one, s_one, w_expand, b_expand, w_reduce, b_reduce, g_two, s_two = node_weights[6:]
    message, far_rows, pre_one, pre_two = three_layers(
        table, own_low, edges, neighbours, node_weights[:6]
    )
    pooled = jnp.sum(message * live_mask[:, :, None], 1) / counts_f[:, None]
    summed = as_float(own_low) + pooled
    normed = layer_norm(summed, as_float(g_one), as_float(s_one))
    pre_expand = jnp.dot(
        normed.astype(jnp.bfloat16), w_expand, preferred_element_type=jnp.float32
    ) + as_float(b_expand)
    act_expand = activation(pre_expand).astype(jnp.bfloat16)
    second_sum = (
        normed
        + jnp.dot(act_expand, w_reduce, preferred_element_type=jnp.float32)
        + as_float(b_reduce)
    )
    result = layer_norm(second_sum, as_float(g_two), as_float(s_two))
    return (result, (pre_one, pre_two, summed, pre_expand, second_sum))


def node_backward(
    grad_out, saved, table, own_low, edges, neighbours, live_mask, counts_f, node_weights
):
    pre_one, pre_two, summed, pre_expand, second_sum = saved
    g_one, s_one, w_expand, b_expand, w_reduce, b_reduce, g_two, s_two = node_weights[6:]
    normed, first_back = jax.vjp(layer_norm, summed, as_float(g_one), as_float(s_one))
    unused_out, second_back = jax.vjp(layer_norm, second_sum, as_float(g_two), as_float(s_two))
    d_second, g_gain_two, g_shift_two = second_back(grad_out)
    d_reduced = d_second.astype(jnp.bfloat16)
    act_expand_f, expand_back = jax.vjp(activation, pre_expand)
    act_expand = act_expand_f.astype(jnp.bfloat16)
    g_reduce = jnp.dot(act_expand.T, d_reduced, preferred_element_type=jnp.float32)
    d_act_expand = jnp.dot(d_reduced, w_reduce.T, preferred_element_type=jnp.float32)
    d_pre_expand = expand_back(d_act_expand)[0].astype(jnp.bfloat16)
    g_expand = jnp.dot(
        normed.astype(jnp.bfloat16).T, d_pre_expand, preferred_element_type=jnp.float32
    )
    d_normed = d_second + jnp.dot(d_pre_expand, w_expand.T, preferred_element_type=jnp.float32)
    d_summed, g_gain_one, g_shift_one = first_back(d_normed)
    d_message = (live_mask[:, :, None] * (d_summed / counts_f[:, None])[:, None, :]).astype(
        jnp.bfloat16
    )
    far_rows = table[neighbours]
    message_grads, d_own, far_table, d_edges = three_back(
        d_message,
        pre_one,
        pre_two,
        far_rows,
        own_low,
        edges,
        neighbours,
        node_weights[:6],
        table.shape[0],
    )
    grads = message_grads + (
        g_gain_one,
        g_shift_one,
        g_expand,
        row_sum(d_pre_expand),
        g_reduce,
        row_sum(d_reduced),
        g_gain_two,
        g_shift_two,
    )
    return (d_summed + d_own, far_table, d_edges, grads)


def edge_pass(table, own_low, edges, neighbours, live_mask, cot_edges, edge_weights):
    g_edge, s_edge = edge_weights[6:]
    update, far_rows, pre_one, pre_two = three_layers(
        table, own_low, edges, neighbours, edge_weights[:6]
    )
    normed, edge_back = jax.vjp(
        layer_norm, as_float(edges) + update, as_float(g_edge), as_float(s_edge)
    )
    result = normed * live_mask[:, :, None]
    d_sum, g_gain, g_shift = edge_back(as_float(cot_edges) * live_mask[:, :, None])
    mlp_grads, d_own, far_table, d_edges = three_back(
        d_sum.astype(jnp.bfloat16),
        pre_one,
        pre_two,
        far_rows,
        own_low,
        edges,
        neighbours,
        edge_weights[:6],
        table.shape[0],
    )
    return (result, d_sum + d_edges, d_own, far_table, mlp_grads + (g_gain, g_shift))


def zero_grads(weights):
    return jax.tree.map(lambda member: jnp.zeros(member.shape, jnp.float32), weights)


def body(
    nodes,
    edges,
    neighbours,
    counts,
    message_first,
    message_first_bias,
    message_second,
    message_second_bias,
    message_third,
    message_third_bias,
    node_norm_gain,
    node_norm_shift,
    expand_weight,
    expand_bias,
    reduce_weight,
    reduce_bias,
    output_norm_gain,
    output_norm_shift,
    edge_first,
    edge_first_bias,
    edge_second,
    edge_second_bias,
    edge_third,
    edge_third_bias,
    edge_norm_gain,
    edge_norm_shift,
    cot_nodes,
    cot_edges,
):
    node_weights = (
        message_first,
        message_first_bias,
        message_second,
        message_second_bias,
        message_third,
        message_third_bias,
        node_norm_gain,
        node_norm_shift,
        expand_weight,
        expand_bias,
        reduce_weight,
        reduce_bias,
        output_norm_gain,
        output_norm_shift,
    )
    edge_weights = (
        edge_first,
        edge_first_bias,
        edge_second,
        edge_second_bias,
        edge_third,
        edge_third_bias,
        edge_norm_gain,
        edge_norm_shift,
    )
    rows_dev, width = nodes.shape
    slot_count = neighbours.shape[1]
    hidden_width = message_second.shape[0]
    is_node = lax.axis_index("half") == 0
    live_mask = (lax.broadcasted_iota(jnp.int32, neighbours.shape, 1) < counts[:, None]).astype(
        jnp.float32
    )
    counts_f = as_float(counts)
    zero_rows = jnp.zeros((rows_dev, width), jnp.float32)
    zero_slots = jnp.zeros(edges.shape, jnp.float32)
    input_table = fetch_rows(nodes)
    picks = neighbours - (lax.axis_index("res") - 1) * rows_dev
    total_rows = input_table.shape[0]

    def first_pass():
        return node_forward(input_table, nodes, edges, picks, live_mask, counts_f, node_weights)[0]

    def blank_rows():
        return zero_rows

    fed = lax.cond(is_node, first_pass, blank_rows).astype(jnp.bfloat16)
    fed_table = fetch_rows(fed)

    def second_pass():
        return node_forward(fed_table, fed, edges, picks, live_mask, counts_f, node_weights)

    def blank_second():
        slot_zeros = jnp.zeros((rows_dev, slot_count, hidden_width), jnp.float32)
        expand_zeros = jnp.zeros((rows_dev, expand_weight.shape[1]), jnp.float32)
        return (zero_rows, (slot_zeros, slot_zeros, zero_rows, expand_zeros, zero_rows))

    node_state, node_saved = lax.cond(is_node, second_pass, blank_second)
    edge_own = broadcast(node_state.astype(jnp.bfloat16), "half", 0)
    edge_table = fetch_rows(edge_own)

    def edge_work():
        return edge_pass(edge_table, edge_own, edges, picks, live_mask, cot_edges, edge_weights)

    def blank_edge():
        return (
            zero_slots,
            zero_slots,
            zero_rows,
            jnp.zeros((total_rows, width), jnp.float32),
            zero_grads(edge_weights),
        )

    edge_result, edge_grad, edge_own_grad, edge_far, edge_grads = lax.cond(
        is_node, blank_edge, edge_work
    )
    from_edges = return_rows(edge_far, rows_dev)
    edge_rounded = as_float(edge_result.astype(jnp.bfloat16))
    returned, edge_states = (
        broadcast(edge_own_grad + from_edges, "half", 1),
        broadcast(edge_rounded, "half", 1),
    )
    grad_out = as_float(cot_nodes) + returned

    def node_work():
        return node_backward(
            grad_out, node_saved, fed_table, fed, edges, picks, live_mask, counts_f, node_weights
        )

    def blank_node():
        return (
            zero_rows,
            jnp.zeros((total_rows, width), jnp.float32),
            zero_slots,
            zero_grads(node_weights),
        )

    own_grad, node_far, message_edge_grad, node_grads = lax.cond(is_node, node_work, blank_node)
    from_nodes = return_rows(node_far, rows_dev)
    node_term = jnp.where(is_node, as_float(edge_own), zero_rows)
    edge_term = jnp.where(is_node, zero_slots, edge_states)
    outputs = (
        lax.psum_scatter(node_term, "half", scatter_dimension=1, tiled=True),
        lax.psum_scatter(edge_term, "half", scatter_dimension=1, tiled=True),
        lax.psum_scatter(own_grad + from_nodes, "half", scatter_dimension=1, tiled=True),
        lax.psum_scatter(edge_grad + message_edge_grad, "half", scatter_dimension=1, tiled=True),
    )
    all_grads = node_grads + edge_grads
    summed_grads = lax.psum(all_grads, "res")
    owned = lax.psum_scatter(summed_grads, "half", scatter_dimension=0, tiled=True)
    return (
        outputs[0].astype(jnp.bfloat16),
        outputs[1].astype(jnp.bfloat16),
        outputs[2],
        outputs[3],
    ) + tuple(owned)


def solution(mesh):
    placed = (
        P("res", None),
        P("res", None, None),
        P("res", None),
        P("res"),
        P(),
        P(),
        P(),
        P(),
        P(),
        P(),
        P(),
        P(),
        P(),
        P(),
        P(),
        P(),
        P(),
        P(),
        P(),
        P(),
        P(),
        P(),
        P(),
        P(),
        P(),
        P(),
        P("res", None),
        P("res", None, None),
    )
    return jax.shard_map(
        body,
        mesh=mesh,
        in_specs=placed,
        out_specs=(
            P("res", "half"),
            P("res", "half", None),
            P("res", "half"),
            P("res", "half", None),
            P("half", None),
            P("half"),
            P("half", None),
            P("half"),
            P("half", None),
            P("half"),
            P("half"),
            P("half"),
            P("half", None),
            P("half"),
            P("half", None),
            P("half"),
            P("half"),
            P("half"),
            P("half", None),
            P("half"),
            P("half", None),
            P("half"),
            P("half", None),
            P("half"),
            P("half"),
            P("half"),
        ),
        check_vma=False,
    )
```

profile of v0, /device:TPU:0, one launch (start us, length us, event | category | flops | bytes accessed | tf_op | source)
XLA Modules:
  0.0 1001.2 jit_solution(10989580257402782453)
XLA Ops:
  8.5 5.5 collective-permute-start
  16.3 2.1 collective-permute-done
  19.3 72.7 %conditional.4 = (bf16[96,512]{1,0:T(8,128)(2,1)S(1)}) conditional(s32[]{:T(128)} %convert_element_type.234, () %tuple.43, (bf16[96,512]{1,0:T(8,128)(2,1)}, bf16[1216,512]{1,0:T(8,128)(2,1)}, bf16[512]{0:T(512)(128)(2,1)}, s32[96,60]{1,0:T(8,128)S(1)}, bf16[288,512]{1,0:T(8,128)(2,1)S(1)}, /*index=5*/bf16[96,60,192]{2,0,1:T(8,128)(2,1)}, ...), branch_computations={%region_0.0_spmd, %region_1.0_spmd} | conditional | flops 10719244288 | bytes 105915104 | solution.py:300
  26.9 17.3 %gather_fusion.3 = bf16[5760,512]{1,0:T(8,128)(2,1)} fusion(bf16[288,512]{1,0:T(8,128)(2,1)S(1)} %get-tuple-element.156, s32[6144]{0:T(1024)S(1)} %pad_clamp_fusion), kind=kCustom, calls=%fused_computation | custom fusion | bytes 11819520 | tf_op jit(solution)/shard_map/cond/branch_1_fun/gather | solution.py:78
  44.2 8.6 reshape.310
  52.8 14.3 %fusion.16 = f32[96,60,512]{2,0,1:T(8,128)} fusion(bf16[96,60,512]{2,1,0:T(8,128)(2,1)} %reshape.310, bf16[1216,512]{1,0:T(8,128)(2,1)} %get-tuple-element.154), kind=kOutput, calls=%fused_computation.25 | convolution fusion | flops 3019898880 | bytes 18612224 | tf_op jit(solution)/shard_map/cond/branch_1_fun/rkc,ch->rkh/dot_general | solution.py:53
  67.1 12.2 %fusion.20 = f32[96,60,512]{2,0,1:T(8,128)} fusion(f32[96,60,512]{2,0,1:T(8,128)} %fusion.16, f32[96,512]{1,0:T(8,128)S(1)} %convolution_add_fusion.2, bf16[96,60,192]{2,0,1:T(8,128)(2,1)S(1)} %copy-done.3, bf16[512,512]{1,0:T(8,128)(2,1)} %get-tuple-element.159, bf16[1216,512]{1,0:T(8,128)(2,1)} %get-tuple-element.154), kind=kOutput, calls=%fused_computation.28 | convolution fusion | flops 4184801280 | bytes 26722304 | tf_op jit(solution)/shard_map/cond/branch_1_fun/rkc,ch->rkh/dot_general | solution.py:53
  79.3 9.0 multiply_reduce_fusion
  88.7 2.6 fusion.257
  93.4 4.9 collective-permute-start.2
  98.9 2.3 collective-permute-done.2
  101.3 76.8 %conditional.5 = (f32[96,60,512]{2,0,1:T(8,128)}, f32[96,60,512]{2,0,1:T(8,128)}, f32[96,512]{1,0:T(8,128)}, f32[96,2048]{1,0:T(8,128)}, f32[96,512]{1,0:T(8,128)}, /*index=5*/bf16[96,512]{1,0:T(8,128)(2,1)S(1)}) conditional(s32[]{:T(128)} %convert_element_type.234, () %tuple.42, (bf16[1216,512]{1,0:T(8,128)(2,1)}, bf16[96,512]{1,0:T(8,128)(2,1)S(1)}, ...), branch_computations={%region_7.0_spmd, %region_8.0_spmd} | conditional | flops 10719242240 | bytes 144258672 | solution.py:311
  107.8 1.9 convolution_add_fusion.5
  109.7 17.2 %gather_fusion = bf16[5760,512]{1,0:T(8,128)(2,1)} fusion(bf16[288,512]{1,0:T(8,128)(2,1)S(1)} %get-tuple-element.176, s32[6144]{0:T(1024)S(1)} %pad_clamp_fusion.1), kind=kCustom, calls=%fused_computation.1 | custom fusion | bytes 11819520 | tf_op jit(solution)/shard_map/cond/branch_1_fun/gather | solution.py:78
  127.0 8.6 reshape.318
  135.5 8.3 fusion.88
  143.9 7.0 add_add_fusion
  150.8 9.9 broadcast_add_fusion
  160.8 8.3 multiply_reduce_fusion.3
  171.1 2.4 convolution_add_fusion.3
  173.5 2.4 fusion.260
  178.8 21.4 %all-reduce.22.cloned.1.call-done = bf16[96,512]{1,0:T(8,128)(2,1)} async-done(((bf16[96,512]{1,0:T(8,128)(2,1)}), bf16[96,512]{1,0:T(8,128)(2,1)}) %all-reduce.22.cloned.1.call-update) | async-done | bytes 98320 | tf_op jit(solution)/shard_map/psum | solution.py:31
  201.6 5.3 collective-permute-start.4
  208.0 2.6 collective-permute-done.4
  211.7 15.1 %conditional.6 = (f32[96,60,192]{2,0,1:T(8,128)}, f32[96,60,192]{2,0,1:T(8,128)}, f32[96,512]{1,0:T(8,128)S(1)}, f32[288,512]{1,0:T(8,128)S(1)}, f32[1216,192]{0...) conditional(s32[]{:T(128)} %convert_element_type.234, ...), branch_computations={%region_16.28_spmd, %region_28.0_spmd} | conditional | flops 7619809280 | bytes 234338080 | solution.py:327
  220.3 3.3 broadcast.439.clone
  223.6 3.2 broadcast.439
  228.1 5.2 collective-permute-start.7
  233.4 5.9 convert_select_fusion
  241.4 2.6 copy.108
  245.9 175.5 %all-reduce.26.cloned.1.call-done = (f32[96,60,192]{2,0,1:T(8,128)}, f32[96,512]{1,0:T(8,128)}) async-done(((f32[96,60,192]{2,0,1:T(8,128)}, f32[96,512]{1,0:T(8,128)}), (f32[96,60,192]{2,0,1:T(8,128)}, f32[96,512]{1,0:T(8,128)})) %all-reduce.26.cloned.1.call-update) | async-done | bytes 4620304 | tf_op jit(solution)/shard_map/psum | solution.py:31
  421.5 192.1 %conditional.7 = (f32[96,512]{1,0:T(8,128)}, f32[288,512]{1,0:T(8,128)}, f32[96,60,192]{2,0,1:T(8,128)}, f32[1216,512]{1,0:T(8,128)}, f32[512]{0:T(512)}, /*inde...) conditional(s32[]{:T(128)} %convert_element_type.234, () %tuple.48, ...), branch_computations={%region_32.33_spmd, %region_33.53_spmd} | conditional | flops 22015922176 | bytes 265763328 | solution.py:351
  424.8 1.9 multiply_reduce_fusion.9
  436.5 2.7 convert_reduce_fusion.8
  439.3 2.4 multiply_reduce_fusion.10
  445.4 10.0 %fusion.207 = f32[512,512]{1,0:T(8,128)} fusion(f32[96,512]{1,0:T(8,128)S(1)} %add_divide_fusion, f32[96,60]{0,1:T(8,128)S(1)} %copy-done.25, f32[96,60,512]{2,0,1:T(8,128)} %get-tuple-element.218), kind=kOutput, calls=%fused_computation.272 | convolution fusion | flops 3052339200 | bytes 13064704 | tf_op jit(solution)/shard_map/cond/branch_1_fun/rkc,rkh->ch/dot_general | solution.py:57
  455.4 13.2 %convert_reduce_fusion.7 = (f32[512]{0:T(512)}, bf16[96,60,512]{2,0,1:T(8,128)(2,1)S(1)}) fusion(f32[96,60,512]{2,0,1:T(8,128)} %get-tuple-element.218, bf16[512,512]{1,0:T(8,128)(2,1)S(1)} %copy-done.61, f32[96,512]{1,0:T(8,128)S(1)} %add_divide_fusion, f32[96,60]{0,1:T(8,128)S(1)} %copy-done.25), kind=kOutput, calls=%fused_computation.256 | convolution fusion | flops 3090677248 | bytes 18440704 | tf_op jit(solution)/shard_map/cond/branch_1_fun/rkh,ch->rkc/dot_general | solution.py:61
  468.6 8.3 fusion.208
  477.0 13.5 %convert_reduce_fusion.4 = (f32[512]{0:T(512)}, f32[96,512]{1,0:T(8,128)S(1)}, bf16[96,60,512]{2,0,1:T(8,128)(2,1)S(1)}) fusion(f32[96,60,512]{2,0,1:T(8,128)} %get-tuple-element.220, bf16[96,60,512]{2,0,1:T(8,128)(2,1)S(1)} %get-tuple-element.489, bf16[512,512]{1,0:T(8,128)(2,1)S(1)} %copy-done.59), kind=kOutput, calls=%fused_computation.238 | convolution fusion | flops 3087678976 | bytes 24315904 | tf_op jit(solution)/shard_map/cond/branch_1_fun/rkh,ch->rkc/dot_general | solution.py:61
  490.5 2.7 convolution_add_fusion.7
  493.2 2.2 convolution_bitcast_fusion.5
  497.0 3.9 fusion.221
  500.9 3.8 fusion.231
  504.7 17.2 %gather_fusion.2 = bf16[5760,512]{1,0:T(8,128)(2,1)} fusion(bf16[288,512]{1,0:T(8,128)(2,1)S(1)} %get-tuple-element.224, s32[6144]{0:T(1024)S(1)} %copy-done.32), kind=kCustom, calls=%fused_computation.3 | custom fusion | bytes 11819520 | tf_op jit(solution)/shard_map/cond/branch_1_fun/gather | solution.py:171
  521.9 8.7 reshape.334
  530.6 18.1 %fusion.204 = f32[512,512]{1,0:T(8,128)S(1)} fusion(bf16[96,60,512]{2,1,0:T(8,128)(2,1)} %reshape.334, bf16[96,60,512]{2,0,1:T(8,128)(2,1)} %copy-done), kind=kOutput, calls=%fused_computation.271 | convolution fusion | flops 3019898880 | bytes 12845056 | tf_op jit(solution)/shard_map/cond/branch_1_fun/rkc,rkh->ch/dot_general | solution.py:57
  550.5 4.2 fusion.228
  554.7 8.0 fusion.200
  562.7 12.4 %reshape.353 = f32[5760,512]{1,0:T(8,128)} reshape(f32[96,60,512]{2,1,0:T(8,128)} %fusion.200) | data formatting | bytes 23592960 | tf_op jit(solution)/shard_map/cond/branch_1_fun/reshape | solution.py:122
  575.1 38.2 %scatter_custom_fusion.1 = f32[288,512]{1,0:T(8,128)} fusion(s32[5760]{0:T(1024)} %fusion.236, f32[5760,512]{1,0:T(8,128)} %reshape.353, f32[]{:T(128)} %constant.116.clone), kind=kCustom, calls=%fused_computation.301 | custom fusion | flops 2949120 | bytes 590336 | tf_op jit(solution)/shard_map/cond/branch_1_fun/scatter-add | solution.py:122
  617.2 3.3 broadcast_select_fusion
  622.9 4.6 collective-permute-start.9
  629.2 3.2 collective-permute-done.9
  634.3 8.6 add.516
  643.0 2.1 copy.109
  645.1 4.4 reduce-scatter.23.cloned.1.call-done
  649.6 15.6 %reduce-scatter.29.cloned.1.call-done = f32[256,2048]{1,0:T(8,128)} async-done(((f32[512,2048]{1,0:T(8,128)}), f32[256,2048]{1,0:T(8,128)}) %reduce-scatter.29.cloned.1.call-update) | async-done | bytes 2097168 | tf_op jit(solution)/shard_map/reduce_scatter | solution.py:363
  665.2 15.6 %reduce-scatter.31.cloned.1.call-done = f32[1024,512]{1,0:T(8,128)} async-done(((f32[2048,512]{1,0:T(8,128)}), f32[1024,512]{1,0:T(8,128)}) %reduce-scatter.31.cloned.1.call-update) | async-done | bytes 2097168 | tf_op jit(solution)/shard_map/reduce_scatter | solution.py:363
  683.4 9.1 reduce-scatter.15.cloned.1.call-done
  694.0 4.1 all-reduce.16
  699.1 78.4 %all-reduce.14 = (f32[256]{0:T(256)}, f32[256]{0:T(256)}, f32[256]{0:T(256)}, f32[256]{0:T(256)}, f32[256]{0:T(256)}, /*index=5*/f32[1024]{0:T(1024)}, f32[256]{...) all-reduce(f32[256]{0:T(256)S(1)} %dynamic-slice.1, ...), channel_id=1, replica_groups=mesh['res'=16,'half'=2] {'res'}, use_global_device_ids=true, to_apply=%region_57.58 | all-reduce | flops 3552 | bytes 28416 | tf_op jit(solution)/shard_map/psum | solution.py:362
  777.4 3.2 convert_element_type.241
  780.6 202.5 %all-reduce.24.cloned.1.call-done = (f32[608,512]{1,0:T(8,128)}, f32[256,512]{1,0:T(8,128)}, f32[256,512]{1,0:T(8,128)}, f32[256,2048]{1,0:T(8,128)}, f32[1024,5...) async-done(((f32[608,512]{1,0:T(8,128)}, f32[256,512]{1,0:T(8,128)}, f32[256,512]{1,0:T(8,128)}, f32[256,2048]{1,0:T(8,128)}, ...) | async-done | bytes 7102480 | tf_op jit(solution)/shard_map/psum | solution.py:362
  983.1 2.6 copy.211
  (290 shorter events, 77.6 us)
Async XLA Ops:
  7.2 193.1 %all-reduce.22.cloned.1.call-start = ((), (), s32[]{:S(2)}) async-start(), calls=%async_computation.12 | async-start | bytes 196608 | tf_op jit(solution)/shard_map/psum | solution.py:31
  7.2 9.0 collective-permute-start.1
  8.5 9.9 collective-permute-start
  14.9 86.4 %copy-start.15 = (s32[96,60]{1,0:T(8,128)}, s32[96,60]{1,0:T(8,128)S(1)}, u32[]{:S(2)}) copy-start(s32[96,60]{1,0:T(8,128)S(1)} %broadcast_subtract_fusion) | copy-start | bytes 69124
  15.6 85.7 %copy-start.23 = (f32[96,60]{0,1:T(8,128)}, f32[96,60]{0,1:T(8,128)S(1)}, u32[]{:S(2)}) copy-start(f32[96,60]{0,1:T(8,128)S(1)} %fusion.251) | copy-start | bytes 69124
  16.3 85.0 %copy-start.43 = (f32[96]{0:T(128)}, f32[96]{0:T(128)S(1)}, u32[]{:S(2)}) copy-start(f32[96]{0:T(128)S(1)} %convert_element_type.236) | copy-start | bytes 1156
  52.8 14.3 %copy-start.3 = (bf16[96,60,192]{2,0,1:T(8,128)(2,1)S(1)}, bf16[96,60,192]{2,0,1:T(8,128)(2,1)}, u32[]{:S(2)}) copy-start(bf16[96,60,192]{2,0,1:T(8,128)(2,1)} %get-tuple-element.158) | copy-start | bytes 6635524 | tf_op jit(solution)/shard_map/cond
  79.3 9.0 copy-start.26
  79.3 9.4 copy-start.7
  92.1 9.3 copy-start.13
  92.1 6.9 collective-permute-start.3
  93.4 7.8 collective-permute-start.2
  101.2 110.4 %copy-start.1 = (bf16[96,60,192]{2,0,1:T(8,128)(2,1)S(1)}, bf16[96,60,192]{2,0,1:T(8,128)(2,1)}, u32[]{:S(2)}) copy-start(bf16[96,60,192]{2,0,1:T(8,128)(2,1)} %param.63) | copy-start | bytes 6635524
  101.3 110.4 %copy-start.64 = (bf16[192]{0:T(256)(128)(2,1)S(1)}, bf16[192]{0:T(256)(128)(2,1)}, u32[]{:S(2)}) copy-start(bf16[192]{0:T(256)(128)(2,1)} %param.55) | copy-start | bytes 1156
  101.3 110.4 %copy-start.65 = (bf16[192]{0:T(256)(128)(2,1)S(1)}, bf16[192]{0:T(256)(128)(2,1)}, u32[]{:S(2)}) copy-start(bf16[192]{0:T(256)(128)(2,1)} %param.57) | copy-start | bytes 1156
  101.3 110.4 %copy-start.66 = (bf16[192]{0:T(256)(128)(2,1)S(1)}, bf16[192]{0:T(256)(128)(2,1)}, u32[]{:S(2)}) copy-start(bf16[192]{0:T(256)(128)(2,1)} %param.60) | copy-start | bytes 1156
  135.5 8.3 copy-start.27
  150.8 9.9 copy-start.60
  160.8 10.3 %copy-start.8 = (bf16[512,2048]{1,0:T(8,128)(2,1)S(1)}, bf16[512,2048]{1,0:T(8,128)(2,1)}, u32[]{:S(2)}) copy-start(bf16[512,2048]{1,0:T(8,128)(2,1)} %get-tuple-element.187) | copy-start | bytes 6291460 | tf_op jit(solution)/shard_map/cond
  160.8 12.7 %copy-start.57 = (bf16[2048,512]{1,0:T(8,128)(2,1)S(1)}, bf16[2048,512]{1,0:T(8,128)(2,1)}, u32[]{:S(2)}) copy-start(bf16[2048,512]{1,0:T(8,128)(2,1)} %get-tuple-element.189) | copy-start | bytes 6291460 | tf_op jit(solution)/shard_map/cond
  178.8 242.7 %all-reduce.26.cloned.1.call-start = ((), (), s32[]{:S(2)}) async-start(), calls=%async_computation.26 | async-start | bytes 12189696 | tf_op jit(solution)/shard_map/psum | solution.py:31
  200.3 7.1 collective-permute-start.5
  201.6 9.1 collective-permute-start.4
  226.8 12.5 %collective-permute-start.6 = (f32[96,512]{1,0:T(8,128)S(1)}, f32[96,512]{1,0:T(8,128)S(1)}, u32[]{:S(2)}, u32[]{:S(2)}) collective-permute-start(f32[96,512]{1,0:T(8,128)S(1)} %get-tuple-element.493), channel_id=1, source_target_pairs={{2,0},{4,2},{6,4},{8,6},{10,8},{12,10},{14,12},{16,14},{18,16},{20... | collective-permute-start | bytes 589832 | tf_op jit(solution)/shard_map/ppermute | solution.py:26
  228.1 11.2 %collective-permute-start.7 = (f32[96,512]{1,0:T(8,128)S(1)}, f32[96,512]{1,0:T(8,128)S(1)}, u32[]{:S(2)}, u32[]{:S(2)}) collective-permute-start(f32[96,512]{1,0:T(8,128)S(1)} %get-tuple-element.494), channel_id=1, source_target_pairs={{0,2},{2,4},{4,6},{6,8},{8,10},{10,12},{12,14},{14,16},{16,18},{18... | collective-permute-start | bytes 589832 | tf_op jit(solution)/shard_map/ppermute | solution.py:26
  239.3 182.2 %copy-start.2 = (bf16[96,60,192]{2,0,1:T(8,128)(2,1)S(1)}, bf16[96,60,192]{2,0,1:T(8,128)(2,1)}, u32[]{:S(2)}) copy-start(bf16[96,60,192]{2,0,1:T(8,128)(2,1)} %param.37) | copy-start | bytes 6635524
  239.3 182.2 %copy-start.14 = (bf16[96,512]{1,0:T(8,128)(2,1)S(1)}, bf16[96,512]{1,0:T(8,128)(2,1)}, u32[]{:S(2)}) copy-start(bf16[96,512]{1,0:T(8,128)(2,1)} %copy-done.13) | copy-start | bytes 294916
  239.3 182.2 %copy-start.16 = (s32[96,60]{1,0:T(8,128)S(1)}, s32[96,60]{1,0:T(8,128)}, u32[]{:S(2)}) copy-start(s32[96,60]{1,0:T(8,128)} %copy-done.15) | copy-start | bytes 69124
  239.3 182.2 %copy-start.37 = (bf16[512]{0:T(512)(128)(2,1)S(1)}, bf16[512]{0:T(512)(128)(2,1)}, u32[]{:S(2)}) copy-start(bf16[512]{0:T(512)(128)(2,1)} %param.46) | copy-start | bytes 3076
  239.3 182.2 %copy-start.38 = (bf16[512]{0:T(512)(128)(2,1)S(1)}, bf16[512]{0:T(512)(128)(2,1)}, u32[]{:S(2)}) copy-start(bf16[512]{0:T(512)(128)(2,1)} %param.47) | copy-start | bytes 3076
  239.3 182.1 %copy-start.39 = (bf16[512]{0:T(512)(128)(2,1)S(1)}, bf16[512]{0:T(512)(128)(2,1)}, u32[]{:S(2)}) copy-start(bf16[512]{0:T(512)(128)(2,1)} %param.52) | copy-start | bytes 3076
  241.3 401.7 %reduce-scatter.37.cloned.1.call-start = ((), (), s32[]{:S(2)}) async-start(), calls=%async_computation.24 | async-start | bytes 1867776
  244.0 401.1 %reduce-scatter.33.cloned.1.call-start = ((), (), s32[]{:S(2)}) async-start(), calls=%async_computation.22 | async-start | bytes 294912 | tf_op jit(solution)/shard_map/reduce_scatter | solution.py:363
  244.6 400.5 %reduce-scatter.35.cloned.1.call-start = ((), (), s32[]{:S(2)}) async-start(), calls=%async_computation.23 | async-start | bytes 294912 | tf_op jit(solution)/shard_map/reduce_scatter | solution.py:363
  245.2 399.9 %reduce-scatter.25.cloned.1.call-start = ((), (), s32[]{:S(2)}) async-start(), calls=%async_computation.18 | async-start | bytes 1572864 | tf_op jit(solution)/shard_map/reduce_scatter | solution.py:363
  424.8 11.8 %copy-start.40 = (f32[96]{0:T(128)}, f32[96]{0:T(128)S(1)}, u32[]{:S(2)}) copy-start(f32[96]{0:T(128)S(1)} %broadcast_multiply_fusion.5) | copy-start | bytes 1156 | tf_op jit(solution)/shard_map/cond
  430.5 8.7 copy-start.20
  432.1 9.6 copy-start.56
  432.1 11.5 %copy-start.25 = (f32[96,60]{0,1:T(8,128)S(1)}, f32[96,60]{0,1:T(8,128)}, u32[]{:S(2)}) copy-start(f32[96,60]{0,1:T(8,128)} %get-tuple-element.215) | copy-start | bytes 69124 | tf_op jit(solution)/shard_map/cond
  445.4 10.0 %copy-start.61 = (bf16[512,512]{1,0:T(8,128)(2,1)S(1)}, bf16[512,512]{1,0:T(8,128)(2,1)}, u32[]{:S(2)}) copy-start(bf16[512,512]{1,0:T(8,128)(2,1)} %get-tuple-element.217) | copy-start | bytes 1572868 | tf_op jit(solution)/shard_map/cond
  495.4 9.3 copy-start.32
  521.9 28.6 %slice-start = ((s8[5898240]{0:T(1024)(128)(4,1)}), s8[1703936]{0:T(1024)(128)(4,1)S(1)}, s32[]{:S(2)}) async-start(s8[5898240]{0:T(1024)(128)(4,1)} %bitcast.128), calls=%async_computation.27 | async-start | bytes 3407872 | tf_op jit(solution)/shard_map/cond
  530.6 18.1 %copy-start.10 = (f32[512,512]{1,0:T(8,128)S(1)}, f32[512,512]{1,0:T(8,128)}, u32[]{:S(2)}) copy-start(f32[512,512]{1,0:T(8,128)} %convolution_bitcast_fusion.4) | copy-start | bytes 3145732 | tf_op jit(solution)/shard_map/cond
  530.6 18.2 %copy-start.31 = (f32[192,512]{1,0:T(8,128)S(1)}, f32[192,512]{1,0:T(8,128)}, u32[]{:S(2)}) copy-start(f32[192,512]{1,0:T(8,128)} %convolution_bitcast_fusion.5) | copy-start | bytes 1179652 | tf_op jit(solution)/shard_map/cond
  530.6 19.9 %slice-start.1 = ((s8[5898240]{0:T(1024)(128)(4,1)}), s8[4194304]{0:T(1024)(128)(4,1)S(1)}, s32[]{:S(2)}) async-start(s8[5898240]{0:T(1024)(128)(4,1)} %bitcast.128), calls=%async_computation.28 | async-start | bytes 8388608 | tf_op jit(solution)/shard_map/cond
  530.6 19.9 %copy-start.6 = (bf16[1216,512]{1,0:T(8,128)(2,1)S(1)}, bf16[1216,512]{1,0:T(8,128)(2,1)}, u32[]{:S(2)}) copy-start(bf16[1216,512]{1,0:T(8,128)(2,1)} %get-tuple-element.221) | copy-start | bytes 3735556 | tf_op jit(solution)/shard_map/cond
  613.6 31.6 %reduce-scatter.27.cloned.1.call-start = ((), (), s32[]{:S(2)}) async-start(), calls=%async_computation.19 | async-start | bytes 1572864 | tf_op jit(solution)/shard_map/reduce_scatter | solution.py:363
  614.3 35.2 %reduce-scatter.23.cloned.1.call-start = ((), (), s32[]{:S(2)}) async-start(), calls=%async_computation.17 | async-start | bytes 3735552 | tf_op jit(solution)/shard_map/reduce_scatter | solution.py:363
  615.1 50.1 %reduce-scatter.29.cloned.1.call-start = ((), (), s32[]{:S(2)}) async-start(), calls=%async_computation.20 | async-start | bytes 6291456 | tf_op jit(solution)/shard_map/reduce_scatter | solution.py:363
  615.8 65.0 %reduce-scatter.31.cloned.1.call-start = ((), (), s32[]{:S(2)}) async-start(), calls=%async_computation.21 | async-start | bytes 6291456 | tf_op jit(solution)/shard_map/reduce_scatter | solution.py:363
  616.4 76.1 %reduce-scatter.15.cloned.1.call-start = ((), (), s32[]{:S(2)}) async-start(), calls=%async_computation.13 | async-start | bytes 294912 | tf_op jit(solution)/shard_map/reduce_scatter | solution.py:356
  617.2 160.3 %reduce-scatter.17.cloned.1.call-start = ((), (), s32[]{:S(2)}) async-start(), calls=%async_computation.14 | async-start | bytes 8847360 | tf_op jit(solution)/shard_map/reduce_scatter | solution.py:357
  620.5 160.1 %reduce-scatter.19.cloned.1.call-start = ((), (), s32[]{:S(2)}) async-start(), calls=%async_computation.15 | async-start | bytes 294912 | tf_op jit(solution)/shard_map/reduce_scatter | solution.py:358
  621.6 7.6 collective-permute-start.8
  622.9 9.4 collective-permute-start.9
  634.3 146.3 %reduce-scatter.21.cloned.1.call-start = ((), (), s32[]{:S(2)}) async-start(), calls=%async_computation.16 | async-start | bytes 8847360 | tf_op jit(solution)/shard_map/reduce_scatter | solution.py:359
  642.9 37.9 %copy-start.68 = (u32[32]{0:T(128)S(1)}, u32[32]{0:T(128)}, u32[]{:S(2)}) copy-start(u32[32]{0:T(128)} %constant.175) | copy-start | bytes 388
  642.9 51.1 %copy-start.45 = (f32[192]{0:T(256)S(1)}, f32[192]{0:T(256)}, u32[]{:S(2)}) copy-start(f32[192]{0:T(256)} %copy-done.44) | copy-start | bytes 2308
  642.9 51.1 %copy-start.47 = (f32[192]{0:T(256)S(1)}, f32[192]{0:T(256)}, u32[]{:S(2)}) copy-start(f32[192]{0:T(256)} %copy-done.46) | copy-start | bytes 2308
  642.9 51.1 %copy-start.49 = (f32[192]{0:T(256)S(1)}, f32[192]{0:T(256)}, u32[]{:S(2)}) copy-start(f32[192]{0:T(256)} %copy-done.48) | copy-start | bytes 2308
  642.9 51.1 %copy-start.52 = (f32[192]{0:T(256)S(1)}, f32[192]{0:T(256)}, u32[]{:S(2)}) copy-start(f32[192]{0:T(256)} %copy-done.51) | copy-start | bytes 2308
  642.9 51.1 %copy-start.54 = (f32[192]{0:T(256)S(1)}, f32[192]{0:T(256)}, u32[]{:S(2)}) copy-start(f32[192]{0:T(256)} %copy-done.53) | copy-start | bytes 2308
  643.0 340.2 %all-reduce.24.cloned.1.call-start = ((), (), s32[]{:S(2)}) async-start(), calls=%async_computation.25 | async-start | bytes 14352384 | tf_op jit(solution)/shard_map/psum | solution.py:362
  983.1 9.0 copy-start.29
  (24 other events, 151.8 us)
Sparse Core Ops, SparseCore 0:
  178.9 21.3 all-reduce.21
  241.4 179.9 all-reduce.25
  424.3 9.8 reduce-scatter.36
  436.4 8.7 reduce-scatter.32
  447.4 8.7 reduce-scatter.34
  613.7 9.7 reduce-scatter.24
  626.3 9.6 reduce-scatter.26
  638.4 11.1 reduce-scatter.22
  651.9 13.2 reduce-scatter.28
  667.4 13.3 reduce-scatter.30
  683.6 8.8 reduce-scatter.14
  694.7 15.0 reduce-scatter.16
  712.7 8.8 reduce-scatter.18
  724.4 15.0 reduce-scatter.20
  746.3 236.7 all-reduce.23
where the time goes:
time: 1010 us; the launch traced here: 1000 us
  waiting for transfers between devices  461 us (46%)
  matrix products  174 us (17%)
  local copies, waits for them, and re-layouts  121 us (12%)
  other arithmetic  105 us (10%)
  blocking collectives  82.4 us (8%)
  starting transfers between devices  32.5 us (3%)
  between operations  17 us (2%)
    psum x1, waiting for transfers between devices, body(): summed_grads = lax.psum(all_grads, 'res')  203 us
    psum x2, waiting for transfers between devices, broadcast(): return lax.psum(block, axis)  197 us
    psum x1, blocking collectives, body(): summed_grads = lax.psum(all_grads, 'res')  78.4 us
    dot_general x7, matrix products, slot_apply(): jnp.einsum('rkc,ch->rkh', left, weight, preferred_element_type=jnp.float32)  68.9 us
    gather x4, local copies, waits for them, and re-layouts, three_layers(): far_rows = table[neighbours]  51.7 us
    dot_general x4, matrix products, slot_back(): jnp.einsum('rkh,ch->rkc', grad_in, weight, preferred_element_type=jnp.flo...  39 us
    dot_general x4, matrix products, slot_product(): jnp.einsum('rkc,rkh->ch', left, right, preferred_element_type=jnp.float32)  38.7 us
    scatter-add x1, other arithmetic, three_back(): far_table = jnp.zeros((total_rows, width), jnp.float32).at[neighbours.res...  38.2 us
  transfers between devices with their start and end apart: 25, of which 14 were waited for; matrix products, arithmetic and copies ran while one was open for 23% of the time, Pallas kernels for 0%

commit v1 on v0

v1 whole, which is shorter than its diff:
```python
import functools

import jax
import jax.numpy as jnp
from jax import lax
from jax.experimental import pallas as pl
from jax.experimental.pallas import tpu as pltpu
from jax.sharding import PartitionSpec as P

EPSILON = 1e-05
REACH = 64
CORES = 2
NEAR = 0.7978845608
CUBE = 0.044715
BLOCK = 8
LANES = 256
VMEM = 60 * 2**20
MESH = pl.DeviceIdType.MESH
F32 = jnp.float32
BF16 = jnp.bfloat16


def dot(left, right):
    return jnp.dot(left, right, preferred_element_type=F32)


def dot_t(left, right):
    return lax.dot_general(left, right, (((1,), (1,)), ((), ())), preferred_element_type=F32)


def t_dot(left, right):
    return lax.dot_general(left, right, (((0,), (0,)), ((), ())), preferred_element_type=F32)


def two_parts(values):
    high = values.astype(BF16)
    return high, (values - high.astype(F32)).astype(BF16)


def dot_wide(values, right, transposed=False):
    rows = values.shape[0]
    both = (dot_t if transposed else dot)(jnp.concatenate(two_parts(values), 0), right)
    return both[:rows] + both[rows:]


def gelu(values):
    square = values * values
    bend = jnp.tanh(values * (NEAR + (NEAR * CUBE) * square))
    return values * (0.5 + 0.5 * bend)


def gelu_and_slope(values):
    square = values * values
    bend = jnp.tanh(values * (NEAR + (NEAR * CUBE) * square))
    part = 0.5 + 0.5 * bend
    act = values * part
    slope = part + act * (1.0 - part) * (2.0 * NEAR + (6.0 * NEAR * CUBE) * square)
    return act, slope


def norm_parts(values):
    centered = values - jnp.mean(values, -1, keepdims=True)
    scale = lax.rsqrt(jnp.mean(centered * centered, -1, keepdims=True) + EPSILON)
    return centered * scale, scale


def norm_back(grad, unit, scale, gain):
    scaled = gain * grad
    flat = jnp.mean(scaled, -1, keepdims=True)
    slant = jnp.mean(scaled * unit, -1, keepdims=True)
    return (scaled - flat - unit * slant) * scale


def col_sum(values):
    return jnp.sum(values, 0, keepdims=True)


def line_neighbours():
    res, half, count = lax.axis_index("res"), lax.axis_index("half"), lax.axis_size("res")
    return (
        (res > 0, (res - 1, half)),
        (res + half > 0, (res - 1 + half, 1 - half)),
        (res + half < count, (res + half, 1 - half)),
        (res < count - 1, (res + 1, half)),
    )


def line_count():
    res, half, count = lax.axis_index("res"), lax.axis_index("half"), lax.axis_size("res")
    return 4 - jnp.where(res > 0, 0, 2 - half) - jnp.where(res < count - 1, 0, 1 + half)


def greet_line():
    barrier = pltpu.get_barrier_semaphore()
    for exists, place in line_neighbours():

        @pl.when(exists)
        def _():
            pl.semaphore_signal(barrier, inc=1, device_id=place, device_id_type=MESH)


def halo_layout(rows):
    edge = REACH - rows
    return ((0, edge), (edge, rows), (REACH + rows, rows), (REACH + 2 * rows, edge))


def halo_kernel(own_ref, out_ref, window, send, recv):
    rows = own_ref.shape[0]
    layout = halo_layout(rows)
    neighbours = line_neighbours()
    greet_line()
    for (exists, _), (offset, size) in zip(neighbours, layout):

        @pl.when(jnp.logical_not(exists))
        def _():
            window[pl.ds(offset, size), :] = jnp.zeros((size, own_ref.shape[1]), own_ref.dtype)

    pl.semaphore_wait(pltpu.get_barrier_semaphore(), line_count())
    copies = []
    for at, (exists, place) in enumerate(neighbours):
        offset, size = layout[3 - at]
        first = rows - size if at == 3 else 0
        copy = pltpu.make_async_remote_copy(
            src_ref=own_ref.at[pl.ds(first, size)],
            dst_ref=window.at[pl.ds(offset, size)],
            send_sem=send.at[at],
            recv_sem=recv.at[3 - at],
            device_id=place,
            device_id_type=MESH,
        )
        copies.append((exists, copy))

        @pl.when(exists)
        def _():
            copy.start()

    window[pl.ds(REACH, rows), :] = own_ref[...]
    for at, (exists, _) in enumerate(neighbours):
        offset, size = layout[at]

        @pl.when(exists)
        def _():
            copies[at][1].wait_send()
            pltpu.make_async_remote_copy(
                src_ref=own_ref.at[pl.ds(0, size)],
                dst_ref=window.at[pl.ds(offset, size)],
                send_sem=send.at[at],
                recv_sem=recv.at[at],
                device_id=neighbours[at][1],
                device_id_type=MESH,
            ).wait_recv()

    out_ref[...] = window[...]


def fetch_window(own, collective):
    rows, width = own.shape
    return pl.pallas_call(
        halo_kernel,
        out_shape=jax.ShapeDtypeStruct((rows + 2 * REACH, width), own.dtype),
        in_specs=[pl.BlockSpec(memory_space=pltpu.VMEM)],
        out_specs=pl.BlockSpec(memory_space=pltpu.VMEM),
        scratch_shapes=[
            pltpu.VMEM((rows + 2 * REACH, width), own.dtype),
            pltpu.SemaphoreType.DMA((4,)),
            pltpu.SemaphoreType.DMA((4,)),
        ],
        compiler_params=pltpu.CompilerParams(collective_id=collective, has_side_effects=True),
        name="fetch_window",
    )(own)


def start_returns(table, landing, send, recv, rows):
    layout = halo_layout(rows)
    copies = []
    for at, (exists, place) in enumerate(line_neighbours()):
        offset, size = layout[at]
        back_offset, _ = layout[3 - at]
        copy = pltpu.make_async_remote_copy(
            src_ref=table.at[pl.ds(offset, size)],
            dst_ref=landing.at[pl.ds(back_offset, size)],
            send_sem=send.at[at],
            recv_sem=recv.at[3 - at],
            device_id=place,
            device_id_type=MESH,
        )
        copies.append(copy)

        @pl.when(exists)
        def _():
            copy.start()

    return copies


def finish_returns(table, landing, total, send, recv, rows, copies):
    layout = halo_layout(rows)
    total[...] = table[pl.ds(REACH, rows), :]
    for at, (exists, place) in enumerate(line_neighbours()):
        offset, size = layout[at]
        first = rows - size if at == 3 else 0

        @pl.when(exists)
        def _():
            copies[at].wait_send()
            pltpu.make_async_remote_copy(
                src_ref=table.at[pl.ds(offset, size)],
                dst_ref=landing.at[pl.ds(offset, size)],
                send_sem=send.at[at],
                recv_sem=recv.at[at],
                device_id=place,
                device_id_type=MESH,
            ).wait_recv()
            total[pl.ds(first, size), :] += landing[pl.ds(offset, size), :]


def return_kernel(table_ref, out_ref, landing, total, send, recv):
    rows = out_ref.shape[0]
    greet_line()
    pl.semaphore_wait(pltpu.get_barrier_semaphore(), line_count())
    copies = start_returns(table_ref, landing, send, recv, rows)
    finish_returns(table_ref, landing, total, send, recv, rows, copies)
    out_ref[...] = total[...]


def return_rows(table, collective):
    window, width = table.shape
    rows = window - 2 * REACH
    return pl.pallas_call(
        return_kernel,
        out_shape=jax.ShapeDtypeStruct((rows, width), F32),
        in_specs=[pl.BlockSpec(memory_space=pltpu.VMEM)],
        out_specs=pl.BlockSpec(memory_space=pltpu.VMEM),
        scratch_shapes=[
            pltpu.VMEM((window, width), F32),
            pltpu.VMEM((rows, width), F32),
            pltpu.SemaphoreType.DMA((4,)),
            pltpu.SemaphoreType.DMA((4,)),
        ],
        compiler_params=pltpu.CompilerParams(collective_id=collective, has_side_effects=True),
        name="return_rows",
    )(table)


def fill_table(window, far, own, table, rows):
    places = window.shape[0]
    table[pl.ds(0, places), :] = dot(window[...], far[...]).astype(BF16)
    table[pl.ds(places, rows), :] = dot(window[pl.ds(REACH, rows), :], own[...]).astype(BF16)
    rest = LANES - places - rows
    if rest:
        table[pl.ds(places + rows, rest), :] = jnp.zeros((rest, table.shape[1]), BF16)


def feed_forward(pooled, counts, own, w, keep):
    mean = pooled / counts
    summed = own + dot_wide(mean, w["third"][...]) + w["third_bias"][...]
    unit, _ = norm_parts(summed)
    normed = unit * w["gain_one"][...] + w["shift_one"][...]
    low = normed.astype(BF16)
    pre = dot(low, w["expand"][...]) + w["expand_bias"][...]
    act = gelu(pre).astype(BF16)
    second = normed + dot(act, w["reduce"][...]) + w["reduce_bias"][...]
    unit_two, _ = norm_parts(second)
    if keep is not None:
        keep["summed"][...] = summed
        keep["pre_expand"][...] = pre
        keep["second"][...] = second
        keep["normed"][...] = low
    return unit_two * w["gain_two"][...] + w["shift_two"][...]


NODE_WEIGHTS = (
    "far",
    "own",
    "edge",
    "second",
    "second_bias",
    "third",
    "third_bias",
    "gain_one",
    "shift_one",
    "expand",
    "expand_bias",
    "reduce",
    "reduce_bias",
    "gain_two",
    "shift_two",
)


def pool_rows(live_row, act_two, step):
    slots = act_two.shape[0] // BLOCK
    shape = (BLOCK, act_two.shape[0])
    mine = lax.broadcasted_iota(jnp.int32, shape, 1) // slots == lax.broadcasted_iota(jnp.int32, shape, 0)
    return dot(jnp.where(mine, live_row, 0.0).astype(BF16), act_two)


def first_kernel(rows, window, picks, edges, live_row, counts, *refs):
    w = dict(zip(NODE_WEIGHTS, refs))
    out, onehot, table, pooled = refs[len(NODE_WEIGHTS) :]
    step = pl.program_id(0)
    places = window.shape[0]

    @pl.when(step == 0)
    def _():
        fill_table(window, w["far"], w["own"], table, rows)

    size = edges.shape[0]
    lane = lax.broadcasted_iota(jnp.int32, (size, LANES), 1)
    residue = lax.broadcasted_iota(jnp.int32, (size, LANES), 0) // (size // BLOCK) + step * BLOCK
    hit = (lane == picks[...]) | (lane == residue + places)
    hot = jnp.where(hit, 1.0, 0.0).astype(BF16)
    onehot[...] = hot
    pre_one = dot(
        jnp.concatenate([hot, edges[...]], 1), jnp.concatenate([table[...], w["edge"][...]], 0)
    )
    act_one = gelu(pre_one).astype(BF16)
    pre_two = dot(act_one, w["second"][...]) + w["second_bias"][...]
    act_two = gelu(pre_two).astype(BF16)
    pooled[pl.ds(step * BLOCK, BLOCK), :] = pool_rows(live_row[...], act_two, step)

    @pl.when(step == pl.num_programs(0) - 1)
    def _():
        own = window[pl.ds(REACH, rows), :].astype(F32)
        out[...] = feed_forward(pooled[...], counts[...], own, w, None).astype(BF16)


def second_kernel(rows, window, onehot, edges, live, live_row, counts, *refs):
    w = dict(zip(NODE_WEIGHTS, refs))
    out, act_kept, slope_one, slope_two, pooled, summed, pre_expand, second, normed, table = refs[
        len(NODE_WEIGHTS) :
    ]
    step = pl.program_id(0)

    @pl.when(step == 0)
    def _():
        fill_table(window, w["far"], w["own"], table, rows)

    pre_one = dot(
        jnp.concatenate([onehot[...], edges[...]], 1),
        jnp.concatenate([table[...], w["edge"][...]], 0),
    )
    act_one, slope = gelu_and_slope(pre_one)
    act_one = act_one.astype(BF16)
    act_kept[...] = act_one
    slope_one[...] = slope.astype(BF16)
    pre_two = dot(act_one, w["second"][...]) + w["second_bias"][...]
    act_two, slope = gelu_and_slope(pre_two)
    slope_two[...] = (slope * live[...]).astype(BF16)
    pooled[pl.ds(step * BLOCK, BLOCK), :] = pool_rows(live_row[...], act_two.astype(BF16), step)

    @pl.when(step == pl.num_programs(0) - 1)
    def _():
        own = window[pl.ds(REACH, rows), :].astype(F32)
        keep = {"summed": summed, "pre_expand": pre_expand, "second": second, "normed": normed}
        out[...] = feed_forward(pooled[...], counts[...], own, w, keep).astype(BF16)


def whole(array):
    return pl.BlockSpec(array.shape, lambda i: (0,) * len(array.shape))


def by_rows(array, size):
    return pl.BlockSpec((size,) + array.shape[1:], lambda i: (i,) + (0,) * (len(array.shape) - 1))


def by_lanes(array, size):
    return pl.BlockSpec((1, size), lambda i: (0, i))


def shape(dims, kind):
    return jax.ShapeDtypeStruct(dims, kind)


def node_pass(first, window, hot, edges, live, live_row, counts, weights):
    rows = window.shape[0] - 2 * REACH
    width = window.shape[1]
    total = edges.shape[0]
    size = total // (rows // BLOCK)
    hidden = weights["second"].shape[0]
    inner = weights["expand"].shape[1]
    args = [window, hot, edges] + ([] if first else [live]) + [live_row, counts]
    specs = [whole(window), by_rows(hot, size), by_rows(edges, size)]
    specs += ([] if first else [by_rows(live, size)]) + [by_lanes(live_row, size), whole(counts)]
    for name in NODE_WEIGHTS:
        args.append(weights[name])
        specs.append(whole(weights[name]))
    out = shape((rows, width), BF16)
    table = pltpu.VMEM((LANES, hidden), BF16)
    if first:
        onehot = shape((total, LANES), BF16)
        outs, out_specs = (out, onehot), (whole(out), by_rows(onehot, size))
        scratch = [table, pltpu.VMEM((rows, hidden), F32)]
        kernel = first_kernel
    else:
        slots = shape((total, hidden), BF16)
        kept = (
            shape((rows, hidden), F32),
            shape((rows, width), F32),
            shape((rows, inner), F32),
            shape((rows, width), F32),
            shape((rows, width), BF16),
        )
        outs = (out, slots, slots, slots) + kept
        out_specs = (whole(out),) + (by_rows(slots, size),) * 3 + tuple(whole(k) for k in kept)
        scratch = [table]
        kernel = second_kernel
    return pl.pallas_call(
        functools.partial(kernel, rows),
        grid=(rows // BLOCK,),
        out_shape=outs,
        in_specs=specs,
        out_specs=out_specs,
        scratch_shapes=scratch,
        compiler_params=pltpu.CompilerParams(vmem_limit_bytes=VMEM),
        name="node_pass_first" if first else "node_pass_second",
    )(*args)


EDGE_WEIGHTS = ("far", "own", "edge", "edge_x", "second", "second_x", "third", "third_x", "gain", "shift")


def edge_kernel(rows, features, window, onehot, edges, cot, live, *refs):
    w = dict(zip(EDGE_WEIGHTS, refs))
    out, grad, spread, g_edge, g_second, g_third, g_norm, g_own, g_far, d_own, table = refs[
        len(EDGE_WEIGHTS) :
    ]
    step = pl.program_id(0)

    @pl.when(step == 0)
    def _():
        fill_table(window, w["far"], w["own"], table, rows)
        for total in (spread, g_edge, g_second, g_third, g_norm):
            total[...] = jnp.zeros(total.shape, F32)

    lane = lax.broadcasted_iota(jnp.int32, (1, LANES), 1)
    one = jnp.where(lane == features, 1.0, 0.0)
    inside = jnp.where(lane < features, 1.0, 0.0)
    hot, feats = onehot[...], edges[...]
    t_one = dot(jnp.concatenate([hot, feats], 1), jnp.concatenate([table[...], w["edge_x"][...]], 0))
    o_one, slope_one = gelu_and_slope(t_one)
    o_one = (o_one + one).astype(BF16)
    o_two, slope_two = gelu_and_slope(dot(o_one, w["second_x"][...]))
    o_two = (o_two + one).astype(BF16)
    summed = feats.astype(F32) + dot(o_two, w["third_x"][...])
    mean = jnp.sum(summed, -1, keepdims=True) * (1.0 / features)
    centered = (summed - mean) * inside
    scale = lax.rsqrt(jnp.sum(centered * centered, -1, keepdims=True) * (1.0 / features) + EPSILON)
    unit = centered * scale
    gain = w["gain"][...]
    out[...] = ((unit * gain + w["shift"][...]) * live[...]).astype(BF16)
    d_out = cot[...].astype(F32)
    tilted = d_out * unit
    scaled = d_out * gain
    flat = jnp.sum(scaled, -1, keepdims=True) * (1.0 / features)
    slant = jnp.sum(tilted * gain, -1, keepdims=True) * (1.0 / features)
    d_sum = ((scaled - flat - unit * slant) * scale) * inside
    g_norm[...] += jnp.concatenate([col_sum(tilted), col_sum(d_out)], 0)
    d_three = d_sum.astype(BF16)
    g_third[...] += t_dot(o_two, d_three)
    d_two = (dot_t(d_three, w["third"][...]) * slope_two).astype(BF16)
    g_second[...] += t_dot(o_one, d_two)
    d_one = (dot_t(d_two, w["second"][...]) * slope_one).astype(BF16)
    g_edge[...] += t_dot(feats, d_one)
    spread[...] += t_dot(hot, d_one)
    grad[...] = d_sum + dot_t(d_one, w["edge"][...])

    @pl.when(step == pl.num_programs(0) - 1)
    def _():
        places = window.shape[0]
        own_spread = spread[pl.ds(places, rows), :]
        g_own[...] = t_dot(window[pl.ds(REACH, rows), :], own_spread.astype(BF16))
        g_far[...] = t_dot(window[...], spread[pl.ds(0, places), :].astype(BF16))
        d_own[...] = dot_wide(own_spread, w["own"][...], True)


def edge_pass(features, window, hot, edges, cot, live, weights):
    places, width = window.shape
    rows = places - 2 * REACH
    total = edges.shape[0]
    size = total // (rows // BLOCK)
    args = [window, hot, edges, cot, live] + [weights[name] for name in EDGE_WEIGHTS]
    specs = [whole(window)] + [by_rows(a, size) for a in args[1:5]] + [whole(a) for a in args[5:]]
    out = shape((total, LANES), BF16)
    grad = shape((total, LANES), F32)
    square = shape((LANES, LANES), F32)
    tall = shape((width, LANES), F32)
    kept = (square,) * 4 + (shape((2, LANES), F32), tall, tall, shape((rows, width), F32))
    return pl.pallas_call(
        functools.partial(edge_kernel, rows, features),
        grid=(rows // BLOCK,),
        out_shape=(out, grad) + kept,
        in_specs=specs,
        out_specs=(by_rows(out, size), by_rows(grad, size)) + tuple(whole(k) for k in kept),
        scratch_shapes=[pltpu.VMEM((LANES, LANES), BF16)],
        compiler_params=pltpu.CompilerParams(vmem_limit_bytes=VMEM),
        name="edge_pass",
    )(*args)


def node_grad_kernel(
    cot, d_own, d_far, edge_far, summed, second, pre_expand, pooled, counts, third, expand, reduce_w,
    gain_one, gain_two, ds_out, du_out, slot_out, g_third, small,
):
    grad = cot[...].astype(F32) + d_own[...] + dot_wide(d_far[...], edge_far[...], True)
    unit, scale = norm_parts(second[...])
    dw = norm_back(grad, unit, scale, gain_two[...])
    gain_grad_two, shift_grad_two = col_sum(grad * unit), col_sum(grad)
    ds = dw.astype(BF16)
    ds_out[...] = ds
    _, slope = gelu_and_slope(pre_expand[...])
    dq = (dot_t(ds, reduce_w[...]) * slope).astype(BF16)
    dv = dw + dot_t(dq, expand[...])
    unit, scale = norm_parts(summed[...])
    du = norm_back(dv, unit, scale, gain_one[...])
    du_out[...] = du
    dm = (du / counts[...]).astype(BF16)
    slot_out[...] = dot_t(dm, third[...])
    g_third[...] = t_dot(jnp.concatenate(two_parts(pooled[...]), 0), jnp.concatenate([dm, dm], 0)).astype(
        BF16
    )
    width = cot.shape[1]
    small[...] = jnp.zeros(small.shape, F32)
    small[2:3, :] = col_sum(counts[...] * dm.astype(F32))
    small[3:4, :] = col_sum(dv * unit)
    small[4:5, :] = col_sum(dv)
    dq_sum = col_sum(dq.astype(F32))
    for part in range(dq_sum.shape[1] // width):
        small[5 + part : 6 + part, :] = dq_sum[:, part * width : (part + 1) * width]
    small[9:10, :] = col_sum(ds.astype(F32))
    small[10:11, :] = gain_grad_two
    small[11:12, :] = shift_grad_two


def node_grad(cot, d_own, d_far, edge_far, summed, second, pre_expand, pooled, counts, weights):
    rows, width = cot.shape
    hidden = weights["third"].shape[0]
    args = [cot, d_own, d_far, edge_far, summed, second, pre_expand, pooled, counts]
    args += [weights[n] for n in ("third", "expand", "reduce", "gain_one", "gain_two")]
    outs = (
        shape((rows, width), BF16),
        shape((rows, width), F32),
        shape((rows, hidden), F32),
        shape((hidden, width), BF16),
        shape((16, width), F32),
    )
    return pl.pallas_call(
        node_grad_kernel,
        out_shape=outs,
        in_specs=[pl.BlockSpec(memory_space=pltpu.VMEM)] * len(args),
        out_specs=tuple(pl.BlockSpec(memory_space=pltpu.VMEM) for _ in outs),
        compiler_params=pltpu.CompilerParams(vmem_limit_bytes=VMEM),
        name="node_grad",
    )(*args)


def pack_rows(pack, first, second, third, e_first, e_second, e_third):
    def cut(pieces, start, stop):
        at, got = 0, []
        for piece in pieces:
            low, high = max(start, at), min(stop, at + piece.shape[0])
            if low < high:
                got.append(piece[low - at : high - at])
            at += piece.shape[0]
        return jnp.concatenate(got, 0) if len(got) > 1 else got[0]

    for half in range(CORES):
        at = 0
        for pieces in (first, (second,), (third,)):
            size = sum(p.shape[0] for p in pieces) // CORES
            pack[half, pl.ds(at, size), :] = cut(pieces, half * size, (half + 1) * size).astype(BF16)
            at += size
        size = sum(p.shape[0] for p in e_first) // (2 * CORES)
        for side in range(2):
            start = (2 * half + side) * size
            pack[half, pl.ds(at, size), pl.ds(side * LANES, LANES)] = cut(
                e_first, start, start + size
            ).astype(BF16)
        at += size
        size = e_second.shape[0] // CORES
        for side, piece in enumerate((e_second, e_third)):
            pack[half, pl.ds(at, size), pl.ds(side * LANES, LANES)] = piece[
                half * size : (half + 1) * size
            ].astype(BF16)
        at += size
    return at


def message_grad_kernel(
    rows, features, window, onehot, edges, act, slope_one, slope_two, edge_grad, slot_grad, du,
    far, own, edge_w, second_w, g_third, small, e_edge, e_second, e_third, e_norm, e_own, e_far,
    grad, pack, spread, d_own, g_second, g_edge, g_bias,
):
    step = pl.program_id(0)

    @pl.when(step == 0)
    def _():
        for total in (spread, g_second, g_edge, g_bias):
            total[...] = jnp.zeros(total.shape, F32)

    slots = onehot.shape[0] // BLOCK
    hidden = act.shape[1]
    coming = slot_grad[pl.ds(step * BLOCK, BLOCK), :]
    coming = jnp.broadcast_to(coming[:, None, :], (BLOCK, slots, hidden)).reshape(BLOCK * slots, hidden)
    dp_two_f = coming * slope_two[...].astype(F32)
    g_bias[...] += col_sum(dp_two_f)
    dp_two = dp_two_f.astype(BF16)
    g_second[...] += t_dot(act[...], dp_two)
    dp_one = (dot_t(dp_two, second_w[...]) * slope_one[...].astype(F32)).astype(BF16)
    spread[...] += t_dot(onehot[...], dp_one)
    g_edge[...] += t_dot(edges[...], dp_one)
    grad[...] = edge_grad[...] + dot_t(dp_one, edge_w[...])

    @pl.when(step == pl.num_programs(0) - 1)
    def _():
        places = window.shape[0]
        own_spread = spread[pl.ds(places, rows), :]
        g_own = t_dot(window[pl.ds(REACH, rows), :], own_spread.astype(BF16))
        g_far = t_dot(window[...], spread[pl.ds(0, places), :].astype(BF16))
        d_own[...] = du[...] + dot_wide(own_spread, own[...], True)
        at = pack_rows(
            pack,
            (g_own, g_far, g_edge[pl.ds(0, features), :]),
            g_second[...],
            g_third[...],
            (e_own[...], e_far[...], e_edge[pl.ds(0, features), :]),
            e_second[pl.ds(0, features), :],
            e_third[pl.ds(0, features), :],
        )
        ones = [r[features : features + 1, :] for r in (e_edge, e_second, e_third)]
        tail = jnp.concatenate(
            [
                g_edge[features : features + 1, :],
                g_bias[...],
                small[2:12, :],
                jnp.concatenate([ones[0], ones[1]], 1),
                jnp.concatenate([ones[2], e_norm[0:1, :]], 1),
                jnp.concatenate([e_norm[1:2, :], jnp.zeros((1, LANES), F32)], 1),
                jnp.zeros((1, 2 * LANES), F32),
            ],
            0,
        ).astype(BF16)
        for half in range(CORES):
            pack[half, pl.ds(at, 16), :] = tail
            rest = pack.shape[1] - at - 16
            if rest:
                pack[half, pl.ds(at + 16, rest), :] = jnp.zeros((rest, pack.shape[2]), BF16)


def pack_size(count, features, width, hidden):
    used = (2 * width + features) // 2 + hidden // 2 + width // 2
    used += (2 * width + features) // 4 + features // 2 + 16
    part = -(-used // (2 * count * 16)) * 16
    return used, part


def message_grad(count, features, window, hot, edges, act, slope_one, slope_two, edge_grad, slot_grad,
                 du, weights, g_third, small, edge_grads):
    places, width = window.shape
    rows = places - 2 * REACH
    total, hidden = act.shape
    size = total // (rows // BLOCK)
    args = [window, hot, edges, act, slope_one, slope_two, edge_grad, slot_grad, du]
    args += [weights[n] for n in ("far", "own", "edge_plain", "second")] + [g_third, small] + edge_grads
    specs = [whole(window)] + [by_rows(a, size) for a in args[1:7]] + [whole(a) for a in args[7:]]
    _, part = pack_size(count, features, width, hidden)
    grad = shape((total, LANES), F32)
    kept = (
        shape((CORES, 2 * count * part, width), BF16),
        shape((LANES, hidden), F32),
        shape((rows, width), F32),
    )
    return pl.pallas_call(
        functools.partial(message_grad_kernel, rows, features),
        grid=(rows // BLOCK,),
        out_shape=(grad,) + kept,
        in_specs=specs,
        out_specs=(by_rows(grad, size),) + tuple(whole(k) for k in kept),
        scratch_shapes=[
            pltpu.VMEM((hidden, hidden), F32),
            pltpu.VMEM((LANES, hidden), F32),
            pltpu.VMEM((1, hidden), F32),
        ],
        compiler_params=pltpu.CompilerParams(vmem_limit_bytes=VMEM),
        name="message_grad",
    )(*args)


def wide_grad_kernel(normed, ds, expand, expand_bias, reduce_w, g_expand, g_reduce):
    chunk, at = pl.program_id(0), pl.program_id(1)
    half = lax.axis_index("half")
    width = normed.shape[1]
    part = expand.shape[1] // pl.num_programs(1)
    count = pl.num_programs(1) // CORES
    block = lax.rem(at + half * count, CORES * count)
    here = pl.ds(pl.multiple_of(block * part, part), part)

    @pl.when((chunk == 0) & (at == 0))
    def _():
        g_expand[...] = jnp.zeros(g_expand.shape, F32)
        g_reduce[...] = jnp.zeros(g_reduce.shape, F32)

    pre = dot(normed[...], expand[:, here]) + expand_bias[:, here]
    act, slope = gelu_and_slope(pre)
    dq = (dot_t(ds[...], reduce_w[here, :]) * slope).astype(BF16)
    mine = pl.ds(pl.multiple_of(half * (width // CORES), width // CORES), width // CORES)
    g_expand[:, here] += t_dot(normed[:, mine], dq)

    @pl.when(at < count)
    def _():
        rows = pl.ds(pl.multiple_of(at * part, part), part)
        g_reduce[rows, :] += t_dot(act.astype(BF16), ds[...])


def wide_grad(normed, ds, weights, chunk):
    total, width = normed.shape
    expand, bias, reduce_w = weights["expand"], weights["expand_bias"], weights["reduce"]
    inner = expand.shape[1]
    blocks = inner // 256
    row_spec = pl.BlockSpec((chunk, width), lambda i, j: (i, 0))
    fixed = lambda a: pl.BlockSpec(a.shape, lambda i, j: (0, 0))
    outs = (shape((width // CORES, inner), F32), shape((inner // CORES, width), F32))
    return pl.pallas_call(
        wide_grad_kernel,
        grid=(total // chunk, blocks),
        out_shape=outs,
        in_specs=[row_spec, row_spec, fixed(expand), fixed(bias), fixed(reduce_w)],
        out_specs=tuple(fixed(o) for o in outs),
        compiler_params=pltpu.CompilerParams(vmem_limit_bytes=VMEM),
        name="wide_grad",
    )(normed, ds, expand, bias, reduce_w)


def chip_dims(count):
    side = 1
    while 2 * (2 * side) ** 3 <= count and count % (4 * side * side) == 0:
        side *= 2
    return {"z": count // (side * side), "y": side, "x": side}


ORDERS = (("x", "y", "z"), ("y", "x", "z"))


def sum_kernel(
    dims, part, pack, out_half, grad_half, table, d_own, far,
    total_out, edges_out, grads_out, nodes_out,
    acc, got, landed, away, gathered, rows_in, row_total, node_buf, node_half, edges_in, grads_in,
    pair_send, pair_recv, step_send, step_recv, line_send, line_recv,
):
    res, half = lax.axis_index("res"), lax.axis_index("half")
    place = {
        "x": lax.rem(res, dims["x"]),
        "y": lax.rem(res // dims["x"], dims["y"]),
        "z": res // (dims["x"] * dims["y"]),
    }
    stride = {"x": 1, "y": dims["x"], "z": dims["x"] * dims["y"]}
    count = dims["x"] * dims["y"] * dims["z"]
    rows = d_own.shape[0]
    partner = (res, 1 - half)

    def peer(axis, ahead):
        to = lax.rem(place[axis] + ahead, dims[axis])
        return to, (res + (to - place[axis]) * stride[axis], half)

    barrier = pltpu.get_barrier_semaphore()
    greet_line()
    pl.semaphore_signal(barrier, inc=1, device_id=partner, device_id_type=MESH)
    others = 1
    for axis in dims:
        for ahead in range(1, dims[axis]):
            pl.semaphore_signal(barrier, inc=1, device_id=peer(axis, ahead)[1], device_id_type=MESH)
            others += 1
    pl.semaphore_wait(barrier, others + line_count())

    def pair_copy(at, source, target):
        copy = pltpu.make_async_remote_copy(
            src_ref=source,
            dst_ref=target,
            send_sem=pair_send.at[at],
            recv_sem=pair_recv.at[at],
            device_id=partner,
            device_id_type=MESH,
        )
        copy.start()
        return copy

    span = count * part
    parts = [
        pair_copy(p, pack.at[1 - half, pl.ds(p * span, span)], got.at[pl.ds(p * span, span)])
        for p in range(2)
    ]
    returns = start_returns(table, rows_in, line_send, line_recv, rows)
    pairs = [pair_copy(2, out_half.at[1 - half], edges_in), pair_copy(3, grad_half.at[1 - half], grads_in)]

    sem = 0
    regions = []
    for p in range(2):
        parts[p].wait()
        here = pl.ds(p * span, span)
        acc[here, :] = (pack[half, here, :].astype(F32) + got[here, :].astype(F32)).astype(BF16)
        regions.append((p * span, span))
    bases = [p * span for p in range(2)]
    for level in range(3):
        started = []
        for p in range(2):
            axis = ORDERS[p][level]
            start, size = regions[p]
            share = size // dims[axis]
            copies = []
            for ahead in range(1, dims[axis]):
                to, device = peer(axis, ahead)
                copy = pltpu.make_async_remote_copy(
                    src_ref=acc.at[pl.ds(pl.multiple_of(start + to * share, 16), share)],
                    dst_ref=landed.at[pl.ds(bases[p], share)],
                    send_sem=step_send.at[sem],
                    recv_sem=step_recv.at[sem],
                    device_id=device,
                    device_id_type=MESH,
                )
                copy.start()
                copies.append((copy, bases[p], share))
                bases[p] += share
                sem += 1
            started.append(copies)
        for p in range(2):
            axis = ORDERS[p][level]
            start, size = regions[p]
            share = size // dims[axis]
            mine = pl.multiple_of(start + place[axis] * share, 16)
            total = acc[pl.ds(mine, share), :].astype(F32)
            for copy, base, _ in started[p]:
                copy.wait()
                total = total + landed[pl.ds(base, share), :].astype(F32)
            acc[pl.ds(mine, share), :] = total.astype(BF16)
            regions[p] = (mine, share)
        if level == 0:
            finish_returns(table, rows_in, row_total, line_send, line_recv, rows, returns)
            grad = d_own[...] + dot_wide(row_total[...], far[...], True)
            wide = grad.shape[1] // CORES
            node_buf[0] = grad[:, :wide]
            node_buf[1] = grad[:, wide:]
            pairs.append(pair_copy(4, node_buf.at[1 - half], node_half))

    for p in range(2):
        mine, share = regions[p]
        gathered[pl.ds(mine, share), :] = acc[pl.ds(mine, share), :]
    for level in (2, 1, 0):
        started = []
        for p in range(2):
            axis = ORDERS[p][level]
            mine, share = regions[p]
            for ahead in range(1, dims[axis]):
                _, device = peer(axis, ahead)
                copy = pltpu.make_async_remote_copy(
                    src_ref=gathered.at[pl.ds(mine, share)],
                    dst_ref=gathered.at[pl.ds(mine, share)],
                    send_sem=step_send.at[sem],
                    recv_sem=step_recv.at[sem],
                    device_id=device,
                    device_id_type=MESH,
                )
                copy.start()
                started.append(copy)
                sem += 1
            regions[p] = (pl.multiple_of(mine - place[axis] * share, 16), share * dims[axis])
        for copy in started:
            copy.wait()
    for copy in pairs:
        copy.wait()
    total_out[...] = gathered[...]
    edges_out[half] = out_half[half]
    edges_out[1 - half] = edges_in[...]
    grads_out[half] = grad_half[half]
    grads_out[1 - half] = grads_in[...]
    nodes_out[half] = node_buf[half]
    nodes_out[1 - half] = node_half[...]


def sum_over_chips(count, pack, out_half, grad_half, table, d_own, far):
    dims = chip_dims(count)
    total, width = pack.shape[1:]
    part = total // (2 * count)
    rows = d_own.shape[0]
    steps = 2 * 2 * sum(size - 1 for size in dims.values())
    vmem = pl.BlockSpec(memory_space=pltpu.VMEM)
    outs = (
        shape((total, width), BF16),
        shape(out_half.shape, BF16),
        shape(grad_half.shape, F32),
        shape((CORES, rows, width // CORES), F32),
    )
    return pl.pallas_call(
        functools.partial(sum_kernel, dims, part),
        out_shape=outs,
        in_specs=[vmem] * 6,
        out_specs=(vmem,) * 4,
        scratch_shapes=[
            pltpu.VMEM((total, width), BF16),
            pltpu.VMEM((total, width), BF16),
            pltpu.VMEM((total, width), BF16),
            pltpu.VMEM((16, width), BF16),
            pltpu.VMEM((total, width), BF16),
            pltpu.VMEM(table.shape, F32),
            pltpu.VMEM((rows, table.shape[1]), F32),
            pltpu.VMEM((CORES, rows, width // CORES), F32),
            pltpu.VMEM((rows, width // CORES), F32),
            pltpu.VMEM(out_half.shape[1:], BF16),
            pltpu.VMEM(grad_half.shape[1:], F32),
            pltpu.SemaphoreType.DMA((5,)),
            pltpu.SemaphoreType.DMA((5,)),
            pltpu.SemaphoreType.DMA((steps,)),
            pltpu.SemaphoreType.DMA((steps,)),
            pltpu.SemaphoreType.DMA((4,)),
            pltpu.SemaphoreType.DMA((4,)),
        ],
        compiler_params=pltpu.CompilerParams(
            collective_id=7, has_side_effects=True, vmem_limit_bytes=VMEM
        ),
        name="sum_over_chips",
    )(pack, out_half, grad_half, table, d_own, far)


def as_row(vector, width=None):
    vector = vector.astype(F32)
    if width is not None:
        vector = jnp.pad(vector, (0, width - vector.shape[0]))
    return vector[None, :]


def spread_slots(values, fill=0):
    rows, slots = values.shape[:2]
    each = slots // CORES
    room = -(-each // 16) * 16
    values = values.reshape((rows, CORES, each) + values.shape[2:])
    pads = [(0, 0), (0, 0), (0, room - each)] + [(0, 0)] * (values.ndim - 3)
    values = jnp.pad(values, pads, constant_values=fill)
    return values.reshape((rows * CORES * room,) + values.shape[3:])


def body(
    nodes, edges, neighbours, counts,
    message_first, message_first_bias, message_second, message_second_bias, message_third, message_third_bias,
    node_norm_gain, node_norm_shift, expand_weight, expand_bias, reduce_weight, reduce_bias,
    output_norm_gain, output_norm_shift,
    edge_first, edge_first_bias, edge_second, edge_second_bias, edge_third, edge_third_bias,
    edge_norm_gain, edge_norm_shift, cot_nodes, cot_edges,
):
    res, half, count = lax.axis_index("res"), lax.axis_index("half"), lax.axis_size("res")
    rows_dev, width = nodes.shape
    slots, features = edges.shape[1:]
    hidden = message_second.shape[0]
    rows = rows_dev // CORES
    room = -(-(slots // CORES) // 16) * 16

    def mine(values):
        return lax.dynamic_slice_in_dim(values, half * rows, rows, 0)

    own = mine(nodes)
    own_counts = mine(counts)
    base = res * rows_dev + half * rows - REACH
    picks = spread_slots(mine(neighbours) - base, -1)[:, None]
    used = lax.broadcasted_iota(jnp.int32, (rows, slots), 1) < own_counts[:, None]
    live_flat = spread_slots(used.astype(F32))
    live, live_row = live_flat[:, None], live_flat[None, :]
    counts_f = own_counts.astype(F32)[:, None]
    lane = lax.broadcasted_iota(jnp.int32, (1, 1, LANES), 2)
    feats = jnp.pad(mine(edges), ((0, 0), (0, 0), (0, LANES - features)))
    feats = spread_slots(jnp.where(lane == features, jnp.ones((), BF16), feats))
    cots = mine(cot_edges) * used.astype(BF16)[:, :, None]
    cots = spread_slots(jnp.pad(cots, ((0, 0), (0, 0), (0, LANES - features))))

    node_w = {
        "own": message_first[:width],
        "far": message_first[width : 2 * width],
        "edge": jnp.concatenate(
            [
                message_first[2 * width :],
                message_first_bias[None],
                jnp.zeros((LANES - features - 1, hidden), BF16),
            ],
            0,
        ),
        "edge_plain": jnp.pad(message_first[2 * width :], ((0, LANES - features), (0, 0))),
        "second": message_second,
        "second_bias": as_row(message_second_bias),
        "third": message_third,
        "third_bias": as_row(message_third_bias),
        "gain_one": as_row(node_norm_gain),
        "shift_one": as_row(node_norm_shift),
        "expand": expand_weight,
        "expand_bias": as_row(expand_bias),
        "reduce": reduce_weight,
        "reduce_bias": as_row(reduce_bias),
        "gain_two": as_row(output_norm_gain),
        "shift_two": as_row(output_norm_shift),
    }

    def square(weight, bias=None):
        weight = jnp.pad(weight, ((0, 0), (0, LANES - weight.shape[1])))
        parts = [weight]
        if bias is not None:
            parts.append(bias[None, :])
        have = sum(p.shape[0] for p in parts)
        return jnp.concatenate(parts + [jnp.zeros((LANES - have, LANES), BF16)], 0)

    def padded(vector):
        return jnp.pad(vector, (0, LANES - features))

    tall = jnp.pad(edge_first[: 2 * width], ((0, 0), (0, LANES - features)))
    take_one = jnp.where(jnp.arange(LANES) == features, -jnp.ones((), BF16), padded(edge_third_bias))
    edge_w = {
        "own": tall[:width],
        "far": tall[width:],
        "edge": square(edge_first[2 * width :]),
        "edge_x": square(edge_first[2 * width :], padded(edge_first_bias)),
        "second": square(edge_second),
        "second_x": square(edge_second, padded(edge_second_bias)),
        "third": square(edge_third),
        "third_x": square(edge_third, take_one),
        "gain": as_row(edge_norm_gain, LANES),
        "shift": as_row(edge_norm_shift, LANES),
    }

    window = fetch_window(own, 1)
    fed, hot = node_pass(True, window, picks, feats, live, live_row, counts_f, node_w)
    fed_window = fetch_window(fed, 2)
    state, act, slope_one, slope_two, pooled, summed, pre_expand, second, normed = node_pass(
        False, fed_window, hot, feats, live, live_row, counts_f, node_w
    )
    state_window = fetch_window(state, 3)
    normed_all = lax.all_gather(normed, ("res", "half"), tiled=True)
    out, grad, spread, e_edge, e_second, e_third, e_norm, e_own, e_far, d_own = edge_pass(
        features, state_window, hot, feats, cots, live, edge_w
    )
    d_far = return_rows(spread[: rows + 2 * REACH], 4)
    ds, du, slot_grad, g_third, small = node_grad(
        mine(cot_nodes), d_own, d_far, edge_w["far"], summed, second, pre_expand, pooled, counts_f, node_w
    )
    ds_all = lax.all_gather(ds, ("res", "half"), tiled=True)
    grad, pack, spread, d_own = message_grad(
        count, features, fed_window, hot, feats, act, slope_one, slope_two, grad, slot_grad, du, node_w,
        g_third, small, [e_edge, e_second, e_third, e_norm, e_own, e_far],
    )

    def by_half(values):
        values = values.reshape(rows, CORES, room, LANES)
        return jnp.transpose(values, (1, 0, 2, 3))

    sums, out_pair, grad_pair, node_pair = sum_over_chips(
        count, pack, by_half(out), by_half(grad), spread[: rows + 2 * REACH], d_own, node_w["far"]
    )
    g_expand, g_reduce = wide_grad(normed_all, ds_all, node_w, rows_dev * min(count, 16))

    each = slots // CORES
    at = 0
    taken = []
    for size in ((2 * width + features) // 2, hidden // 2, hidden // 2):
        taken.append(sums[at : at + size].astype(F32))
        at += size
    size = (2 * width + features) // 4
    first = sums[at : at + size]
    e_first_grad = jnp.concatenate([first[:, :features], first[:, LANES : LANES + features]], 0).astype(F32)
    at += size
    both = sums[at : at + features // 2].astype(F32)
    at += features // 2
    tail = sums[at : at + 16].astype(F32)

    def share(row, size):
        return lax.dynamic_slice_in_dim(row, half * (size // CORES), size // CORES, 0)

    inner = expand_weight.shape[1]
    wide_bias = tail[5 : 5 + inner // width].reshape(-1)
    state_out = lax.dynamic_slice(
        state_window, (REACH - half * rows, half * (width // CORES)), (rows_dev, width // CORES)
    )
    return (
        state_out,
        out_pair[:, :, :each, :features].reshape(rows_dev, each, features),
        node_pair.reshape(rows_dev, width // CORES),
        grad_pair[:, :, :each, :features].reshape(rows_dev, each, features),
        taken[0],
        share(tail[0], hidden),
        taken[1],
        share(tail[1], hidden),
        taken[2],
        share(tail[2], width),
        share(tail[3], width),
        share(tail[4], width),
        g_expand,
        share(wide_bias, inner),
        g_reduce,
        share(tail[9], width),
        share(tail[10], width),
        share(tail[11], width),
        e_first_grad,
        share(tail[12, :features], features),
        both[:, :features],
        share(tail[12, LANES : LANES + features], features),
        both[:, LANES : LANES + features],
        share(tail[13, :features], features),
        share(tail[13, LANES : LANES + features], features),
        share(tail[14, :features], features),
    )


def solution(mesh):
    rows, slots = P("res", None), P("res", None, None)
    copied = P()
    down, vec = P("half", None), P("half")
    return jax.shard_map(
        body,
        mesh=mesh,
        in_specs=(rows, slots, rows, P("res")) + (copied,) * 22 + (rows, slots),
        out_specs=(
            P("res", "half"),
            P("res", "half", None),
            P("res", "half"),
            P("res", "half", None),
            down, vec, down, vec, down, vec, vec, vec, down, vec, down, vec, vec, vec,
            down, vec, down, vec, down, vec, vec, vec,
        ),
        check_vma=False,
    )
```

time: 1010 us -> 257 us (0.25)
  waiting for transfers between devices: 461 us -> 0.04 us
  Pallas kernels: 0 us -> 185 us
  matrix products: 174 us -> 0 us
  other arithmetic: 105 us -> 13.6 us
  blocking collectives: 82.4 us -> 0 us
  local copies, waits for them, and re-layouts: 121 us -> 42.9 us
  starting transfers between devices: 32.5 us -> 0.08 us
    psum x3 -> x0, waiting for transfers between devices: 399 us -> none  [the longest x1 203 us: body(): summed_grads = lax.psum(all_grads, 'res')]
    pallas_call x0 -> x11, Pallas kernels: none -> 185 us  [the longest x1 67.8 us: sum_over_chips(): pl.pallas_call(functools.partial(sum_kernel, dims, part), out_shape=outs,...]
    dot_general x26 -> x0, matrix products: 174 us -> none  [the longest x7 68.9 us: slot_apply(): jnp.einsum('rkc,ch->rkh', left, weight, preferred_element_type=jnp.float32)]
    psum x1 -> x0, blocking collectives: 78.4 us -> none  [body(): summed_grads = lax.psum(all_grads, 'res')]
    gather x6 -> x0, local copies, waits for them, and re-layouts: 77.6 us -> none  [the longest x4 51.7 us: three_layers(): far_rows = table[neighbours]]
    reduce_scatter x11 -> x0, waiting for transfers between devices: 44.8 us -> none  [the longest x7 35.7 us: body(): lax.psum_scatter(summed_grads, 'half', scatter_dimension=0, tiled=True)]
    scatter-add x1 -> x0, other arithmetic: 38.2 us -> none  [three_back(): far_table = jnp.zeros((total_rows, width), jnp.float32).at[neighbours.res...]
    ppermute x10 -> x0, starting transfers between devices: 31.9 us -> none  [the longest x3 15.7 us: with_halo(): lax.ppermute(lax.slice_in_dim(block, block.shape[dim] - width, None, axis...]
  transfers between devices with their start and end apart: 25 -> 2, of which waited for: 14 -> 0; matrix products, arithmetic and copies ran while one was open for 23% -> 14% of each run, Pallas kernels for 0% -> 46%
where the time goes in v1:
time: 257 us; the launch traced here: 256 us
  Pallas kernels  185 us (72%)
  local copies, waits for them, and re-layouts  42.9 us (17%)
  between operations  14.6 us (6%)
  other arithmetic  13.6 us (5%)
    pallas_call x1, Pallas kernels, sum_over_chips(): pl.pallas_call(functools.partial(sum_kernel, dims, part), out_shape=outs,...  67.8 us
    pallas_call x2, Pallas kernels, node_pass(): pl.pallas_call(functools.partial(kernel, rows), grid=(rows // BLOCK,), ou...  30.5 us
    pallas_call x3, Pallas kernels, fetch_window(): pl.pallas_call(halo_kernel, out_shape=jax.ShapeDtypeStruct((rows + 2 * RE...  22.3 us
    pallas_call x1, Pallas kernels, wide_grad(): pl.pallas_call(wide_grad_kernel, grid=(total // chunk, blocks), out_shape...  20.9 us
    pallas_call x1, Pallas kernels, message_grad(): pl.pallas_call(functools.partial(message_grad_kernel, rows, features), gr...  15.3 us
    pallas_call x1, Pallas kernels, edge_pass(): pl.pallas_call(functools.partial(edge_kernel, rows, features), grid=(rows...  14.9 us
    unnamed x59, local copies, waits for them, and re-layouts  8.98 us
    dynamic_slice x14, local copies, waits for them, and re-layouts, share(): lax.dynamic_slice_in_dim(row, half * (size // CORES), size // CORES, 0)  8.01 us
  transfers between devices with their start and end apart: 2, of which 0 were waited for; matrix products, arithmetic and copies ran while one was open for 14% of the time, Pallas kernels for 46%

profile of v1, /device:TPU:0, one launch (start us, length us, event | category | flops | bytes accessed | tf_op | source)
XLA Modules:
  0.0 256.0 jit_solution(7146521498555138196)
XLA Ops:
  7.3 2.2 fusion.7
  9.8 0.7 broadcast_in_dim_reshape.10.live_row
  10.5 2.8 %broadcast_in_dim_reshape.13.live = f32[3072,1]{1,0:T(8,128)} reshape(f32[48,2,32]{2,1,0:T(2,128)S(1)} %pad_convert_fusion) | data formatting | bytes 24576 | tf_op jit(solution)/shard_map/broadcast_in_dim;reshape | solution.py:964
  13.3 0.6 constant_dynamic-slice_fusion.13
  13.9 7.8 %fetch_window.3.window = bf16[176,512]{1,0:T(8,128)(2,1)} custom-call(bf16[48,512]{1,0:T(8,128)(2,1)} %get-tuple-element.190.own_ref), custom_call_target="tpu_custom_call" | custom-call | tf_op jit(solution)/shard_map/fetch_window/pallas_call | solution.py:158
  22.0 2.8 %broadcast_in_dim_reshape.12.picks = s32[3072,1]{1,0:T(8,128)} reshape(s32[48,2,32]{2,1,0:T(2,128)S(1)} %pad.68.clone) | data formatting | bytes 24576 | tf_op jit(solution)/shard_map/broadcast_in_dim;reshape | solution.py:961
  24.7 2.3 dynamic-slice_multiply_fusion
  27.0 0.3 pad_select_fusion
  27.5 0.5 copy.66
  28.0 0.7 copy.68.counts
  28.7 0.6 broadcast_in_dim.115
  29.3 0.5 broadcast_in_dim.116
  29.9 0.6 broadcast_in_dim.117
  30.5 0.6 broadcast_in_dim.118
  31.1 0.6 broadcast_in_dim.119
  31.7 0.6 broadcast_in_dim.120
  32.3 0.6 broadcast_in_dim.121
  32.9 0.6 broadcast_in_dim.122
  33.4 1.3 pad.70
  34.8 0.8 fusion.9
  35.7 13.7 %node_pass_first.1 = (bf16[48,512]{1,0:T(8,128)(2,1)}, bf16[3072,256]{1,0:T(8,128)(2,1)}) custom-call(bf16[176,512]{1,0:T(8,128)(2,1)} %fetch_window.3.window, s32[3072,1]{1,0:T(8,128)} %broadcast_in_dim_reshape.12.picks, bf16[3072,256]{1,0:T(8,128)(2,1)} %bitcast.52, f32[1,3072]{1,0:T(1,128)} %broadcast_in_dim_reshape.10.live_row, f32[48,1]{1,0:T(8,128)} %copy.68.counts, ...), custom_call_target="tpu_custom_call" | custom-call | tf_op jit(solution)/shard_map/node_pass_first/pallas_call | solution.py:408
  49.4 7.2 %fetch_window.4.window = bf16[176,512]{1,0:T(8,128)(2,1)} custom-call(bf16[48,512]{1,0:T(8,128)(2,1)} %get-tuple-element.62.own_ref), custom_call_target="tpu_custom_call" | custom-call | tf_op jit(solution)/shard_map/fetch_window/pallas_call | solution.py:158
  56.6 16.8 %node_pass_second.1 = (bf16[48,512]{1,0:T(8,128)(2,1)}, bf16[3072,512]{1,0:T(8,128)(2,1)}, bf16[3072,512]{1,0:T(8,128)(2,1)}, bf16[3072,512]{1,0:T(8,128)(2,1)},...) custom-call(bf16[176,512]{1,0:T(8,128)(2,1)} %fetch_window.4.window,, ...), custom_call_target="tpu_custom_call" | custom-call | tf_op jit(solution)/shard_map/node_pass_second/pallas_call | solution.py:408
  73.5 7.2 %fetch_window.5.window = bf16[176,512]{1,0:T(8,128)(2,1)} custom-call(bf16[48,512]{1,0:T(8,128)(2,1)} %get-tuple-element.64.own_ref), custom_call_target="tpu_custom_call" | custom-call | tf_op jit(solution)/shard_map/fetch_window/pallas_call | solution.py:158
  81.0 0.5 copy.71
  81.6 1.4 pad.74
  83.7 0.6 pad_convert_fusion.2
  84.2 0.6 pad_convert_fusion.1
  84.8 0.9 pad_slice_fusion
  85.7 0.9 maximum_maximum_fusion.3
  86.6 14.9 %edge_pass.1 = (bf16[3072,256]{1,0:T(8,128)(2,1)}, f32[3072,256]{1,0:T(8,128)}, f32[256,256]{1,0:T(8,128)}, f32[256,256]{1,0:T(8,128)}, f32[256,256]{1,0:T(8,128...) custom-call(bf16[176,512]{1,0:T(8,128)(2,1)} %fetch_window.5.window,, ...), custom_call_target="tpu_custom_call" | custom-call | tf_op jit(solution)/shard_map/edge_pass/pallas_call | solution.py:489
  101.5 1.6 slice.114.table_ref
  103.1 7.3 %return_rows.1.d_far = f32[48,256]{1,0:T(8,128)} custom-call(f32[176,256]{1,0:T(8,128)} %slice.114.table_ref), custom_call_target="tpu_custom_call" | custom-call | tf_op jit(solution)/shard_map/return_rows/pallas_call | solution.py:229
  110.5 5.9 %node_grad.1 = (bf16[48,512]{1,0:T(8,128)(2,1)}, f32[48,512]{1,0:T(8,128)}, f32[48,512]{1,0:T(8,128)}, bf16[512,512]{1,0:T(8,128)(2,1)}, f32[16,512]{1,0:T(8,128)}) custom-call(bf16[48,512]{1,0:T(8,128)(2,1)} %get-tuple-element.189.cot, f32[48,512]{1,0:T(8,128)} %get-tuple-element.69.d_own, f32[48,256]{1,0:T(8,128)} %return_rows.1.d_far, ...), custom_call_target="tpu_custom_call" | custom-call | tf_op jit(solution)/shard_map/node_grad/pallas_call | solution.py:547
  116.4 1.3 copy.88
  117.6 15.3 %message_grad.1 = (f32[3072,256]{1,0:T(8,128)}, bf16[2,1536,512]{2,1,0:T(8,128)(2,1)}, f32[256,512]{1,0:T(8,128)}, f32[48,512]{1,0:T(8,128)}) custom-call(bf16[176,512]{1,0:T(8,128)(2,1)} %fetch_window.4.window, bf16[3072,256]{1,0:T(8,128)(2,1)} %get-tuple-element.63.onehot, bf16[3072,256]{1,0:T(8,128)(2,1)} %bitcast.55, ...), custom_call_target="tpu_custom_call" | custom-call | tf_op jit(solution)/shard_map/message_grad/pallas_call | solution.py:673
  132.9 4.0 %copy.87 = f32[48,2,32,256]{3,2,0,1:T(8,128)} copy(f32[48,2,32,256]{3,2,1,0:T(8,128)} %bitcast.62) | data formatting | bytes 6291456 | tf_op jit(solution)/shard_map/reshape | solution.py:1046
  136.9 0.8 slice.115.table
  137.7 67.8 %sum_over_chips.1 = (bf16[1536,512]{1,0:T(8,128)(2,1)}, bf16[2,48,32,256]{3,2,1,0:T(8,128)(2,1)}, f32[2,48,32,256]{3,2,1,0:T(8,128)}, f32[2,48,256]{2,1,0:T(8,128)}) custom-call(bf16[2,1536,512]{2,1,0:T(8,128)(2,1)} %get-tuple-element.85.pack, bf16[2,48,32,256]{3,2,1,0:T(8,128)(2,1)} %bitcast.58, f32[2,48,32,256]{3,2,1,0:T(8,128)} %bitcast.56, ...), custom_call_target="tpu_custom_call" | custom-call | tf_op jit(solution)/shard_map/sum_over_chips/pallas_call | solution.py:892
  205.5 0.7 slice_convert_fusion.4
  206.2 1.2 fusion.6
  207.4 3.3 %copy.78 = bf16[96,30,192]{2,0,1:T(8,128)(2,1)} copy(bf16[96,30,192]{2,1,0:T(8,128)(2,1)} %bitcast.64) | data formatting | bytes 2211840
  210.8 3.3 %copy.79 = f32[96,30,192]{2,0,1:T(8,128)} copy(f32[96,30,192]{2,1,0:T(8,128)S(1)} %bitcast.61) | data formatting | bytes 4423680
  214.1 1.0 copy.80
  215.1 1.4 dynamic_slice.93
  216.5 0.6 dynamic_slice.106
  217.1 0.6 fusion.1
  217.7 0.6 fusion.2
  218.3 0.6 fusion.3
  218.9 0.6 fusion.4
  219.5 0.6 fusion.5
  220.1 0.6 constant_dynamic-slice_fusion.12
  220.6 0.6 constant_dynamic-slice_fusion.11
  221.2 0.6 constant_dynamic-slice_fusion.10
  221.8 0.6 constant_dynamic-slice_fusion.9
  222.3 0.6 constant_dynamic-slice_fusion.8
  222.9 0.6 constant_dynamic-slice_fusion.7
  223.5 0.6 constant_dynamic-slice_fusion.6
  224.0 0.6 constant_dynamic-slice_fusion.5
  224.6 0.7 fusion.8
  225.3 1.1 slice_convert_fusion.1
  226.4 1.2 slice_convert_fusion
  227.6 20.9 %wide_grad.1 = (f32[256,2048]{1,0:T(8,128)}, f32[1024,512]{1,0:T(8,128)}) custom-call(bf16[1536,512]{1,0:T(8,128)(2,1)} %all-gather.3.cloned.1.call-done.normed, bf16[1536,512]{1,0:T(8,128)(2,1)} %all-gather.5.cloned.1.call-done.ds, bf16[512,2048]{1,0:T(8,128)(2,1)} %expand.3, f32[1,2048]{1,0:T(1,128)} %bitcast.67, bf16[2048,512]{1,0:T(8,128)(2,1)} %reduce_w.3), custom_call_target="tpu_custom_call" | custom-call | tf_op jit(solution)/shard_map/wide_grad/pallas_call | solution.py:723
  248.5 0.6 copy.90
  (93 shorter events, 1.7 us)
Async XLA Ops:
  7.2 2.3 copy-start.19
  7.2 220.4 %all-gather.3.cloned.1.call-start = ((), (), s32[]{:S(2)}) async-start(), calls=%async_computation | async-start | bytes 1622016 | tf_op jit(solution)/shard_map/all_gather | solution.py:1031
  9.5 3.8 %copy-start.8 = (bf16[96,512]{1,0:T(8,128)(2,1)S(1)}, bf16[96,512]{1,0:T(8,128)(2,1)}, u32[]{:S(2)}) copy-start(bf16[96,512]{1,0:T(8,128)(2,1)} %param.54) | copy-start | bytes 294916
  9.5 3.8 %copy-start.9 = (bf16[96,512]{1,0:T(8,128)(2,1)S(1)}, bf16[96,512]{1,0:T(8,128)(2,1)}, u32[]{:S(2)}) copy-start(bf16[96,512]{1,0:T(8,128)(2,1)} %param.28) | copy-start | bytes 294916
  9.5 12.2 %copy-start.7 = (s32[96,60]{0,1:T(8,128)S(1)}, s32[96,60]{0,1:T(8,128)}, u32[]{:S(2)}) copy-start(s32[96,60]{0,1:T(8,128)} %param.30) | copy-start | bytes 69124
  27.4 1.4 copy-start.11
  27.4 1.4 copy-start.12
  27.4 1.9 copy-start.13
  27.4 2.5 copy-start.14
  27.4 3.0 %copy-start.15 = (bf16[512]{0:T(512)(128)(2,1)S(1)}, bf16[512]{0:T(512)(128)(2,1)}, u32[]{:S(2)}) copy-start(bf16[512]{0:T(512)(128)(2,1)} %param.39) | copy-start | bytes 3076
  27.4 3.6 %copy-start.10 = (bf16[2048]{0:T(1024)(128)(2,1)S(1)}, bf16[2048]{0:T(1024)(128)(2,1)}, u32[]{:S(2)}) copy-start(bf16[2048]{0:T(1024)(128)(2,1)} %param.41) | copy-start | bytes 12292
  27.5 4.2 %copy-start.16 = (bf16[512]{0:T(512)(128)(2,1)S(1)}, bf16[512]{0:T(512)(128)(2,1)}, u32[]{:S(2)}) copy-start(bf16[512]{0:T(512)(128)(2,1)} %param.43) | copy-start | bytes 3076
  27.5 4.8 %copy-start.17 = (bf16[512]{0:T(512)(128)(2,1)S(1)}, bf16[512]{0:T(512)(128)(2,1)}, u32[]{:S(2)}) copy-start(bf16[512]{0:T(512)(128)(2,1)} %param.44) | copy-start | bytes 3076
  27.5 5.4 %copy-start.18 = (bf16[512]{0:T(512)(128)(2,1)S(1)}, bf16[512]{0:T(512)(128)(2,1)}, u32[]{:S(2)}) copy-start(bf16[512]{0:T(512)(128)(2,1)} %param.45) | copy-start | bytes 3076
  33.4 1.4 slice-start.2
  73.4 154.2 %all-gather.5.cloned.1.call-start = ((), (), s32[]{:S(2)}) async-start(), calls=%async_computation.1 | async-start | bytes 1622016 | tf_op jit(solution)/shard_map/all_gather | solution.py:1039
  81.5 1.4 slice-start
  81.6 1.6 copy-start.20
  81.6 1.7 copy-start.4
  81.6 1.7 copy-start.5
  81.6 1.7 copy-start.21
  81.6 1.7 slice-start.1
  83.0 0.7 copy-start.22
  83.0 0.7 copy-start.23
  83.0 1.2 copy-start.24
  110.4 5.9 %copy-start.2 = (bf16[3072,256]{1,0:T(8,128)(2,1)S(1)}, bf16[3072,256]{1,0:T(8,128)(2,1)}, u32[]{:S(2)}) copy-start(bf16[3072,256]{1,0:T(8,128)(2,1)} %get-tuple-element.86) | copy-start | bytes 4718596
  132.9 4.0 %copy-start.3 = (f32[256,512]{1,0:T(8,128)S(1)}, f32[256,512]{1,0:T(8,128)}, u32[]{:S(2)}) copy-start(f32[256,512]{1,0:T(8,128)} %get-tuple-element.88) | copy-start | bytes 1572868
  206.2 4.5 %copy-start = (f32[2,48,32,256]{3,2,1,0:T(8,128)S(1)}, f32[2,48,32,256]{3,2,1,0:T(8,128)}, u32[]{:S(2)}) copy-start(f32[2,48,32,256]{3,2,1,0:T(8,128)} %get-tuple-element.92) | copy-start | bytes 9437188
  214.1 10.5 %copy-start.1 = (bf16[1536,512]{1,0:T(8,128)(2,1)S(1)}, bf16[1536,512]{1,0:T(8,128)(2,1)}, u32[]{:S(2)}) copy-start(bf16[1536,512]{1,0:T(8,128)(2,1)} %get-tuple-element.93) | copy-start | bytes 4718596
  227.6 20.9 %copy-start.6 = (f32[2,48,256]{2,1,0:T(8,128)S(1)}, f32[2,48,256]{2,1,0:T(8,128)}, u32[]{:S(2)}) copy-start(f32[2,48,256]{2,1,0:T(8,128)} %get-tuple-element.91) | copy-start | bytes 294916
Sparse Core Ops, SparseCore 0:
  73.5 56.1 all-gather.2
  132.6 54.5 all-gather.4

commit v2 on v0

v2 whole, which is shorter than its diff:
```python
import functools
import types

import jax
import jax.numpy as jnp
from jax import lax
from jax.experimental import pallas as pl
from jax.experimental.pallas import tpu as pltpu
from jax.sharding import PartitionSpec as P

EPSILON = 1e-05
REACH = 64
CORES = 2
NEAR = 0.7978845608
CUBE = 0.044715
STEP = 20
CHAIN = 5
LANES = 256
LANE = 128
WIDE = 256
VMEM = 62 * 2**20
MESH = pl.DeviceIdType.MESH
F32 = jnp.float32
BF16 = jnp.bfloat16


def dot(left, right):
    return jnp.dot(left, right, preferred_element_type=F32)


def dot_t(left, right):
    return lax.dot_general(left, right, (((1,), (1,)), ((), ())), preferred_element_type=F32)


def t_dot(left, right):
    return lax.dot_general(left, right, (((0,), (0,)), ((), ())), preferred_element_type=F32)


def two_parts(values):
    high = values.astype(BF16)
    return high, (values - high.astype(F32)).astype(BF16)


def dot_wide(values, right, transposed=False):
    rows = values.shape[0]
    both = (dot_t if transposed else dot)(jnp.concatenate(two_parts(values), 0), right)
    return both[:rows] + both[rows:]


def gelu(values):
    square = values * values
    bend = jnp.tanh(values * (NEAR + (NEAR * CUBE) * square))
    return values * (0.5 + 0.5 * bend)


def gelu_and_slope(values):
    square = values * values
    bend = jnp.tanh(values * (NEAR + (NEAR * CUBE) * square))
    part = 0.5 + 0.5 * bend
    act = values * part
    slope = part + act * (1.0 - part) * (2.0 * NEAR + (6.0 * NEAR * CUBE) * square)
    return act, slope


def norm_parts(values):
    centered = values - jnp.mean(values, -1, keepdims=True)
    scale = lax.rsqrt(jnp.mean(centered * centered, -1, keepdims=True) + EPSILON)
    return centered * scale, scale


def norm_back(grad, unit, scale, gain):
    scaled = gain * grad
    flat = jnp.mean(scaled, -1, keepdims=True)
    slant = jnp.mean(scaled * unit, -1, keepdims=True)
    return (scaled - flat - unit * slant) * scale


def col_sum(values):
    return jnp.sum(values, 0, keepdims=True)


def iota(dims, axis):
    return lax.broadcasted_iota(jnp.int32, dims, axis)


def chip_dims(count):
    side = 1
    while 2 * (2 * side) ** 3 <= count and count % (4 * side * side) == 0:
        side *= 2
    return side, count // (side * side)


def up(size, unit):
    return -(-size // unit) * unit


def chunk_rows(count, width, hidden, features):
    tall = (2 * width + features) // CORES
    wide = width // LANE
    early = (hidden // CORES) * wide + features * (up(tall, LANE) // LANE) + 3 * (features // CORES)
    second = (hidden // CORES) * wide
    first = tall * wide + 16 * wide
    return tuple(up(rows, 16 * count) for rows in (early, second, first))


def cut(pieces, start, stop):
    at, got = 0, []
    for piece in pieces:
        low, high = max(start, at), min(stop, at + piece.shape[0])
        if low < high:
            got.append(piece[low - at : high - at])
        at += piece.shape[0]
    return jnp.concatenate(got, 0) if len(got) > 1 else got[0]


def put_wide(pack, half, at, piece):
    rows = piece.shape[0]
    for block in range(piece.shape[1] // LANE):
        pack[half, pl.ds(at, rows), :] = piece[:, block * LANE : (block + 1) * LANE].astype(BF16)
        at += rows
    return at


def put_rest(pack, at):
    rest = pack.shape[1] - at
    if rest:
        for half in range(CORES):
            pack[half, pl.ds(at, rest), :] = jnp.zeros((rest, LANE), BF16)


def take_wide(packed, at, rows, blocks):
    pieces = [packed[pl.ds(at + b * rows, rows), :] for b in range(blocks)]
    return jnp.concatenate(pieces, 1).astype(F32), at + blocks * rows


class Copies:
    def __init__(self, send, recv):
        self.send, self.recv, self.used = send, recv, 0

    def group(self, entries):
        made = []
        for source, target, device in entries:
            at = self.used
            self.used += 1
            made.append(functools.partial(self._make, source, target, device, at))
        return Group(made)

    def _make(self, source, target, device, at):
        return pltpu.make_async_remote_copy(
            src_ref=source,
            dst_ref=target,
            send_sem=self.send.at[at],
            recv_sem=self.recv.at[at],
            device_id=device,
            device_id_type=MESH,
        )


class Group:
    def __init__(self, made):
        self.made = made

    def start(self):
        for make in self.made:
            make().start()

    def wait(self):
        for make in self.made:
            make().wait()


class Place:
    def __init__(self):
        res, half, count = lax.axis_index("res"), lax.axis_index("half"), lax.axis_size("res")
        side, deep = chip_dims(count)
        x, y, z = lax.rem(res, side), lax.rem(res // side, side), res // (side * side)
        first = half == 0
        self.res, self.half, self.count = res, half, count
        self.dims = (side, side, deep)
        self.at = (jnp.where(first, x, y), jnp.where(first, y, x), z)
        self.strides = (jnp.where(first, 1, side), jnp.where(first, side, 1), side * side)
        self.partner = (res, 1 - half)

    def peers(self, level):
        size, here = self.dims[level], self.at[level]
        found = []
        for ahead in range(1, size):
            to = lax.rem(here + ahead, size)
            found.append((to, (self.res + (to - here) * self.strides[level], self.half)))
        return found

    def line(self):
        res, half, count = self.res, self.half, self.count
        return (
            (res > 0, (res - 1, half)),
            (res + half > 0, (res - 1 + half, 1 - half)),
            (res + half < count, (res + half, 1 - half)),
            (res < count - 1, (res + 1, half)),
        )

    def line_count(self):
        res, half, count = self.res, self.half, self.count
        return 4 - jnp.where(res > 0, 0, 2 - half) - jnp.where(res < count - 1, 0, 1 + half)


def greet(place):
    barrier = pltpu.get_barrier_semaphore()

    def signal(device):
        pl.semaphore_signal(barrier, inc=1, device_id=device, device_id_type=MESH)

    for exists, device in place.line():
        pl.when(exists)(functools.partial(signal, device))
    signal(place.partner)
    others = 1
    for level in range(3):
        for _, device in place.peers(level):
            signal(device)
            others += 1
    pl.semaphore_wait(barrier, others + place.line_count())


def halo_layout(rows):
    edge = REACH - rows
    return ((0, edge), (edge, rows), (REACH + rows, rows), (REACH + 2 * rows, edge))


class Halo:
    def __init__(self, place, window, rows, send, recv, first):
        self.place, self.window, self.rows = place, window, rows
        self.send, self.recv, self.first = send, recv, first

    def clear(self):
        for (exists, _), (offset, size) in zip(self.place.line(), halo_layout(self.rows)):

            @pl.when(jnp.logical_not(exists))
            def _():
                self.window[pl.ds(offset, size), :] = jnp.zeros((size, self.window.shape[1]), self.window.dtype)

    def _copy(self, at, device):
        offset, size = halo_layout(self.rows)[3 - at]
        first = REACH + (self.rows - size if at == 3 else 0)
        return pltpu.make_async_remote_copy(
            src_ref=self.window.at[pl.ds(first, size)],
            dst_ref=self.window.at[pl.ds(offset, size)],
            send_sem=self.send.at[self.first + at],
            recv_sem=self.recv.at[self.first + 3 - at],
            device_id=device,
            device_id_type=MESH,
        )

    def start(self):
        for at, (exists, device) in enumerate(self.place.line()):

            @pl.when(exists)
            def _():
                self._copy(at, device).start()

    def wait(self):
        for at, (exists, device) in enumerate(self.place.line()):
            offset, size = halo_layout(self.rows)[at]

            @pl.when(exists)
            def _():
                self._copy(at, device).wait_send()
                pltpu.make_async_remote_copy(
                    src_ref=self.window.at[pl.ds(offset, size)],
                    dst_ref=self.window.at[pl.ds(offset, size)],
                    send_sem=self.send.at[self.first + at],
                    recv_sem=self.recv.at[self.first + at],
                    device_id=device,
                    device_id_type=MESH,
                ).wait_recv()


class Returns:
    def __init__(self, place, table, landing, rows, send, recv, first):
        self.place, self.table, self.landing, self.rows = place, table, landing, rows
        self.send, self.recv, self.first = send, recv, first

    def _copy(self, at, device):
        layout = halo_layout(self.rows)
        offset, size = layout[at]
        return pltpu.make_async_remote_copy(
            src_ref=self.table.at[pl.ds(offset, size)],
            dst_ref=self.landing.at[pl.ds(layout[3 - at][0], size)],
            send_sem=self.send.at[self.first + at],
            recv_sem=self.recv.at[self.first + 3 - at],
            device_id=device,
            device_id_type=MESH,
        )

    def start(self):
        for at, (exists, device) in enumerate(self.place.line()):

            @pl.when(exists)
            def _():
                self._copy(at, device).start()

    def finish(self, total):
        total[...] = self.table[pl.ds(REACH, self.rows), :]
        for at, (exists, device) in enumerate(self.place.line()):
            offset, size = halo_layout(self.rows)[at]
            first = self.rows - size if at == 3 else 0

            @pl.when(exists)
            def _():
                self._copy(at, device).wait_send()
                pltpu.make_async_remote_copy(
                    src_ref=self.table.at[pl.ds(offset, size)],
                    dst_ref=self.landing.at[pl.ds(offset, size)],
                    send_sem=self.send.at[self.first + at],
                    recv_sem=self.recv.at[self.first + at],
                    device_id=device,
                    device_id_type=MESH,
                ).wait_recv()
                total[pl.ds(first, size), :] += self.landing[pl.ds(offset, size), :]


def gather_groups(place, copies, ref, unit, source=None, base=0):
    mine = (place.at[0] * place.dims[1] + place.at[1]) * place.dims[2] + place.at[2]
    groups, size = [], unit
    start = mine * unit
    for level in (2, 1, 0):
        here = ref.at[pl.ds(pl.multiple_of(base + start, 16), size)]
        from_ref = here if source is None or level < 2 else source
        groups.append(copies.group([(from_ref, here, device) for _, device in place.peers(level)]))
        start = start - place.at[level] * size
        size = size * place.dims[level]
    return groups


class ChipSum:
    def __init__(self, place, copies, pack, got, landed, gathered):
        self.place, self.pack, self.got, self.landed, self.gathered = place, pack, got, landed, gathered
        half, size = place.half, pack.shape[1]
        self.pair = copies.group([(pack.at[1 - half], got, place.partner)])
        self.steps, self.shares = [], []
        start, base = 0, 0
        for level in range(3):
            share = size // place.dims[level]
            entries, lands = [], []
            for to, device in place.peers(level):
                source = pack.at[half, pl.ds(pl.multiple_of(start + to * share, 16), share)]
                entries.append((source, landed.at[pl.ds(base, share)], device))
                lands.append(base)
                base += share
            start = pl.multiple_of(start + place.at[level] * share, 16)
            size = share
            self.steps.append(copies.group(entries))
            self.shares.append((start, share, lands))
        self.back = gather_groups(place, copies, gathered, size)

    def send_pair(self):
        self.pair.start()

    def add_pair(self):
        self.pair.wait()
        half = self.place.half
        self.pack[half] = (self.pack[half].astype(F32) + self.got[...].astype(F32)).astype(BF16)

    def start(self, level):
        self.steps[level].start()

    def finish(self, level):
        self.steps[level].wait()
        start, share, lands = self.shares[level]
        half = self.place.half
        total = self.pack[half, pl.ds(start, share), :].astype(F32)
        for base in lands:
            total = total + self.landed[pl.ds(base, share), :].astype(F32)
        if level < 2:
            self.pack[half, pl.ds(start, share), :] = total.astype(BF16)
        else:
            self.gathered[pl.ds(start, share), :] = total.astype(BF16)

    def start_back(self, step):
        self.back[step].start()

    def finish_back(self, step):
        self.back[step].wait()


def flat(values):
    return values.reshape(values.shape[0] * values.shape[1], values.shape[2])


def feed_forward(r, pooled, own):
    width = own.shape[1]
    v = r.vec
    mean = pooled / r.counts[:, 0:1]
    summed = own + dot_wide(mean, r.third[...]) + v[2:3, :width]
    unit, _ = norm_parts(summed)
    normed = unit * v[3:4, :width] + v[4:5, :width]
    low = normed.astype(BF16)
    pre = dot(low, r.expand[...]) + v[8:9, :]
    second = normed + dot(gelu(pre).astype(BF16), r.reduce[...]) + v[5:6, :width]
    unit_two, _ = norm_parts(second)
    r.summed[...] = summed
    r.pre_expand[...] = pre
    r.second[...] = second
    r.normed[...] = low
    return unit_two * v[6:7, :width] + v[7:8, :width]


def fill_table(window, far, own, bias, table, rows, multiply):
    places = window.shape[0]
    table[pl.ds(0, places), :] = multiply(window[...], far).astype(BF16)
    table[pl.ds(places, rows), :] = (multiply(window[pl.ds(REACH, rows), :], own) + bias).astype(BF16)


def chain_parts(step):
    return [step * STEP + part * CHAIN for part in range(STEP // CHAIN)]


def chain_rows(r, slot):
    rows = r.counts.shape[0]
    return pl.ds(pl.multiple_of(slot * rows, CHAIN * rows), CHAIN * rows)


def step_rows(r, step):
    rows = r.counts.shape[0]
    return pl.ds(pl.multiple_of(step * (STEP * rows), STEP * rows), STEP * rows)


def build_block(r, step, half, places):
    rows = r.counts.shape[0]
    here = pl.ds(step * STEP, STEP)
    named = r.picks[here]
    dims = (STEP, rows, named.shape[2])
    spread = jnp.broadcast_to(named, dims)
    mine = iota(dims, 2) == iota(dims, 1) + half * rows
    pick = jnp.sum(jnp.where(mine, spread, 0.0), -1, keepdims=True)
    dims = (STEP, rows, LANES)
    lane = iota(dims, 2)
    hit = (lane.astype(F32) == pick) | (lane == iota(dims, 1) + places)
    r.onehot[here] = jnp.where(hit, 1.0, 0.0).astype(BF16)


def joined_rows(r, slot, slots):
    here = pl.ds(slot, slots)
    return jnp.concatenate([flat(r.onehot[here]), flat(r.edges_raw[here])], 1)


def live_rows(r, slot, width):
    count = r.counts[...]
    dims = (CHAIN,) + count.shape
    live = jnp.where(iota(dims, 0) + slot < count[None], 1.0, 0.0)
    return flat(jnp.concatenate([live] * (width // LANE), -1))


def live_column(r, slot):
    count = r.counts[...]
    dims = (CHAIN,) + count.shape
    return flat(jnp.where(iota(dims, 0) + slot < count[None], 1.0, 0.0))[:, 0:1]


def node_block(r, step, keep):
    rows = r.counts.shape[0]
    hidden = r.second_w.shape[0]
    slots = chain_parts(step)
    dims = (rows, CHAIN * rows)
    count = jnp.broadcast_to(r.counts[:, 0:1], dims)
    pre = [dot(joined_rows(r, slot, CHAIN), r.table[...]) for slot in slots]
    acts = []
    for slot, values in zip(slots, pre):
        if keep:
            here = chain_rows(r, slot)
            act, slope = gelu_and_slope(values)
            act = act.astype(BF16)
            r.act[here, :] = act
            r.slope_one[here, :] = slope.astype(BF16)
        else:
            act = gelu(values).astype(BF16)
        acts.append(act)
    pre = [dot(act, r.second_w[...]) + r.vec[1:2, :hidden] for act in acts]
    total = r.pooled[...]
    for slot, values in zip(slots, pre):
        if keep:
            act, slope = gelu_and_slope(values)
            r.slope_two[chain_rows(r, slot), :] = (slope * live_rows(r, slot, hidden)).astype(BF16)
        else:
            act = gelu(values)
        used = jnp.where(r.lane_slot[0:1, :] + slot.astype(F32) < count, r.diagonal[...], 0.0)
        total = total + dot(used.astype(BF16), act.astype(BF16))
    r.pooled[...] = total


def edge_block(r, step, features):
    v = r.vec
    bias_two, bias_three = v[10:11, :features], v[11:12, :features]
    gain, shift = v[12:13, :features], v[13:14, :features]
    rows = r.counts.shape[0]
    split = lambda values: values.reshape(CHAIN, rows, features)
    for slot in chain_parts(step):
        here = pl.ds(slot, CHAIN)
        joined = joined_rows(r, slot, CHAIN)
        live = live_column(r, slot)
        o_one, slope_one = gelu_and_slope(dot(joined, r.e_table[...]))
        o_one = o_one.astype(BF16)
        o_two, slope_two = gelu_and_slope(dot(o_one, r.e_second_w[...]) + bias_two)
        o_two = o_two.astype(BF16)
        summed = joined[:, LANES:].astype(F32) + (dot(o_two, r.e_third_w[...]) + bias_three)
        unit, scale = norm_parts(summed)
        r.edge_out[here] = split((unit * gain + shift) * live).astype(BF16)
        d_out = flat(r.cots_raw[here]).astype(F32) * live
        r.ge_norm[0:1, :] += col_sum(d_out * unit)
        r.ge_norm[1:2, :] += col_sum(d_out)
        d_sum = norm_back(d_out, unit, scale, gain)
        r.ge_norm[2:3, :] += col_sum(d_sum)
        d_three = d_sum.astype(BF16)
        r.ge_third[...] += t_dot(o_two, d_three)
        d_two = dot_t(d_three, r.e_third_w[...]) * slope_two
        r.ge_norm[3:4, :] += col_sum(d_two)
        d_two = d_two.astype(BF16)
        r.ge_second[...] += t_dot(o_one, d_two)
        d_one = (dot_t(d_two, r.e_second_w[...]) * slope_one).astype(BF16)
        r.ge_first[...] += t_dot(joined, d_one)
        r.edge_grad[here] = split(d_sum + dot(d_one, r.e_first_t[:, pl.ds(2 * r.nodes_width, features)]))


def node_grad(r, cot, far_total):
    v = r.vec
    width = cot.shape[1]
    grad = cot.astype(F32) + r.e_own_back[...] + dot_wide(far_total, r.e_first_t[:, pl.ds(width, width)])
    unit, scale = norm_parts(r.second[...])
    dw = norm_back(grad, unit, scale, v[6:7, :width])
    gain_two, shift_two = col_sum(grad * unit), col_sum(grad)
    ds = dw.astype(BF16)
    r.ds[...] = ds
    _, slope = gelu_and_slope(r.pre_expand[...])
    dq = (dot_t(ds, r.reduce[...]) * slope).astype(BF16)
    dv = dw + dot_t(dq, r.expand[...])
    unit, scale = norm_parts(r.summed[...])
    du = norm_back(dv, unit, scale, v[3:4, :width])
    r.du[...] = du
    counts = r.counts[:, 0:1]
    dm = (du / counts).astype(BF16)
    r.slot_grad[...] = dot_t(dm, r.third[...])
    r.dm[...] = dm
    small = r.small
    small[...] = jnp.zeros(small.shape, F32)
    small[2:3, :] = col_sum(counts * dm.astype(F32))
    small[3:4, :] = col_sum(dv * unit)
    small[4:5, :] = col_sum(dv)
    dq_sum = col_sum(dq.astype(F32))
    for part in range(dq_sum.shape[1] // width):
        small[5 + part : 6 + part, :] = dq_sum[:, part * width : (part + 1) * width]
    small[9:10, :] = col_sum(ds.astype(F32))
    small[10:11, :] = gain_two
    small[11:12, :] = shift_two


def put_features(pack, half, at, e_second, e_third):
    part = e_second.shape[0] // CORES
    two = [ref[pl.ds(half * part, part), :] for ref in (e_second, e_third)]
    for piece in two:
        at = put_wide(pack, half, at, piece[:, :LANE])
    return put_wide(pack, half, at, jnp.concatenate([piece[:, LANE:] for piece in two], 1))


def pack_early(r, pack):
    hidden, width = r.third.shape
    features = r.ge_second.shape[0]
    dm = r.dm[...]
    g_third = t_dot(jnp.concatenate(two_parts(r.pooled[...]), 0), jnp.concatenate([dm, dm], 0))
    g_edge = jnp.transpose(r.ge_first[pl.ds(LANES, features), :])
    e_first = jnp.concatenate([r.ge_own[...], r.ge_far[...], g_edge], 1)
    tall = e_first.shape[1] // CORES
    fill = jnp.zeros((features, up(tall, LANE) - tall), F32)
    for half in range(CORES):
        part = hidden // CORES
        at = put_wide(pack, half, 0, g_third[half * part : (half + 1) * part])
        piece = jnp.concatenate([e_first[:, half * tall : (half + 1) * tall], fill], 1)
        at = put_wide(pack, half, at, piece)
        at = put_features(pack, half, at, r.ge_second, r.ge_third)
    put_rest(pack, at)


def pack_second(r, pack):
    part = r.g_second.shape[0] // CORES
    for half in range(CORES):
        at = put_wide(pack, half, 0, r.g_second[pl.ds(half * part, part), :])
    put_rest(pack, at)


def small_rows(r, places):
    rows = r.counts.shape[0]
    features = r.ge_norm.shape[1]
    fill = jnp.zeros((1, LANES - features), F32)
    own = pl.ds(places, rows)
    edge = [col_sum(r.ge_first[own, :])] + [r.ge_norm[at : at + 1, :] for at in (3, 2, 0, 1)]
    edge = [jnp.concatenate([row, fill], 1) for row in edge] + [jnp.zeros((1, LANES), F32)]
    lines = [col_sum(r.g_first[own, :]), r.g_bias[...], r.small[2:12, :]]
    lines += [jnp.concatenate(edge[at : at + 2], 1) for at in (0, 2, 4)]
    return jnp.concatenate(lines + [jnp.zeros((1, r.small.shape[1]), F32)], 0)


def pack_first(r, pack, g_own, g_far, features, places):
    pieces = [g_own, g_far, r.g_first[pl.ds(LANES, features), :]]
    tall = sum(piece.shape[0] for piece in pieces) // CORES
    small = small_rows(r, places)
    for half in range(CORES):
        at = put_wide(pack, half, 0, cut(pieces, half * tall, (half + 1) * tall))
        at = put_wide(pack, half, at, small)
    put_rest(pack, at)


def second_block(r, step):
    hidden = r.act.shape[1]
    here = step_rows(r, step)
    coming = jnp.broadcast_to(r.slot_grad[...][None], (STEP,) + r.slot_grad.shape)
    d_two_f = flat(coming) * r.slope_two[here, :].astype(F32)
    r.g_bias[...] += col_sum(d_two_f)
    d_two = d_two_f.astype(BF16)
    r.g_second[...] += t_dot(r.act[here, :], d_two)
    r.slope_one[here, :] = (dot_t(d_two, r.second_w[...]) * r.slope_one[here, :].astype(F32)).astype(BF16)


def first_block(r, step, features):
    rows = r.counts.shape[0]
    d_one = r.slope_one[step_rows(r, step), :]
    r.g_first[...] += t_dot(joined_rows(r, step * STEP, STEP), d_one)
    more = dot_t(d_one, r.table[pl.ds(LANES, features), :])
    r.edge_grad[pl.ds(step * STEP, STEP)] += more.reshape(STEP, rows, features)


def wide_block(r, step, half, fresh):
    width, inner = r.expand.shape
    blocks = inner // WIDE
    mine = blocks // CORES
    block = lax.rem(step + half * mine, blocks)
    here = pl.ds(pl.multiple_of(block * WIDE, WIDE), WIDE)
    cols = pl.ds(pl.multiple_of(half * (width // CORES), width // CORES), width // CORES)
    bias = r.vec[8:9, here]
    total_rows = r.normed_all.shape[0]
    parts = 4
    size = total_rows // parts
    g_expand = jnp.zeros((width // CORES, WIDE), F32)
    g_reduce = jnp.zeros((WIDE, width), F32)
    for part in range(parts):
        rows = pl.ds(part * size, size)
        normed, ds = r.normed_all[rows, :], r.ds_all[rows, :]
        act, slope = gelu_and_slope(dot(normed, r.expand[:, here]) + bias)
        dq = (dot_t(ds, r.reduce[here, :]) * slope).astype(BF16)
        g_expand = g_expand + t_dot(r.normed_all[rows, cols], dq)
        r.wide_act[rows, :] = act.astype(BF16)
    if fresh:
        r.g_expand[:, here] = g_expand
    else:
        r.g_expand[:, here] += g_expand

    @pl.when(step < mine)
    def _():
        out = pl.ds(pl.multiple_of(step * WIDE, WIDE), WIDE)
        found = t_dot(r.wide_act[...], r.ds_all[...])
        if fresh:
            r.g_reduce[out, :] = found
        else:
            r.g_reduce[out, :] += found


INPUTS = (
    "vec", "nodes", "edges", "neighbours", "first_in", "second_in", "third_in", "expand_in", "reduce_in",
    "e_first_in", "e_second_in", "e_third_in", "cot_nodes", "cot_edges",
)
OUTPUTS = (
    "state_out", "edges_out", "fed_out", "grads_out", "sum_early", "sum_second", "sum_first",
    "expand_out", "reduce_out", "normed_slots", "ds_slots",
)


def kernel(names, features, *refs):
    r = types.SimpleNamespace(**dict(zip(names, refs)))
    place = Place()
    res, half, count = place.res, place.half, place.count
    rows_dev, width = r.nodes.shape
    rows = rows_dev // CORES
    places = rows + 2 * REACH
    slots = r.edges.shape[0]
    each = slots // CORES
    steps = slots // STEP
    r.nodes_width = width
    own = pl.ds(REACH, rows)
    mine = pl.ds(pl.multiple_of(half * rows, 16), rows)

    loads = {}

    def load(name, source, target):
        copy = pltpu.make_async_copy(source, target, r.load_sem.at[len(loads)])
        loads[name] = copy
        copy.start()

    load("nodes", r.nodes.at[mine], r.windows.at[0, own])
    load("neighbours", r.neighbours, r.neighbours_raw)
    load("first", r.first_in, r.first)
    load("edges", r.edges.at[:, mine, :], r.edges_raw)
    load("second", r.second_in, r.second_w)
    load("e_first", r.e_first_in, r.e_first_t)
    load("e_second", r.e_second_in, r.e_second_w)
    load("e_third", r.e_third_in, r.e_third_w)
    load("third", r.third_in, r.third)
    load("expand", r.expand_in, r.expand)
    load("reduce", r.reduce_in, r.reduce)
    load("cot_edges", r.cot_edges.at[:, mine, :], r.cots_raw)
    load("cot_nodes", r.cot_nodes.at[mine], r.cot_rows)

    halos = [
        Halo(place, r.windows.at[k], rows, r.line_send, r.line_recv, 4 * k) for k in range(3)
    ]
    edge_returns = Returns(place, r.ge_first, r.edge_landing, rows, r.line_send, r.line_recv, 12)
    node_returns = Returns(place, r.g_first, r.node_landing, rows, r.line_send, r.line_recv, 16)
    copies = Copies(r.step_send, r.step_recv)
    sums = [
        ChipSum(place, copies, pack, got, landed, gathered)
        for pack, got, landed, gathered in (
            (r.pack_early, r.got_early, r.landed_early, r.all_early),
            (r.pack_second, r.got_second, r.landed_second, r.all_second),
            (r.pack_first, r.got_first, r.landed_first, r.all_first),
        )
    ]
    early, second, first = sums
    span = count * rows

    def row_gather(source, slot_ref):
        base = half * span
        groups = gather_groups(place, copies, slot_ref, rows, source, base)
        here = slot_ref.at[pl.ds(pl.multiple_of(base, 16), span)]
        groups.append(copies.group([(here, here, place.partner)]))
        return groups

    normed_gather = row_gather(r.normed, r.normed_slots)
    ds_gather = row_gather(r.ds, r.ds_slots)
    my_unit = (place.at[0] * place.dims[1] + place.at[1]) * place.dims[2] + place.at[2]
    my_slot = pl.ds(pl.multiple_of(half * span + my_unit * rows, 16), rows)
    normed_keep = pltpu.make_async_copy(r.normed, r.normed_slots.at[my_slot], r.keep_sem.at[0])
    ds_keep = pltpu.make_async_copy(r.ds, r.ds_slots.at[my_slot], r.keep_sem.at[1])
    there = pl.ds(pl.multiple_of(half * rows, 16), rows)
    my_slots = pl.ds(half * each, each)
    its_slots = pl.ds((1 - half) * each, each)
    edges_target = r.edges_out.at[:, there, :]
    edges_pair = copies.group([(r.edge_out.at[its_slots], edges_target, place.partner)])
    edges_keep = pltpu.make_async_copy(r.edge_out.at[my_slots], edges_target, r.keep_sem.at[2])
    grads_target = r.grads_out.at[:, there, :]
    grads_pair = copies.group([(r.edge_grad.at[its_slots], grads_target, place.partner)])
    grads_keep = pltpu.make_async_copy(r.edge_grad.at[my_slots], grads_target, r.keep_sem.at[3])
    fed_pair = copies.group([(r.fed_grad.at[1 - half], r.fed_out.at[there], place.partner)])
    fed_keep = pltpu.make_async_copy(r.fed_grad.at[half], r.fed_out.at[there], r.keep_sem.at[4])

    greet(place)
    loads["nodes"].wait()
    halos[0].start()
    for halo in halos:
        halo.clear()
    dims = (rows, LANE)
    counted = jnp.broadcast_to(r.vec[14:15, :LANE], dims)
    counted = jnp.sum(jnp.where(iota(dims, 1) == iota(dims, 0) + half * rows, counted, 0.0), -1, keepdims=True)
    r.counts[...] = jnp.broadcast_to(counted, dims)
    dims = (rows, CHAIN * rows)
    lane = iota(dims, 1)
    r.diagonal[...] = jnp.where(lax.rem(lane, rows) == iota(dims, 0), 1.0, 0.0)
    r.lane_slot[...] = (iota(r.lane_slot.shape, 1) // rows).astype(F32)
    loads["neighbours"].wait()
    base = res * rows_dev + half * rows - REACH
    named = (r.neighbours_raw[...] - base).astype(F32)
    r.picks[...] = named.reshape(slots, 1, rows_dev)

    def build(step, carry):
        build_block(r, step, half, places)
        return carry

    lax.fori_loop(0, steps, build, 0)
    for table in (r.table, r.e_table):
        rest = LANES - places - rows
        if rest:
            table[pl.ds(places + rows, rest), :] = jnp.zeros((rest, table.shape[1]), BF16)
    hidden = r.table.shape[1]
    for name in ("first", "e_first", "e_second", "e_third"):
        loads[name].wait()
    r.table[pl.ds(LANES, features), :] = r.first[pl.ds(2 * width, features), :]
    edge_part = r.e_first_t[:, pl.ds(2 * width, features)]
    r.e_table[pl.ds(LANES, features), :] = jnp.transpose(edge_part.astype(F32)).astype(BF16)
    loads["edges"].wait()
    bias = r.vec[0:1, :hidden]
    far_w, own_w = r.first[pl.ds(width, width), :], r.first[pl.ds(0, width), :]
    halos[0].wait()
    fill_table(r.windows.at[0], far_w, own_w, bias, r.table, rows, dot)
    r.pooled[...] = jnp.zeros(r.pooled.shape, F32)
    loads["second"].wait()

    def first_pass(step, carry):
        node_block(r, step, False)
        return carry

    lax.fori_loop(0, steps, first_pass, 0)
    loads["third"].wait()
    loads["expand"].wait()
    loads["reduce"].wait()
    r.windows[1, own, :] = feed_forward(r, r.pooled[...], r.windows[0, own, :].astype(F32)).astype(BF16)

    halos[1].start()
    loads["cot_edges"].wait()
    loads["cot_nodes"].wait()
    halos[1].wait()
    fill_table(r.windows.at[1], far_w, own_w, bias, r.table, rows, dot)
    r.pooled[...] = jnp.zeros(r.pooled.shape, F32)

    def second_pass(step, carry):
        node_block(r, step, True)
        return carry

    lax.fori_loop(0, steps, second_pass, 0)
    r.windows[2, own, :] = feed_forward(r, r.pooled[...], r.windows[1, own, :].astype(F32)).astype(BF16)

    halos[2].start()
    normed_keep.start()
    normed_gather[0].start()
    for ref in (r.ge_norm, r.ge_first, r.ge_second, r.ge_third, r.g_second, r.g_first, r.g_bias):
        ref[...] = jnp.zeros(ref.shape, F32)
    halos[2].wait()
    e_own, e_far = r.e_first_t[:, pl.ds(0, width)], r.e_first_t[:, pl.ds(width, width)]
    fill_table(r.windows.at[2], e_far, e_own, r.vec[9:10, :features], r.e_table, rows, dot_t)
    state_keep = pltpu.make_async_copy(
        r.windows.at[
            2,
            pl.ds(pl.multiple_of(REACH - half * rows, 16), rows_dev),
            pl.ds(pl.multiple_of(half * (width // CORES), width // CORES), width // CORES),
        ],
        r.state_out,
        r.keep_sem.at[5],
    )
    state_keep.start()

    def edge_pass(step, carry):
        edge_block(r, step, features)

        @pl.when(step == 1)
        def _():
            normed_keep.wait()
            normed_gather[0].wait()
            normed_gather[1].start()

        return carry

    lax.fori_loop(0, steps, edge_pass, 0)
    edge_returns.start()
    edges_keep.start()
    edges_pair.start()
    normed_gather[1].wait()
    normed_gather[2].start()
    own_spread = r.ge_first[pl.ds(places, rows), :]
    r.ge_own[...] = t_dot(own_spread.astype(BF16), r.windows[2, own, :])
    r.ge_far[...] = t_dot(r.ge_first[pl.ds(0, places), :].astype(BF16), r.windows[2])
    r.e_own_back[...] = dot_wide(own_spread, e_own)
    edge_returns.finish(r.edge_total)

    node_grad(r, r.cot_rows[...], r.edge_total[...])
    ds_keep.start()
    ds_gather[0].start()
    pack_early(r, r.pack_early)
    early.send_pair()
    normed_gather[2].wait()
    normed_gather[3].start()

    def second_layer(step, carry):
        second_block(r, step)

        @pl.when(step == 0)
        def _():
            early.add_pair()
            early.start(0)

        @pl.when(step == 1)
        def _():
            ds_keep.wait()
            ds_gather[0].wait()
            ds_gather[1].start()

        return carry

    lax.fori_loop(0, steps, second_layer, 0)
    pack_second(r, r.pack_second)
    second.send_pair()
    early.finish(0)
    early.start(1)
    ds_gather[1].wait()
    ds_gather[2].start()

    def first_layer(step, carry):
        first_block(r, step, features)

        @pl.when(step == 0)
        def _():
            second.add_pair()
            second.start(0)

        @pl.when(step == 1)
        def _():
            early.finish(1)
            early.start(2)

        return carry

    lax.fori_loop(0, steps, first_layer, 0)
    node_returns.start()
    grads_keep.start()
    own_spread = r.g_first[pl.ds(places, rows), :]
    g_own = t_dot(r.windows[1, own, :], own_spread.astype(BF16))
    g_far = t_dot(r.windows[1], r.g_first[pl.ds(0, places), :].astype(BF16))
    pack_first(r, r.pack_first, g_own, g_far, features, places)
    first.send_pair()
    grads_pair.start()
    second.finish(0)
    second.start(1)
    ds_gather[2].wait()
    ds_gather[3].start()
    own_back = r.du[...] + dot_wide(own_spread, own_w, True)
    first.add_pair()
    first.start(0)
    node_returns.finish(r.node_total)
    fed = own_back + dot_wide(r.node_total[...], far_w, True)
    for part in range(CORES):
        r.fed_grad[part] = fed[:, part * (width // CORES) : (part + 1) * (width // CORES)]
    fed_keep.start()
    fed_pair.start()
    early.finish(2)
    early.start_back(0)
    second.finish(1)
    second.start(2)
    normed_gather[3].wait()
    ds_gather[3].wait()

    events = {
        0: (lambda: early.finish_back(0), lambda: early.start_back(1)),
        1: (lambda: second.finish(2), lambda: second.start_back(0), lambda: first.finish(0), lambda: first.start(1)),
        2: (lambda: early.finish_back(1), lambda: early.start_back(2)),
        3: (lambda: second.finish_back(0), lambda: second.start_back(1), lambda: first.finish(1), lambda: first.start(2)),
        4: (lambda: early.finish_back(2),),
        5: (lambda: second.finish_back(1), lambda: second.start_back(2), lambda: first.finish(2), lambda: first.start_back(0)),
        7: (lambda: second.finish_back(2), lambda: first.finish_back(0), lambda: first.start_back(1)),
    }
    blocks = r.expand.shape[1] // WIDE
    chunk = r.normed_all.shape[0]
    for at in range(2 * span // chunk):
        rows_here = pl.ds(at * chunk, chunk)
        fetches = [
            pltpu.make_async_copy(r.normed_slots.at[rows_here], r.normed_all, r.keep_sem.at[6]),
            pltpu.make_async_copy(r.ds_slots.at[rows_here], r.ds_all, r.keep_sem.at[7]),
        ]
        for fetch in fetches:
            fetch.start()
        for fetch in fetches:
            fetch.wait()

        def wide(step, carry):
            wide_block(r, step, half, at == 0)
            if at == 0:
                for when, actions in events.items():

                    @pl.when(step == when)
                    def _():
                        for act in actions:
                            act()

            return carry

        lax.fori_loop(0, blocks, wide, 0)

    outs = [
        (r.g_expand, r.expand_out),
        (r.g_reduce, r.reduce_out),
        (r.all_early, r.sum_early),
        (r.all_second, r.sum_second),
        (r.all_first, r.sum_first),
    ]
    stores = [
        pltpu.make_async_copy(source, target, r.keep_sem.at[8 + at]) for at, (source, target) in enumerate(outs)
    ]
    for store in stores[:4]:
        store.start()
    first.finish_back(1)
    first.start_back(2)
    for group in (edges_pair, grads_pair, fed_pair):
        group.wait()
    for copy in (edges_keep, grads_keep, fed_keep, state_keep):
        copy.wait()
    first.finish_back(2)
    stores[4].start()
    for store in stores:
        store.wait()


def shape(dims, kind):
    return jax.ShapeDtypeStruct(dims, kind)


def run(arrays):
    by_name = dict(zip(INPUTS, arrays))
    count = lax.axis_size("res")
    rows_dev, width = by_name["nodes"].shape
    slots, _, features = by_name["edges"].shape
    hidden = by_name["second_in"].shape[0]
    inner = by_name["expand_in"].shape[1]
    rows = rows_dev // CORES
    places = rows + 2 * REACH
    total = rows * slots
    each = slots // CORES
    tall = by_name["first_in"].shape[0]
    early, second, first = chunk_rows(count, width, hidden, features)
    side, deep = chip_dims(count)
    everyone = CORES * count * rows
    chunk = min(everyone, 16 * rows_dev)
    outs = (
        shape((rows_dev, width // CORES), BF16),
        shape((each, rows_dev, features), BF16),
        shape((rows_dev, width // CORES), F32),
        shape((each, rows_dev, features), F32),
        shape((early, LANE), BF16),
        shape((second, LANE), BF16),
        shape((first, LANE), BF16),
        shape((width // CORES, inner), F32),
        shape((inner // CORES, width), F32),
        shape((everyone, width), BF16),
        shape((everyone, width), BF16),
    )
    peers = 2 * (side - 1) + deep - 1
    remote = 3 * (2 * peers + 1) + 2 * (peers + 1) + 3
    scratch = {
        "windows": ((3, places, width), BF16),
        "neighbours_raw": ((slots, rows_dev), jnp.int32),
        "picks": ((slots, 1, rows_dev), F32),
        "counts": ((rows, LANE), F32),
        "diagonal": ((rows, CHAIN * rows), F32),
        "lane_slot": ((8, CHAIN * rows), F32),
        "first": ((tall, hidden), BF16),
        "second_w": ((hidden, hidden), BF16),
        "third": ((hidden, width), BF16),
        "expand": ((width, inner), BF16),
        "reduce": ((inner, width), BF16),
        "e_first_t": ((features, tall), BF16),
        "e_second_w": ((features, features), BF16),
        "e_third_w": ((features, features), BF16),
        "edges_raw": ((slots, rows, features), BF16),
        "cots_raw": ((slots, rows, features), BF16),
        "cot_rows": ((rows, width), BF16),
        "onehot": ((slots, rows, LANES), BF16),
        "table": ((LANES + features, hidden), BF16),
        "e_table": ((LANES + features, features), BF16),
        "act": ((total, hidden), BF16),
        "slope_one": ((total, hidden), BF16),
        "slope_two": ((total, hidden), BF16),
        "pooled": ((rows, hidden), F32),
        "summed": ((rows, width), F32),
        "second": ((rows, width), F32),
        "pre_expand": ((rows, inner), F32),
        "normed": ((rows, width), BF16),
        "edge_out": ((slots, rows, features), BF16),
        "edge_grad": ((slots, rows, features), F32),
        "ge_norm": ((8, features), F32),
        "ge_first": ((LANES + features, features), F32),
        "ge_second": ((features, features), F32),
        "ge_third": ((features, features), F32),
        "ge_own": ((features, width), F32),
        "ge_far": ((features, width), F32),
        "e_own_back": ((rows, width), F32),
        "edge_landing": ((places, features), F32),
        "edge_total": ((rows, features), F32),
        "ds": ((rows, width), BF16),
        "du": ((rows, width), F32),
        "dm": ((rows, width), BF16),
        "slot_grad": ((rows, hidden), F32),
        "small": ((16, width), F32),
        "g_second": ((hidden, hidden), F32),
        "g_first": ((LANES + features, hidden), F32),
        "g_bias": ((1, hidden), F32),
        "node_landing": ((places, hidden), F32),
        "node_total": ((rows, hidden), F32),
        "fed_grad": ((CORES, rows, width // CORES), F32),
        "normed_all": ((chunk, width), BF16),
        "ds_all": ((chunk, width), BF16),
        "wide_act": ((chunk, WIDE), BF16),
        "g_expand": ((width // CORES, inner), F32),
        "g_reduce": ((inner // CORES, width), F32),
    }
    for name, size in (("early", early), ("second", second), ("first", first)):
        scratch["pack_" + name] = ((CORES, size, LANE), BF16)
        for kind in ("got_", "landed_", "all_"):
            scratch[kind + name] = ((size, LANE), BF16)
    sems = {"load_sem": 13, "keep_sem": 13, "line_send": 20, "line_recv": 20, "step_send": remote, "step_recv": remote}
    names = INPUTS + OUTPUTS + tuple(scratch) + tuple(sems)
    anywhere = pl.BlockSpec(memory_space=pl.ANY)
    return pl.pallas_call(
        functools.partial(kernel, names, features),
        out_shape=outs,
        in_specs=[pl.BlockSpec(memory_space=pltpu.VMEM)] + [anywhere] * (len(INPUTS) - 1),
        out_specs=(anywhere,) * len(outs),
        scratch_shapes=[pltpu.VMEM(dims, kind) for dims, kind in scratch.values()]
        + [pltpu.SemaphoreType.DMA((size,)) for size in sems.values()],
        compiler_params=pltpu.CompilerParams(
            collective_id=1, has_side_effects=True, vmem_limit_bytes=VMEM
        ),
        name="graph_layer",
    )(*arrays)


def unpack_kernel(width, hidden, features, inner, early, second, first, *outs):
    (first_g, b_one, second_g, b_two, third_g, b_three, gain_one, shift_one, b_expand, b_reduce, gain_two,
     shift_two, e_first, eb_one, e_second, eb_two, e_third, eb_three, e_gain, e_shift) = outs
    half = lax.axis_index("half")
    wide = width // LANE
    tall = (2 * width + features) // CORES
    third_g[...], at = take_wide(early, 0, hidden // CORES, wide)
    e_whole, at = take_wide(early, at, features, up(tall, LANE) // LANE)
    e_first[...] = e_whole[:, :tall]
    rest = features - LANE
    part = features // CORES
    left_two, at = take_wide(early, at, part, 1)
    left_three, at = take_wide(early, at, part, 1)
    right, at = take_wide(early, at, part, 1)
    e_second[...] = jnp.concatenate([left_two, right[:, :rest]], 1)
    e_third[...] = jnp.concatenate([left_three, right[:, rest:]], 1)
    second_g[...], _ = take_wide(second, 0, hidden // CORES, wide)
    first_g[...], at = take_wide(first, 0, tall, wide)
    small, _ = take_wide(first, at, 16, wide)

    def share(target, row):
        size = target.shape[-1]
        target[...] = jnp.where(half == 0, row[:, :size], row[:, size : 2 * size])

    for target, row in ((b_one, 0), (b_two, 1), (b_three, 2), (gain_one, 3), (shift_one, 4), (b_reduce, 9), (gain_two, 10), (shift_two, 11)):
        share(target, small[row : row + 1])
    share(b_expand, jnp.concatenate([small[5 + p : 6 + p] for p in range(inner // width)], 1))
    share(eb_one, small[12:13, :LANES])
    share(eb_two, small[12:13, LANES:])
    share(eb_three, small[13:14, :LANES])
    share(e_gain, small[13:14, LANES:])
    share(e_shift, small[14:15, :LANES])


def unpack(sums, width, hidden, features, inner):
    tall = (2 * width + features) // CORES
    flat = lambda size: shape((1, size // CORES), F32)
    outs = (
        shape((tall, hidden), F32), flat(hidden),
        shape((hidden // CORES, hidden), F32), flat(hidden),
        shape((hidden // CORES, width), F32), flat(width),
        flat(width), flat(width), flat(inner), flat(width), flat(width), flat(width),
        shape((features, tall), F32), flat(features),
        shape((features // CORES, features), F32), flat(features),
        shape((features // CORES, features), F32), flat(features),
        flat(features), flat(features),
    )
    vmem = pl.BlockSpec(memory_space=pltpu.VMEM)
    return pl.pallas_call(
        functools.partial(unpack_kernel, width, hidden, features, inner),
        out_shape=outs,
        in_specs=[vmem] * 3,
        out_specs=(vmem,) * len(outs),
        compiler_params=pltpu.CompilerParams(vmem_limit_bytes=VMEM),
        name="unpack",
    )(*sums)


def body(
    nodes, edges, neighbours, counts,
    message_first, message_first_bias, message_second, message_second_bias, message_third, message_third_bias,
    node_norm_gain, node_norm_shift, expand_weight, expand_bias, reduce_weight, reduce_bias,
    output_norm_gain, output_norm_shift,
    edge_first, edge_first_bias, edge_second, edge_second_bias, edge_third, edge_third_bias,
    edge_norm_gain, edge_norm_shift, cot_nodes, cot_edges,
):
    width, features = nodes.shape[1], edges.shape[2]
    hidden, inner = message_second.shape[0], expand_weight.shape[1]

    rows = (
        message_first_bias, message_second_bias, message_third_bias, node_norm_gain, node_norm_shift, reduce_bias,
        output_norm_gain, output_norm_shift, expand_bias, edge_first_bias, edge_second_bias, edge_third_bias,
        edge_norm_gain, edge_norm_shift, counts,
    )
    at = iota((16, inner), 0)
    vec = jnp.zeros((16, inner), F32)
    for row, vector in enumerate(rows):
        line = jnp.pad(vector.astype(F32), (0, inner - vector.shape[0]))
        vec = jnp.where(at == row, line[None, :], vec)
    by_slots = lambda values: jnp.transpose(values, (1, 0, 2))
    (state, out, fed_grad, edge_grad, early, second, first, g_expand, g_reduce, _, _) = run(
        (vec, nodes, by_slots(edges), neighbours.T, message_first, message_second, message_third, expand_weight,
         reduce_weight, edge_first.T, edge_second, edge_third, cot_nodes, by_slots(cot_edges))
    )
    got = unpack((early, second, first), width, hidden, features, inner)
    got = [g[0] if g.shape[0] == 1 else g for g in got]
    got[12] = got[12].T
    return (state, by_slots(out), fed_grad, by_slots(edge_grad)) + tuple(got[:8]) + (g_expand, got[8], g_reduce) + tuple(got[9:])


def solution(mesh):
    rows, slots = P("res", None), P("res", None, None)
    copied = P()
    down, vec = P("half", None), P("half")
    return jax.shard_map(
        body,
        mesh=mesh,
        in_specs=(rows, slots, rows, P("res")) + (copied,) * 22 + (rows, slots),
        out_specs=(
            P("res", "half"),
            P("res", "half", None),
            P("res", "half"),
            P("res", "half", None),
            down, vec, down, vec, down, vec, vec, vec, down, vec, down, vec, vec, vec,
            down, vec, down, vec, down, vec, vec, vec,
        ),
        check_vma=False,
    )
```

time: 1010 us -> 139 us (0.14)
  waiting for transfers between devices: 461 us -> 0 us
  matrix products: 174 us -> 0 us
  Pallas kernels: 0 us -> 121 us
  local copies, waits for them, and re-layouts: 121 us -> 9.66 us
  other arithmetic: 105 us -> 6.99 us
  blocking collectives: 82.4 us -> 0 us
  starting transfers between devices: 32.5 us -> 0 us
  between operations: 17 us -> 0.77 us
    psum x3 -> x0, waiting for transfers between devices: 399 us -> none  [the longest x1 203 us: body(): summed_grads = lax.psum(all_grads, 'res')]
    dot_general x26 -> x0, matrix products: 174 us -> none  [the longest x7 68.9 us: slot_apply(): jnp.einsum('rkc,ch->rkh', left, weight, preferred_element_type=jnp.float32)]
    pallas_call x0 -> x2, Pallas kernels: none -> 121 us  [the longest x1 118 us: run(): pl.pallas_call(functools.partial(kernel, names, features), out_shape=outs...]
    psum x1 -> x0, blocking collectives: 78.4 us -> none  [body(): summed_grads = lax.psum(all_grads, 'res')]
    gather x6 -> x0, local copies, waits for them, and re-layouts: 77.6 us -> none  [the longest x4 51.7 us: three_layers(): far_rows = table[neighbours]]
    reduce_scatter x11 -> x0, waiting for transfers between devices: 44.8 us -> none  [the longest x7 35.7 us: body(): lax.psum_scatter(summed_grads, 'half', scatter_dimension=0, tiled=True)]
    scatter-add x1 -> x0, other arithmetic: 38.2 us -> none  [three_back(): far_table = jnp.zeros((total_rows, width), jnp.float32).at[neighbours.res...]
    ppermute x10 -> x0, starting transfers between devices: 31.9 us -> none  [the longest x3 15.7 us: with_halo(): lax.ppermute(lax.slice_in_dim(block, block.shape[dim] - width, None, axis...]
  transfers between devices with their start and end apart: 25 -> 0, of which waited for: 14 -> 0; matrix products, arithmetic and copies ran while one was open for 23% -> 0% of each run, Pallas kernels for 0% -> 0%
where the time goes in v2:
time: 139 us; the launch traced here: 138 us
  Pallas kernels  121 us (87%)
  local copies, waits for them, and re-layouts  9.66 us (7%)
  other arithmetic  6.99 us (5%)
    pallas_call x1, Pallas kernels, run(): pl.pallas_call(functools.partial(kernel, names, features), out_shape=outs...  118 us
    unnamed x16, local copies, waits for them, and re-layouts  9.66 us
    pad x7, other arithmetic, body(): line = jnp.pad(vector.astype(F32), (0, inner - vector.shape[0]))  4.8 us
    pallas_call x1, Pallas kernels, unpack(): pl.pallas_call(functools.partial(unpack_kernel, width, hidden, features,...  3.18 us

profile of v2, /device:TPU:0, one launch (start us, length us, event | category | flops | bytes accessed | tf_op | source)
XLA Modules:
  0.0 138.4 jit_solution(6148590638473866382)
XLA Ops:
  0.7 0.7 convert_element_type.36
  1.4 0.7 convert_element_type.37
  2.1 0.7 pad_convert_fusion.12
  2.8 0.7 pad_convert_fusion
  3.5 0.7 pad_convert_fusion.2
  4.2 0.7 pad_convert_fusion.4
  4.9 0.7 pad_convert_fusion.6
  5.6 0.7 pad_convert_fusion.8
  6.2 0.7 pad_convert_fusion.10
  6.9 0.8 select_select_fusion.refs_0_
  7.7 117.8 %graph_layer.1 = (bf16[96,256]{1,0:T(8,128)(2,1)}, bf16[30,96,192]{2,1,0:T(8,128)(2,1)}, f32[96,256]{1,0:T(8,128)}, f32[30,96,192]{2,1,0:T(8,128)}, bf16[2304,12...) custom-call(f32[16,2048]{1,0:T(8,128)} %select_select_fusion.refs_0_, ...), custom_call_target="tpu_custom_call" | custom-call | tf_op jit(solution)/shard_map/graph_layer/pallas_call | solution.py:1092
  125.6 0.0 copy-start.3
  125.6 0.0 copy-start.4
  125.6 3.2 %unpack.1 = (f32[608,512]{1,0:T(8,128)}, f32[1,256]{1,0:T(1,128)}, f32[256,512]{1,0:T(8,128)}, f32[1,256]{1,0:T(1,128)}, f32[256,512]{1,0:T(8,128)}, /*index=5*/...) custom-call(bf16[2304,128]{1,0:T(8,128)(2,1)} %get-tuple-element.59., ...), custom_call_target="tpu_custom_call" | custom-call | tf_op jit(solution)/shard_map/unpack/pallas_call | solution.py:1154
  128.8 0.0 copy-start
  128.8 1.6 %copy.60 = bf16[96,256]{1,0:T(8,128)(2,1)} copy(bf16[96,256]{1,0:T(8,128)(2,1)} %get-tuple-element.136) | data formatting | bytes 98304
  130.3 0.0 copy-done.3
  130.3 1.1 copy.61
  131.5 0.0 copy-done.4
  131.5 0.6 copy.62
  132.1 0.0 copy-done
  132.1 0.0 copy-start.2
  132.1 1.6 %copy.63 = f32[96,30,192]{2,0,1:T(8,128)} copy(f32[96,30,192]{2,0,1:T(8,128)S(1)} %bitcast.23) | data formatting | bytes 4423680
  133.7 1.1 copy-done.2
  134.8 0.0 copy-start.1
  134.8 1.3 copy.64
  136.1 1.0 copy-done.1
  137.1 1.3 copy.65
  (9 shorter events, 0.0 us)
Async XLA Ops:
  125.6 4.8 %copy-start.3 = (bf16[30,96,192]{2,1,0:T(8,128)(2,1)S(1)}, bf16[30,96,192]{2,1,0:T(8,128)(2,1)}, u32[]{:S(2)}) copy-start(bf16[30,96,192]{2,1,0:T(8,128)(2,1)} %get-tuple-element.56) | copy-start | bytes 3317764
  125.6 5.9 %copy-start.4 = (f32[96,256]{1,0:T(8,128)S(1)}, f32[96,256]{1,0:T(8,128)}, u32[]{:S(2)}) copy-start(f32[96,256]{1,0:T(8,128)} %get-tuple-element.138) | copy-start | bytes 294916
  128.8 3.3 %copy-start = (f32[30,96,192]{2,1,0:T(8,128)S(1)}, f32[30,96,192]{2,1,0:T(8,128)}, u32[]{:S(2)}) copy-start(f32[30,96,192]{2,1,0:T(8,128)} %get-tuple-element.58) | copy-start | bytes 6635524
  132.1 2.7 %copy-start.2 = (f32[256,2048]{1,0:T(8,128)S(1)}, f32[256,2048]{1,0:T(8,128)}, u32[]{:S(2)}) copy-start(f32[256,2048]{1,0:T(8,128)} %get-tuple-element.148) | copy-start | bytes 6291460
  134.8 2.3 %copy-start.1 = (f32[1024,512]{1,0:T(8,128)S(1)}, f32[1024,512]{1,0:T(8,128)}, u32[]{:S(2)}) copy-start(f32[1024,512]{1,0:T(8,128)} %get-tuple-element.150) | copy-start | bytes 6291460

commit v3 on v2

v3 whole, which is shorter than its diff:
```python
import functools
import types
from typing import Any, NamedTuple

import jax
import jax.numpy as jnp
from jax import lax
from jax.experimental import pallas as pl
from jax.experimental.pallas import tpu as pltpu
from jax.sharding import PartitionSpec as P

EPSILON = 1e-05
REACH = 64
CORES = 2
NEAR = 0.7978845608
CUBE = 0.044715
STEP = 30
CHAIN = 5
BACK_CHAIN = 15
EDGE_CHAIN = 15
EARLY_WIDE = 6
PARTS = 2
LANES = 256
LANE = 128
WIDE = 256
VMEM = 62 * 2**20
MESH = pl.DeviceIdType.MESH
F32 = jnp.float32
BF16 = jnp.bfloat16


def dot(left, right):
    return jnp.dot(left, right, preferred_element_type=F32)


def dot_t(left, right):
    return lax.dot_general(left, right, (((1,), (1,)), ((), ())), preferred_element_type=F32)


def t_dot(left, right):
    return lax.dot_general(left, right, (((0,), (0,)), ((), ())), preferred_element_type=F32)


def two_parts(values):
    high = values.astype(BF16)
    return high, (values - high.astype(F32)).astype(BF16)


def dot_wide(values, right, transposed=False):
    rows = values.shape[0]
    both = (dot_t if transposed else dot)(jnp.concatenate(two_parts(values), 0), right)
    return both[:rows] + both[rows:]


def gelu(values):
    square = values * values
    bend = jnp.tanh(values * (NEAR + (NEAR * CUBE) * square))
    return values * (0.5 + 0.5 * bend)


def gelu_slope(values):
    square = values * values
    part = 0.5 + 0.5 * jnp.tanh(values * (NEAR + (NEAR * CUBE) * square))
    return part + values * part * (1.0 - part) * (2.0 * NEAR + (6.0 * NEAR * CUBE) * square)


def gelu_and_slope(values):
    values = values.astype(BF16)
    square = values * values
    part = BF16(0.5) + BF16(0.5) * jnp.tanh(values * (BF16(NEAR) + BF16(NEAR * CUBE) * square))
    act = values * part
    slope = part + act * (1 - part) * (BF16(2.0 * NEAR) + BF16(6.0 * NEAR * CUBE) * square)
    return act, slope


def norm_parts(values):
    centered = values - jnp.mean(values, -1, keepdims=True)
    scale = lax.rsqrt(jnp.mean(centered * centered, -1, keepdims=True) + EPSILON)
    return centered * scale, scale


def norm_back(grad, unit, scale, gain):
    scaled = gain * grad
    flat = jnp.mean(scaled, -1, keepdims=True)
    slant = jnp.mean(scaled * unit, -1, keepdims=True)
    return (scaled - flat - unit * slant) * scale


def col_sum(values):
    return jnp.sum(values, 0, keepdims=True)


def iota(dims, axis):
    return lax.broadcasted_iota(jnp.int32, dims, axis)


def chip_dims(count):
    side = 1
    while 2 * (2 * side) ** 3 <= count and count % (4 * side * side) == 0:
        side *= 2
    return side, count // (side * side)


def up(size, unit):
    return -(-size // unit) * unit


class Chunks(NamedTuple):
    edge: Any
    third: Any
    first_a: Any
    first_b: Any
    second: Any


ORDERS = Chunks((0, 2, 1), (0, 1, 2), (2, 0, 1), (0, 1, 2), (0, 2, 1))


def chunk_rows(count, width, hidden, features):
    tall = (2 * width + features) // CORES
    wide = width // LANE
    edge = features * (up(tall, LANE) // LANE) + 3 * (features // CORES)
    square = (hidden // CORES) * wide
    first = tall * (wide // 2)
    sizes = (edge, square, first, first + 16 * wide, square)
    return Chunks(*(up(rows, 16 * count) for rows in sizes))


def cut(pieces, start, stop):
    at, got = 0, []
    for piece in pieces:
        low, high = max(start, at), min(stop, at + piece.shape[0])
        if low < high:
            got.append(piece[low - at : high - at])
        at += piece.shape[0]
    return jnp.concatenate(got, 0) if len(got) > 1 else got[0]


def put_wide(pack, half, at, piece):
    rows = piece.shape[0]
    for block in range(piece.shape[1] // LANE):
        pack[half, pl.ds(at, rows), :] = piece[:, block * LANE : (block + 1) * LANE].astype(BF16)
        at += rows
    return at


def put_rest(pack, at):
    rest = pack.shape[1] - at
    if rest:
        for half in range(CORES):
            pack[half, pl.ds(at, rest), :] = jnp.zeros((rest, LANE), BF16)


def take_wide(packed, at, rows, blocks):
    pieces = [packed[pl.ds(at + b * rows, rows), :] for b in range(blocks)]
    return jnp.concatenate(pieces, 1).astype(F32), at + blocks * rows


class Copies:
    def __init__(self, send, recv):
        self.send, self.recv, self.used = send, recv, 0

    def group(self, entries):
        made = []
        for source, target, device in entries:
            at = self.used
            self.used += 1
            made.append(functools.partial(self._make, source, target, device, at))
        return Group(made)

    def _make(self, source, target, device, at):
        return pltpu.make_async_remote_copy(
            src_ref=source,
            dst_ref=target,
            send_sem=self.send.at[at],
            recv_sem=self.recv.at[at],
            device_id=device,
            device_id_type=MESH,
        )


class Group:
    def __init__(self, made):
        self.made = made

    def start(self):
        for make in self.made:
            make().start()

    def wait(self):
        for make in self.made:
            make().wait()


class Place:
    def __init__(self):
        res, half, count = lax.axis_index("res"), lax.axis_index("half"), lax.axis_size("res")
        side, deep = chip_dims(count)
        x, y, z = lax.rem(res, side), lax.rem(res // side, side), res // (side * side)
        first = half == 0
        self.res, self.half, self.count = res, half, count
        self.dims = (side, side, deep)
        self.at = (jnp.where(first, x, y), jnp.where(first, y, x), z)
        self.strides = (jnp.where(first, 1, side), jnp.where(first, side, 1), side * side)
        self.partner = (res, 1 - half)

    def peers(self, level):
        size, here = self.dims[level], self.at[level]
        found = []
        for ahead in range(1, size):
            to = lax.rem(here + ahead, size)
            found.append((to, (self.res + (to - here) * self.strides[level], self.half)))
        return found

    def line(self):
        res, half, count = self.res, self.half, self.count
        return (
            (res > 0, (res - 1, half)),
            (res + half > 0, (res - 1 + half, 1 - half)),
            (res + half < count, (res + half, 1 - half)),
            (res < count - 1, (res + 1, half)),
        )

    def line_count(self):
        res, half, count = self.res, self.half, self.count
        return 4 - jnp.where(res > 0, 0, 2 - half) - jnp.where(res < count - 1, 0, 1 + half)


def greet(place):
    barrier = pltpu.get_barrier_semaphore()

    def signal(device):
        pl.semaphore_signal(barrier, inc=1, device_id=device, device_id_type=MESH)

    for exists, device in place.line():
        pl.when(exists)(functools.partial(signal, device))
    signal(place.partner)
    others = 1
    for level in range(3):
        for _, device in place.peers(level):
            signal(device)
            others += 1
    pl.semaphore_wait(barrier, others + place.line_count())


def halo_layout(rows):
    edge = REACH - rows
    return ((0, edge), (edge, rows), (REACH + rows, rows), (REACH + 2 * rows, edge))


class Halo:
    def __init__(self, place, window, rows, send, recv, first):
        self.place, self.window, self.rows = place, window, rows
        self.send, self.recv, self.first = send, recv, first

    def clear(self):
        for (exists, _), (offset, size) in zip(self.place.line(), halo_layout(self.rows)):

            @pl.when(jnp.logical_not(exists))
            def _():
                self.window[pl.ds(offset, size), :] = jnp.zeros((size, self.window.shape[1]), self.window.dtype)

    def _copy(self, at, device):
        offset, size = halo_layout(self.rows)[3 - at]
        first = REACH + (self.rows - size if at == 3 else 0)
        return pltpu.make_async_remote_copy(
            src_ref=self.window.at[pl.ds(first, size)],
            dst_ref=self.window.at[pl.ds(offset, size)],
            send_sem=self.send.at[self.first + at],
            recv_sem=self.recv.at[self.first + 3 - at],
            device_id=device,
            device_id_type=MESH,
        )

    def start(self):
        for at, (exists, device) in enumerate(self.place.line()):

            @pl.when(exists)
            def _():
                self._copy(at, device).start()

    def wait(self):
        for at, (exists, device) in enumerate(self.place.line()):
            offset, size = halo_layout(self.rows)[at]

            @pl.when(exists)
            def _():
                self._copy(at, device).wait_send()
                pltpu.make_async_remote_copy(
                    src_ref=self.window.at[pl.ds(offset, size)],
                    dst_ref=self.window.at[pl.ds(offset, size)],
                    send_sem=self.send.at[self.first + at],
                    recv_sem=self.recv.at[self.first + at],
                    device_id=device,
                    device_id_type=MESH,
                ).wait_recv()


class Returns:
    def __init__(self, place, table, landing, rows, send, recv, first):
        self.place, self.table, self.landing, self.rows = place, table, landing, rows
        self.send, self.recv, self.first = send, recv, first

    def _copy(self, at, device):
        layout = halo_layout(self.rows)
        offset, size = layout[at]
        return pltpu.make_async_remote_copy(
            src_ref=self.table.at[pl.ds(offset, size)],
            dst_ref=self.landing.at[pl.ds(layout[3 - at][0], size)],
            send_sem=self.send.at[self.first + at],
            recv_sem=self.recv.at[self.first + 3 - at],
            device_id=device,
            device_id_type=MESH,
        )

    def start(self):
        for at, (exists, device) in enumerate(self.place.line()):

            @pl.when(exists)
            def _():
                self._copy(at, device).start()

    def finish(self, total):
        total[...] = self.table[pl.ds(REACH, self.rows), :]
        for at, (exists, device) in enumerate(self.place.line()):
            offset, size = halo_layout(self.rows)[at]
            first = self.rows - size if at == 3 else 0

            @pl.when(exists)
            def _():
                self._copy(at, device).wait_send()
                pltpu.make_async_remote_copy(
                    src_ref=self.table.at[pl.ds(offset, size)],
                    dst_ref=self.landing.at[pl.ds(offset, size)],
                    send_sem=self.send.at[self.first + at],
                    recv_sem=self.recv.at[self.first + at],
                    device_id=device,
                    device_id_type=MESH,
                ).wait_recv()
                total[pl.ds(first, size), :] += self.landing[pl.ds(offset, size), :]


def gather_groups(place, copies, ref, unit, source=None, base=0):
    mine = (place.at[0] * place.dims[1] + place.at[1]) * place.dims[2] + place.at[2]
    groups, size = [], unit
    start = mine * unit
    for level in (2, 1, 0):
        here = ref.at[pl.ds(pl.multiple_of(base + start, 16), size)]
        from_ref = here if source is None or level < 2 else source
        groups.append(copies.group([(from_ref, here, device) for _, device in place.peers(level)]))
        start = start - place.at[level] * size
        size = size * place.dims[level]
    return groups


class ChipSum:
    def __init__(self, place, copies, order, pack, got, landed, gathered):
        self.place, self.pack, self.got, self.landed, self.gathered = place, pack, got, landed, gathered
        half, size = place.half, pack.shape[1]
        self.pair = copies.group([(pack.at[1 - half], got, place.partner)])
        self.steps, self.shares, self.back = [], [], []
        start, base = 0, 0
        for level in order:
            share = size // place.dims[level]
            entries, lands = [], []
            for to, device in place.peers(level):
                source = pack.at[half, pl.ds(pl.multiple_of(start + to * share, 16), share)]
                entries.append((source, landed.at[pl.ds(base, share)], device))
                lands.append(base)
                base += share
            start = pl.multiple_of(start + place.at[level] * share, 16)
            size = share
            self.steps.append(copies.group(entries))
            self.shares.append((start, share, lands))
            here = gathered.at[pl.ds(start, share)]
            back = [(here, here, device) for _, device in place.peers(level)]
            self.back.insert(0, copies.group(back))

    def send_pair(self):
        self.pair.start()

    def add_pair(self):
        self.pair.wait()
        half = self.place.half
        self.pack[half] = (self.pack[half].astype(F32) + self.got[...].astype(F32)).astype(BF16)

    def start(self, level):
        self.steps[level].start()

    def finish(self, level):
        self.steps[level].wait()
        start, share, lands = self.shares[level]
        half = self.place.half
        total = self.pack[half, pl.ds(start, share), :].astype(F32)
        for base in lands:
            total = total + self.landed[pl.ds(base, share), :].astype(F32)
        if level < len(self.steps) - 1:
            self.pack[half, pl.ds(start, share), :] = total.astype(BF16)
        else:
            self.gathered[pl.ds(start, share), :] = total.astype(BF16)

    def start_back(self, step):
        self.back[step].start()

    def finish_back(self, step):
        self.back[step].wait()


def flat(values):
    return values.reshape(values.shape[0] * values.shape[1], values.shape[2])


def feed_forward(r, pooled, own):
    width = own.shape[1]
    mean = pooled / r.counts[:, 0:1]
    summed = own + dot_wide(mean, r.third[...]) + r.b_three
    unit, _ = norm_parts(summed)
    normed = unit * r.gain_one + r.shift_one
    low = normed.astype(BF16)
    pre = dot(low, r.expand[...]) + r.b_expand
    second = normed + dot(gelu(pre).astype(BF16), r.reduce[...]) + r.b_reduce
    unit_two, _ = norm_parts(second)
    r.summed[...] = summed
    r.pre_expand[...] = pre
    r.second[...] = second
    r.normed[...] = low
    return unit_two * r.gain_two + r.shift_two


def fill_table(window, far, own, bias, table, rows, multiply):
    places = window.shape[0]
    table[pl.ds(0, places), :] = multiply(window[...], far).astype(BF16)
    table[pl.ds(places, rows), :] = (multiply(window[pl.ds(REACH, rows), :], own) + bias).astype(BF16)


def chain_parts(step):
    return [step * STEP + part * CHAIN for part in range(STEP // CHAIN)]


def chain_rows(r, slot):
    rows = r.counts.shape[0]
    return pl.ds(pl.multiple_of(slot * rows, CHAIN * rows), CHAIN * rows)


def step_rows(r, step):
    rows = r.counts.shape[0]
    return pl.ds(pl.multiple_of(step * (STEP * rows), STEP * rows), STEP * rows)


def build_block(r, step, half, places):
    rows = r.counts.shape[0]
    here = pl.ds(step * STEP, STEP)
    named = r.picks[here]
    dims = (STEP, rows, named.shape[2])
    spread = jnp.broadcast_to(named, dims)
    mine = iota(dims, 2) == iota(dims, 1) + half * rows
    pick = jnp.sum(jnp.where(mine, spread, 0.0), -1, keepdims=True)
    dims = (STEP, rows, LANES)
    lane = iota(dims, 2)
    hit = (lane.astype(F32) == pick) | (lane == iota(dims, 1) + places)
    r.onehot[here] = jnp.where(hit, 1.0, 0.0).astype(BF16)


def joined_rows(r, slot, slots):
    here = pl.ds(slot, slots)
    return jnp.concatenate([flat(r.onehot[here]), flat(r.edges_raw[here])], 1)


def live_rows(r, slot, width):
    count = r.counts[...]
    dims = (CHAIN,) + count.shape
    live = jnp.where(iota(dims, 0) + slot < count[None], 1.0, 0.0)
    return flat(jnp.concatenate([live] * (width // LANE), -1))


def live_column(r, slot, slots):
    count = r.counts[...]
    dims = (slots,) + count.shape
    return flat(jnp.where(iota(dims, 0) + slot < count[None], 1.0, 0.0))[:, 0:1]


def node_block(r, step, keep):
    rows = r.counts.shape[0]
    hidden = r.second_w.shape[0]
    slots = chain_parts(step)
    dims = (rows, CHAIN * rows)
    count = jnp.broadcast_to(r.counts[:, 0:1], dims)
    pre = [dot(joined_rows(r, slot, CHAIN), r.table[...]) for slot in slots]
    acts = []
    for slot, values in zip(slots, pre):
        if keep:
            here = chain_rows(r, slot)
            act, slope = gelu_and_slope(values)
            r.act[here, :] = act
            r.slope_one[here, :] = slope
        else:
            act = gelu(values).astype(BF16)
        acts.append(act)
    pre = [dot(act, r.second_w[...]) + r.b_two for act in acts]
    total = r.pooled[...]
    for slot, values in zip(slots, pre):
        if keep:
            act, slope = gelu_and_slope(values)
            r.slope_two[chain_rows(r, slot), :] = slope * live_rows(r, slot, hidden).astype(BF16)
        else:
            act = gelu(values)
        used = jnp.where(r.lane_slot[0:1, :] + slot.astype(F32) < count, r.diagonal[...], 0.0)
        total = total + dot(used.astype(BF16), act.astype(BF16))
    r.pooled[...] = total


def edge_block(r, step, features):
    rows = r.counts.shape[0]
    split = lambda values: values.reshape(values.shape[0] // rows, rows, features)
    slots = [step * STEP + part * EDGE_CHAIN for part in range(STEP // EDGE_CHAIN)]
    each = lambda body, *lists: [body(*items) for items in zip(*lists)]
    joined = [joined_rows(r, slot, EDGE_CHAIN) for slot in slots]
    live = [live_column(r, slot, EDGE_CHAIN) for slot in slots]
    pre = each(lambda z: dot(z, r.e_table[...]), joined)
    o_one, slope_one = zip(*each(gelu_and_slope, pre))
    pre = each(lambda a: dot(a, r.e_second_w[...]) + r.eb_two, o_one)
    o_two, slope_two = zip(*each(gelu_and_slope, pre))
    summed = each(lambda z, a: z[:, LANES:].astype(F32) + (dot(a, r.e_third_w[...]) + r.eb_three), joined, o_two)
    unit, scale = zip(*each(norm_parts, summed))
    d_three, d_sums = [], []
    for slot, u, k, used in zip(slots, unit, scale, live):
        here = pl.ds(slot, EDGE_CHAIN)
        r.edge_out[here] = split((u * r.e_gain + r.e_shift) * used).astype(BF16)
        d_out = flat(r.cots_raw[here]).astype(F32) * used
        r.ge_norm[0:1, :] += col_sum(d_out * u)
        r.ge_norm[1:2, :] += col_sum(d_out)
        d_sum = norm_back(d_out, u, k, r.e_gain)
        r.ge_norm[2:3, :] += col_sum(d_sum)
        d_sums.append(d_sum)
        d_three.append(d_sum.astype(BF16))
    d_two = each(lambda d, k: dot_t(d, r.e_third_w[...]) * k, d_three, slope_two)
    r.ge_norm[3:4, :] += sum(col_sum(d) for d in d_two)
    d_two = each(lambda d: d.astype(BF16), d_two)
    d_one = each(lambda d, k: (dot_t(d, r.e_second_w[...]) * k).astype(BF16), d_two, slope_one)
    for slot, d_sum, d in zip(slots, d_sums, d_one):
        more = dot(d, r.e_first_t[:, pl.ds(2 * r.nodes_width, features)])
        r.edge_grad[pl.ds(slot, EDGE_CHAIN)] = split(d_sum + more)
    together = lambda values: jnp.concatenate(values, 0)
    r.ge_third[...] += t_dot(together(o_two), together(d_three))
    r.ge_second[...] += t_dot(together(o_one), together(d_two))
    r.ge_first[...] += t_dot(together(joined), together(d_one))


def node_grad(r, cot, far_total, when_ds):
    width = cot.shape[1]
    grad = cot.astype(F32) + r.e_own_back[...] + dot_wide(far_total, r.e_first_t[:, pl.ds(width, width)])
    unit, scale = norm_parts(r.second[...])
    dw = norm_back(grad, unit, scale, r.gain_two)
    gain_two, shift_two = col_sum(grad * unit), col_sum(grad)
    ds = dw.astype(BF16)
    r.ds[...] = ds
    when_ds()
    slope = gelu_slope(r.pre_expand[...])
    dq = (dot_t(ds, r.reduce[...]) * slope).astype(BF16)
    dv = dw + dot_t(dq, r.expand[...])
    unit, scale = norm_parts(r.summed[...])
    du = norm_back(dv, unit, scale, r.gain_one)
    r.du[...] = du
    counts = r.counts[:, 0:1]
    dm = (du / counts).astype(BF16)
    r.slot_grad[...] = dot_t(dm, r.third[...])
    r.dm[...] = dm
    small = r.small
    small[...] = jnp.zeros(small.shape, F32)
    small[2:3, :] = col_sum(counts * dm.astype(F32))
    small[3:4, :] = col_sum(dv * unit)
    small[4:5, :] = col_sum(dv)
    dq_sum = col_sum(dq.astype(F32))
    for part in range(dq_sum.shape[1] // width):
        small[5 + part : 6 + part, :] = dq_sum[:, part * width : (part + 1) * width]
    small[9:10, :] = col_sum(ds.astype(F32))
    small[10:11, :] = gain_two
    small[11:12, :] = shift_two


def put_features(pack, half, at, e_second, e_third):
    part = e_second.shape[0] // CORES
    two = [ref[pl.ds(half * part, part), :] for ref in (e_second, e_third)]
    for piece in two:
        at = put_wide(pack, half, at, piece[:, :LANE])
    return put_wide(pack, half, at, jnp.concatenate([piece[:, LANE:] for piece in two], 1))


def pack_edge(r, pack):
    features = r.ge_second.shape[0]
    g_edge = jnp.transpose(r.ge_first[pl.ds(LANES, features), :])
    e_first = jnp.concatenate([r.ge_own[...], r.ge_far[...], g_edge], 1)
    tall = e_first.shape[1] // CORES
    fill = jnp.zeros((features, up(tall, LANE) - tall), F32)
    for half in range(CORES):
        piece = jnp.concatenate([e_first[:, half * tall : (half + 1) * tall], fill], 1)
        at = put_wide(pack, half, 0, piece)
        at = put_features(pack, half, at, r.ge_second, r.ge_third)
    put_rest(pack, at)


def pack_third(r, pack):
    dm = r.dm[...]
    found = t_dot(jnp.concatenate(two_parts(r.pooled[...]), 0), jnp.concatenate([dm, dm], 0))
    part = found.shape[0] // CORES
    for half in range(CORES):
        at = put_wide(pack, half, 0, found[half * part : (half + 1) * part])
    put_rest(pack, at)


def pack_second(r, pack):
    part = r.g_second.shape[0] // CORES
    for half in range(CORES):
        at = put_wide(pack, half, 0, r.g_second[pl.ds(half * part, part), :])
    put_rest(pack, at)


def small_rows(r, places):
    rows = r.counts.shape[0]
    features = r.ge_norm.shape[1]
    fill = jnp.zeros((1, LANES - features), F32)
    own = pl.ds(places, rows)
    edge = [col_sum(r.ge_first[own, :])] + [r.ge_norm[at : at + 1, :] for at in (3, 2, 0, 1)]
    edge = [jnp.concatenate([row, fill], 1) for row in edge] + [jnp.zeros((1, LANES), F32)]
    lines = [col_sum(r.g_first[own, :]), r.g_bias[...], r.small[2:12, :]]
    lines += [jnp.concatenate(edge[at : at + 2], 1) for at in (0, 2, 4)]
    return jnp.concatenate(lines + [jnp.zeros((1, r.small.shape[1]), F32)], 0)


def pack_first(r, packs, g_own, g_far, features, small):
    pieces = [g_own, g_far, r.g_first[pl.ds(LANES, features), :]]
    tall = sum(piece.shape[0] for piece in pieces) // CORES
    hidden = g_own.shape[1]
    for side, pack in enumerate(packs):
        cols = slice(side * (hidden // 2), (side + 1) * (hidden // 2))
        for half in range(CORES):
            at = put_wide(pack, half, 0, cut([piece[:, cols] for piece in pieces], half * tall, (half + 1) * tall))
            if side == 1:
                at = put_wide(pack, half, at, small)
        put_rest(pack, at)


def first_grad_block(r, step, features):
    rows = r.counts.shape[0]
    hidden = r.act.shape[1]
    coming = jnp.broadcast_to(r.slot_grad[...][None], (BACK_CHAIN,) + r.slot_grad.shape)
    slots = [step * STEP + part * BACK_CHAIN for part in range(STEP // BACK_CHAIN)]
    places = [pl.ds(pl.multiple_of(slot * rows, BACK_CHAIN * rows), BACK_CHAIN * rows) for slot in slots]
    twos, ones = [], []
    for here in places:
        d_two = flat(coming) * r.slope_two[here, :].astype(F32)
        r.g_bias[...] += col_sum(d_two)
        twos.append(d_two.astype(BF16))
        r.slope_two[here, :] = twos[-1]
    backs = [dot_t(d_two, r.second_w[...]) for d_two in twos]
    for here, back in zip(places, backs):
        ones.append((back * r.slope_one[here, :].astype(F32)).astype(BF16))
        r.slope_one[here, :] = ones[-1]
    r.g_first[...] += t_dot(joined_rows(r, step * STEP, STEP), jnp.concatenate(ones, 0))


def second_grad_block(r, step, features):
    rows = r.counts.shape[0]
    here = step_rows(r, step)
    r.g_second[...] += t_dot(r.act[here, :], r.slope_two[here, :])
    more = dot_t(r.slope_one[here, :], r.table[pl.ds(LANES, features), :])
    r.edge_grad[pl.ds(step * STEP, STEP)] += more.reshape(STEP, rows, features)


class WideBlock:
    def __init__(self, r, step, half):
        width, inner = r.expand.shape
        blocks = inner // WIDE
        self.r, self.step, self.mine = r, step, blocks // CORES
        self.block = lax.rem(step + half * self.mine, blocks)
        self.here = pl.ds(pl.multiple_of(self.block * WIDE, WIDE), WIDE)
        part = width // CORES
        self.cols = pl.ds(pl.multiple_of(half * part, part), part)
        self.total = r.normed_all.shape[0]
        size = self.total // PARTS
        self.rows = [pl.ds(at * size, size) for at in range(PARTS)]

    def forward(self):
        r = self.r
        bias = r.bias_wide[pl.ds(self.block, 1), :]
        pre = [dot(r.normed_all[rows, :], r.expand[:, self.here]) + bias for rows in self.rows]
        both = [gelu_and_slope(values) for values in pre]
        return [act for act, _ in both], [slope for _, slope in both]

    def place(self, slot, rows=None):
        size = self.total if rows is None else rows.size
        first = (slot // 2) * self.total + (0 if rows is None else rows.start)
        return self.r.kept.at[
            pl.ds(pl.multiple_of(first, 16), size), pl.ds(pl.multiple_of(lax.rem(slot, 2) * WIDE, WIDE), WIDE)
        ]

    def keep(self):
        acts, slopes = self.forward()
        for rows, slope in zip(self.rows, slopes):
            self.place(self.step, rows)[...] = slope

        @pl.when(self.step < self.mine)
        def _():
            for rows, act in zip(self.rows, acts):
                self.place(EARLY_WIDE + self.step, rows)[...] = act

    def backward(self, slopes, act, fresh):
        r = self.r
        back = [dot_t(r.ds_all[rows, :], r.reduce[self.here, :]) for rows in self.rows]
        dqs = [(grad * slope.astype(F32)).astype(BF16) for grad, slope in zip(back, slopes)]
        found = t_dot(r.normed_all[:, self.cols], jnp.concatenate(dqs, 0))
        r.g_expand[:, self.here] = found if fresh else r.g_expand[:, self.here] + found

        @pl.when(self.step < self.mine)
        def _():
            out = pl.ds(pl.multiple_of(self.step * WIDE, WIDE), WIDE)
            found = t_dot(act(), r.ds_all[...])
            r.g_reduce[out, :] = found if fresh else r.g_reduce[out, :] + found

    def from_kept(self):
        slopes = [self.place(self.step, rows)[...] for rows in self.rows]
        self.backward(slopes, lambda: self.place(EARLY_WIDE + self.step)[...], True)

    def whole(self, fresh):
        acts, slopes = self.forward()
        self.backward(slopes, lambda: jnp.concatenate(acts, 0), fresh)


class Vectors(NamedTuple):
    b_one: Any
    b_two: Any
    b_three: Any
    gain_one: Any
    shift_one: Any
    b_reduce: Any
    gain_two: Any
    shift_two: Any
    b_expand: Any
    eb_one: Any
    eb_two: Any
    eb_three: Any
    e_gain: Any
    e_shift: Any
    counts_in: Any


class Arrays(NamedTuple):
    nodes: Any
    edges: Any
    neighbours: Any
    first_in: Any
    second_in: Any
    third_in: Any
    expand_in: Any
    reduce_in: Any
    e_first_in: Any
    e_second_in: Any
    e_third_in: Any
    cot_nodes: Any
    cot_edges: Any


class Results(NamedTuple):
    state_out: Any
    edges_out: Any
    fed_out: Any
    grads_out: Any
    expand_out: Any
    reduce_out: Any
    normed_slots: Any
    ds_slots: Any


def kernel(names, features, *refs):
    kinds, refs = (Vectors, Arrays, Results), list(refs)
    r = types.SimpleNamespace()
    for kind in kinds:
        for name in kind._fields:
            setattr(r, name, refs.pop(0))
    r.sums_out = Chunks(*(refs.pop(0) for _ in Chunks._fields))
    for name in names:
        setattr(r, name, refs.pop(0))
    r.pack, r.got, r.landed, r.gathered = (Chunks(*(refs.pop(0) for _ in Chunks._fields)) for _ in range(4))
    place = Place()
    res, half, count = place.res, place.half, place.count
    rows_dev, width = r.nodes.shape
    rows = rows_dev // CORES
    places = rows + 2 * REACH
    slots = r.edges.shape[0]
    each = slots // CORES
    steps = slots // STEP
    r.nodes_width = width
    total = r.edges_raw.shape[0] * rows
    r.act, r.slope_one, r.slope_two = (r.kept.at[pl.ds(at * total, total)] for at in range(3))
    for name in Vectors._fields:
        vector = getattr(r, name)
        setattr(r, name, vector[...].astype(F32).reshape(1, vector.shape[0]))
    own = pl.ds(REACH, rows)
    mine = pl.ds(pl.multiple_of(half * rows, 16), rows)

    pairs = dict(
        nodes=(r.nodes.at[mine], r.windows.at[0, own]),
        neighbours=(r.neighbours, r.neighbours_raw),
        first=(r.first_in, r.first),
        edges=(r.edges.at[:, mine, :], r.edges_raw),
        second=(r.second_in, r.second_w),
        e_first=(r.e_first_in, r.e_first_t),
        e_second=(r.e_second_in, r.e_second_w),
        e_third=(r.e_third_in, r.e_third_w),
        third=(r.third_in, r.third),
        expand=(r.expand_in, r.expand),
        reduce=(r.reduce_in, r.reduce),
        cot_edges=(r.cot_edges.at[:, mine, :], r.cots_raw),
        cot_nodes=(r.cot_nodes.at[mine], r.cot_rows),
    )
    loads = types.SimpleNamespace()
    for at, (name, pair) in enumerate(pairs.items()):
        copy = pltpu.make_async_copy(*pair, r.load_sem.at[at])
        setattr(loads, name, copy)
        copy.start()

    halos = [
        Halo(place, r.windows.at[k], rows, r.line_send, r.line_recv, 4 * k) for k in range(3)
    ]
    edge_returns = Returns(place, r.ge_first, r.edge_landing, rows, r.line_send, r.line_recv, 12)
    node_returns = Returns(place, r.g_first, r.node_landing, rows, r.line_send, r.line_recv, 16)
    copies = Copies(r.step_send, r.step_recv)
    edge, third, first_a, first_b, second = sums = Chunks(
        *(ChipSum(place, copies, *parts) for parts in zip(ORDERS, r.pack, r.got, r.landed, r.gathered))
    )
    span = count * rows

    def row_gather(source, slot_ref):
        base = half * span
        groups = gather_groups(place, copies, slot_ref, rows, source, base)
        here = slot_ref.at[pl.ds(pl.multiple_of(base, 16), span)]
        groups.append(copies.group([(here, here, place.partner)]))
        return groups

    normed_gather = row_gather(r.normed, r.normed_slots)
    ds_gather = row_gather(r.ds, r.ds_slots)
    my_unit = (place.at[0] * place.dims[1] + place.at[1]) * place.dims[2] + place.at[2]
    my_slot = pl.ds(pl.multiple_of(half * span + my_unit * rows, 16), rows)
    normed_keep = pltpu.make_async_copy(r.normed, r.normed_slots.at[my_slot], r.keep_sem.at[0])
    ds_keep = pltpu.make_async_copy(r.ds, r.ds_slots.at[my_slot], r.keep_sem.at[1])
    there = pl.ds(pl.multiple_of(half * rows, 16), rows)
    my_slots = pl.ds(half * each, each)
    its_slots = pl.ds((1 - half) * each, each)
    edges_target = r.edges_out.at[:, there, :]
    edges_pair = copies.group([(r.edge_out.at[its_slots], edges_target, place.partner)])
    edges_keep = pltpu.make_async_copy(r.edge_out.at[my_slots], edges_target, r.keep_sem.at[2])
    grads_target = r.grads_out.at[:, there, :]
    grads_pair = copies.group([(r.edge_grad.at[its_slots], grads_target, place.partner)])
    grads_keep = pltpu.make_async_copy(r.edge_grad.at[my_slots], grads_target, r.keep_sem.at[3])
    fed_pair = copies.group([(r.fed_grad.at[1 - half], r.fed_out.at[there], place.partner)])
    fed_keep = pltpu.make_async_copy(r.fed_grad.at[half], r.fed_out.at[there], r.keep_sem.at[4])

    greet(place)
    loads.nodes.wait()
    halos[0].start()
    for halo in halos:
        halo.clear()
    dims = (rows, LANE)
    counted = jnp.broadcast_to(r.counts_in, (rows, rows_dev))
    here = iota(counted.shape, 1) == iota(counted.shape, 0) + half * rows
    r.counts[...] = jnp.broadcast_to(jnp.sum(jnp.where(here, counted, 0.0), -1, keepdims=True), dims)
    for block in range(r.expand.shape[1] // WIDE):
        r.bias_wide[block : block + 1, :] = r.b_expand[:, block * WIDE : (block + 1) * WIDE]
    dims = (rows, CHAIN * rows)
    lane = iota(dims, 1)
    r.diagonal[...] = jnp.where(lax.rem(lane, rows) == iota(dims, 0), 1.0, 0.0)
    r.lane_slot[...] = (iota(r.lane_slot.shape, 1) // rows).astype(F32)
    loads.neighbours.wait()
    base = res * rows_dev + half * rows - REACH
    named = (r.neighbours_raw[...] - base).astype(F32)
    r.picks[...] = named.reshape(slots, 1, rows_dev)

    def build(step, carry):
        build_block(r, step, half, places)
        return carry

    lax.fori_loop(0, steps, build, 0)
    for table in (r.table, r.e_table):
        rest = LANES - places - rows
        if rest:
            table[pl.ds(places + rows, rest), :] = jnp.zeros((rest, table.shape[1]), BF16)
    for load in (loads.first, loads.e_first, loads.e_second, loads.e_third):
        load.wait()
    r.table[pl.ds(LANES, features), :] = r.first[pl.ds(2 * width, features), :]
    edge_part = r.e_first_t[:, pl.ds(2 * width, features)]
    r.e_table[pl.ds(LANES, features), :] = jnp.transpose(edge_part.astype(F32)).astype(BF16)
    loads.edges.wait()
    bias = r.b_one
    far_w, own_w = r.first[pl.ds(width, width), :], r.first[pl.ds(0, width), :]
    halos[0].wait()
    fill_table(r.windows.at[0], far_w, own_w, bias, r.table, rows, dot)
    r.pooled[...] = jnp.zeros(r.pooled.shape, F32)
    loads.second.wait()

    def first_pass(step, carry):
        node_block(r, step, False)
        return carry

    lax.fori_loop(0, steps, first_pass, 0)
    loads.third.wait()
    loads.expand.wait()
    loads.reduce.wait()
    r.windows[1, own, :] = feed_forward(r, r.pooled[...], r.windows[0, own, :].astype(F32)).astype(BF16)

    halos[1].start()
    loads.cot_edges.wait()
    loads.cot_nodes.wait()
    halos[1].wait()
    fill_table(r.windows.at[1], far_w, own_w, bias, r.table, rows, dot)
    r.pooled[...] = jnp.zeros(r.pooled.shape, F32)

    def second_pass(step, carry):
        node_block(r, step, True)
        return carry

    lax.fori_loop(0, steps, second_pass, 0)
    r.windows[2, own, :] = feed_forward(r, r.pooled[...], r.windows[1, own, :].astype(F32)).astype(BF16)

    halos[2].start()
    normed_keep.start()
    normed_gather[0].start()
    for ref in (r.ge_norm, r.ge_first, r.ge_second, r.ge_third, r.g_second, r.g_first, r.g_bias):
        ref[...] = jnp.zeros(ref.shape, F32)
    halos[2].wait()
    e_own, e_far = r.e_first_t[:, pl.ds(0, width)], r.e_first_t[:, pl.ds(width, width)]
    fill_table(r.windows.at[2], e_far, e_own, r.eb_one, r.e_table, rows, dot_t)
    state_keep = pltpu.make_async_copy(
        r.windows.at[
            2,
            pl.ds(pl.multiple_of(REACH - half * rows, 16), rows_dev),
            pl.ds(pl.multiple_of(half * (width // CORES), width // CORES), width // CORES),
        ],
        r.state_out,
        r.keep_sem.at[5],
    )
    state_keep.start()

    def loop(count, body, events=None):
        def one(step, carry):
            body(step)
            for when, actions in (events or {}).items():

                @pl.when(step == when)
                def _():
                    for act in actions:
                        act()

            return carry

        lax.fori_loop(0, count, one, 0)

    loop(
        steps,
        lambda step: edge_block(r, step, features),
        {0: (normed_keep.wait, normed_gather[0].wait, normed_gather[1].start)},
    )
    edge_returns.start()
    edges_keep.start()
    normed_gather[1].wait()
    normed_gather[2].start()
    own_spread = r.ge_first[pl.ds(places, rows), :]
    r.ge_own[...] = t_dot(own_spread.astype(BF16), r.windows[2, own, :])
    r.ge_far[...] = t_dot(r.ge_first[pl.ds(0, places), :].astype(BF16), r.windows[2])
    pack_edge(r, r.pack.edge)
    edge.send_pair()
    edges_pair.start()
    r.e_own_back[...] = dot_wide(own_spread, e_own)

    outs = [(r.g_expand, r.expand_out), (r.g_reduce, r.reduce_out)] + list(zip(r.gathered, r.sums_out))
    stores = [pltpu.make_async_copy(*pair, r.keep_sem.at[8 + at]) for at, pair in enumerate(outs)]
    expand_store, reduce_store = stores[:2]
    sum_stores = dict(zip(sums, stores[2:]))

    def move(chunk, at):
        if at == 0:
            chunk.add_pair()
            chunk.start(0)
        elif at < 3:
            chunk.finish(at - 1)
            chunk.start(at)
        elif at == 3:
            chunk.finish(2)
            chunk.start_back(0)
        elif at < 6:
            chunk.finish_back(at - 4)
            chunk.start_back(at - 3)
        else:
            chunk.finish_back(2)
            sum_stores[chunk].start()

    def ahead(groups, at):
        groups[at].wait()
        if at + 1 < len(groups):
            groups[at + 1].start()

    def moves(*pairs):
        for chunk, at in pairs:
            (move if isinstance(chunk, ChipSum) else ahead)(chunk, at)

    def events(*pairs):
        return (functools.partial(moves, *pairs),)

    moves((edge, 0))
    edge_returns.finish(r.edge_total)

    def send_ds():
        ds_keep.start()
        ds_gather[0].start()

    node_grad(r, r.cot_rows[...], r.edge_total[...], send_ds)
    pack_third(r, r.pack.third)
    third.send_pair()
    loop(steps, lambda step: first_grad_block(r, step, features), {0: events((third, 0))})
    node_returns.start()
    moves((normed_gather, 2))
    own_spread = r.g_first[pl.ds(places, rows), :]
    g_own = t_dot(r.windows[1, own, :], own_spread.astype(BF16))
    g_far = t_dot(r.windows[1], r.g_first[pl.ds(0, places), :].astype(BF16))
    pack_first(r, (r.pack.first_a, r.pack.first_b), g_own, g_far, features, small_rows(r, places))
    first_a.send_pair()
    first_b.send_pair()
    moves((edge, 1))
    ds_keep.wait()
    moves((ds_gather, 0))
    own_back = r.du[...] + dot_wide(own_spread, own_w, True)
    loop(steps, lambda step: second_grad_block(r, step, features), {0: events((third, 1))})
    moves((normed_gather, 3), (first_a, 0))
    pack_second(r, r.pack.second)
    second.send_pair()
    grads_keep.start()
    moves((first_b, 0))
    grads_pair.start()
    node_returns.finish(r.node_total)
    fed = own_back + dot_wide(r.node_total[...], far_w, True)
    for part in range(CORES):
        r.fed_grad[part] = fed[:, part * (width // CORES) : (part + 1) * (width // CORES)]
    fed_keep.start()
    fed_pair.start()

    blocks = r.expand.shape[1] // WIDE
    chunk = r.normed_all.shape[0]
    chunks = 2 * span // chunk
    waiting = events((second, 0), (ds_gather, 1), (edge, 2), (third, 2)), events((first_b, 1))
    until_ds = (
        (second, 1), (first_a, 1), (third, 3), (ds_gather, 2), (edge, 3), (first_b, 2), (second, 2), (first_a, 2),
        (third, 4), (edge, 4), (ds_gather, 3),
    )
    beside = {
        0: events((second, 3)),
        1: events((first_a, 3), (first_b, 3)),
        2: events((third, 5)),
        3: events((second, 4)) + (reduce_store.start,),
        4: events((first_a, 4), (edge, 5)),
        5: events((first_b, 4)),
        6: events((third, 6), (first_a, 5)),
        7: events((second, 5), (edge, 6), (first_b, 5)),
    }

    def fetch(slots, target, sem, at=0):
        return pltpu.make_async_copy(slots.at[pl.ds(at * chunk, chunk)], target, r.keep_sem.at[sem])

    if chunks == 1:
        normed_fetch = fetch(r.normed_slots, r.normed_all, 6)
        normed_fetch.start()
        normed_fetch.wait()
        loop(EARLY_WIDE, lambda step: WideBlock(r, step, half).keep(), {1: waiting[0], 4: waiting[1]})
        moves(*until_ds)
        ds_fetch = fetch(r.ds_slots, r.ds_all, 7)
        ds_fetch.start()
        ds_fetch.wait()
        loop(EARLY_WIDE, lambda step: WideBlock(r, step, half).from_kept(), beside)
        last = {at - EARLY_WIDE: actions for at, actions in beside.items() if at >= EARLY_WIDE}
        loop(blocks - EARLY_WIDE, lambda step: WideBlock(r, step + EARLY_WIDE, half).whole(True), last)
    else:
        for actions in waiting:
            for act in actions:
                act()
        moves(*until_ds)
        for at in range(chunks):
            fetches = [fetch(r.normed_slots, r.normed_all, 6, at), fetch(r.ds_slots, r.ds_all, 7, at)]
            for copy in fetches:
                copy.start()
            for copy in fetches:
                copy.wait()
            loop(blocks, lambda step: WideBlock(r, step, half).whole(at == 0))
        for actions in beside.values():
            for act in actions:
                act()
    expand_store.start()
    for group in (edges_pair, grads_pair, fed_pair):
        group.wait()
    for copy in (edges_keep, grads_keep, fed_keep, state_keep):
        copy.wait()
    moves((second, 6), (first_b, 6), (first_a, 6))
    for store in stores:
        store.wait()


def shape(dims, kind):
    return jax.ShapeDtypeStruct(dims, kind)


def run(vectors, arrays):
    count = lax.axis_size("res")
    rows_dev, width = arrays.nodes.shape
    slots, _, features = arrays.edges.shape
    hidden = arrays.second_in.shape[0]
    inner = arrays.expand_in.shape[1]
    rows = rows_dev // CORES
    places = rows + 2 * REACH
    total = rows * slots
    each = slots // CORES
    tall = arrays.first_in.shape[0]
    chunks = chunk_rows(count, width, hidden, features)
    side, deep = chip_dims(count)
    everyone = CORES * count * rows
    chunk = everyone if everyone <= 16 * rows_dev else 8 * rows_dev
    outs = (
        shape((rows_dev, width // CORES), BF16),
        shape((each, rows_dev, features), BF16),
        shape((rows_dev, width // CORES), F32),
        shape((each, rows_dev, features), F32),
        shape((width // CORES, inner), F32),
        shape((inner // CORES, width), F32),
        shape((everyone, width), BF16),
        shape((everyone, width), BF16),
    ) + tuple(shape((size, LANE), BF16) for size in chunks)
    peers = 2 * (side - 1) + deep - 1
    remote = len(chunks) * (2 * peers + 1) + 2 * (peers + 1) + 3
    scratch = dict(
        windows=((3, places, width), BF16),
        neighbours_raw=((slots, rows_dev), jnp.int32),
        picks=((slots, 1, rows_dev), F32),
        counts=((rows, LANE), F32),
        bias_wide=((inner // WIDE, WIDE), F32),
        diagonal=((rows, CHAIN * rows), F32),
        lane_slot=((8, CHAIN * rows), F32),
        first=((tall, hidden), BF16),
        second_w=((hidden, hidden), BF16),
        third=((hidden, width), BF16),
        expand=((width, inner), BF16),
        reduce=((inner, width), BF16),
        e_first_t=((features, tall), BF16),
        e_second_w=((features, features), BF16),
        e_third_w=((features, features), BF16),
        edges_raw=((slots, rows, features), BF16),
        cots_raw=((slots, rows, features), BF16),
        cot_rows=((rows, width), BF16),
        onehot=((slots, rows, LANES), BF16),
        table=((LANES + features, hidden), BF16),
        e_table=((LANES + features, features), BF16),
        kept=((3 * total, hidden), BF16),
        pooled=((rows, hidden), F32),
        summed=((rows, width), F32),
        second=((rows, width), F32),
        pre_expand=((rows, inner), F32),
        normed=((rows, width), BF16),
        edge_out=((slots, rows, features), BF16),
        edge_grad=((slots, rows, features), F32),
        ge_norm=((8, features), F32),
        ge_first=((LANES + features, features), F32),
        ge_second=((features, features), F32),
        ge_third=((features, features), F32),
        ge_own=((features, width), F32),
        ge_far=((features, width), F32),
        e_own_back=((rows, width), F32),
        edge_landing=((places, features), F32),
        edge_total=((rows, features), F32),
        ds=((rows, width), BF16),
        du=((rows, width), F32),
        dm=((rows, width), BF16),
        slot_grad=((rows, hidden), F32),
        small=((16, width), F32),
        g_second=((hidden, hidden), F32),
        g_first=((LANES + features, hidden), F32),
        g_bias=((1, hidden), F32),
        node_landing=((places, hidden), F32),
        node_total=((rows, hidden), F32),
        fed_grad=((CORES, rows, width // CORES), F32),
        normed_all=((chunk, width), BF16),
        ds_all=((chunk, width), BF16),
        g_expand=((width // CORES, inner), F32),
        g_reduce=((inner // CORES, width), F32),
    )
    packed = [(CORES, size, LANE) for size in chunks] + [(size, LANE) for size in chunks] * 3
    sems = dict(load_sem=13, keep_sem=15, line_send=20, line_recv=20, step_send=remote, step_recv=remote)
    for name, size in sems.items():
        scratch[name] = pltpu.SemaphoreType.DMA((size,))
    anywhere = pl.BlockSpec(memory_space=pl.ANY)
    return pl.pallas_call(
        functools.partial(kernel, tuple(scratch), features),
        out_shape=outs,
        in_specs=[pl.BlockSpec(memory_space=pltpu.VMEM)] * len(vectors) + [anywhere] * len(arrays),
        out_specs=(anywhere,) * len(outs),
        scratch_shapes=[pltpu.VMEM(*kind) if isinstance(kind, tuple) else kind for kind in scratch.values()]
        + [pltpu.VMEM(dims, BF16) for dims in packed],
        compiler_params=pltpu.CompilerParams(
            collective_id=1, has_side_effects=True, vmem_limit_bytes=VMEM
        ),
        name="graph_layer",
    )(*vectors, *arrays)


class Moved(NamedTuple):
    grads: Any
    expand: Any
    reduce: Any
    edges: Any
    state: Any
    fed: Any


class Grads(NamedTuple):
    third_g: Any
    e_first: Any
    e_second: Any
    e_third: Any
    second_g: Any
    first_g: Any


class Biases(NamedTuple):
    b_one: Any
    b_two: Any
    b_three: Any
    gain_one: Any
    shift_one: Any
    b_expand: Any
    b_reduce: Any
    gain_two: Any
    shift_two: Any
    eb_one: Any
    eb_two: Any
    eb_three: Any
    e_gain: Any
    e_shift: Any


def finish_kernel(width, hidden, features, inner, *refs):
    refs = list(refs)
    take = lambda kind: kind(*(refs.pop(0) for _ in kind._fields))
    moved_in, packed_in = take(Moved), take(Chunks)
    moved_out, grads_out, biases = take(Moved), take(Grads), take(Biases)
    r, g, via = take(Chunks), take(Grads), take(Moved)
    sem, move_sem = refs
    half = lax.axis_index("half")
    wide = width // LANE
    tall = (2 * width + features) // CORES
    copy = pltpu.make_async_copy
    fetches = [copy(*pair, sem.at[at]) for at, pair in enumerate(zip(moved_in, via))]
    moves = [copy(*pair, move_sem.at[at]) for at, pair in enumerate(zip(via, moved_out))]
    first = len(fetches)
    loads = Chunks(*(copy(*pair, sem.at[first + at]) for at, pair in enumerate(zip(packed_in, r))))
    first += len(loads)
    stores = Grads(*(copy(*pair, sem.at[first + at]) for at, pair in enumerate(zip(g, grads_out))))
    for load in loads:
        load.start()
    for fetch in fetches:
        fetch.start()
    loads.third.wait()
    g.third_g[...], _ = take_wide(r.third, 0, hidden // CORES, wide)
    stores.third_g.start()
    loads.edge.wait()
    e_whole, at = take_wide(r.edge, 0, features, up(tall, LANE) // LANE)
    g.e_first[...] = e_whole[:, :tall]
    rest = features - LANE
    part = features // CORES
    left_two, at = take_wide(r.edge, at, part, 1)
    left_three, at = take_wide(r.edge, at, part, 1)
    right, at = take_wide(r.edge, at, part, 1)
    g.e_second[...] = jnp.concatenate([left_two, right[:, :rest]], 1)
    g.e_third[...] = jnp.concatenate([left_three, right[:, rest:]], 1)
    for store in (stores.e_first, stores.e_second, stores.e_third):
        store.start()
    for fetch, move in zip(fetches[:2], moves[:2]):
        fetch.wait()
        move.start()
    loads.second.wait()
    g.second_g[...], _ = take_wide(r.second, 0, hidden // CORES, wide)
    stores.second_g.start()
    for fetch, move in zip(fetches[2:], moves[2:]):
        fetch.wait()
        move.start()
    loads.first_a.wait()
    g.first_g[:, : hidden // 2], _ = take_wide(r.first_a, 0, tall, wide // 2)
    loads.first_b.wait()
    g.first_g[:, hidden // 2 :], at = take_wide(r.first_b, 0, tall, wide // 2)
    stores.first_g.start()
    small, _ = take_wide(r.first_b, at, 16, wide)

    def share(target, row):
        size = target.shape[0]
        target[...] = jnp.where(half == 0, row[:, :size], row[:, size : 2 * size]).reshape(size)

    b = biases
    for target, at in (
        (b.b_one, 0), (b.b_two, 1), (b.b_three, 2), (b.gain_one, 3), (b.shift_one, 4), (b.b_reduce, 9),
        (b.gain_two, 10), (b.shift_two, 11),
    ):
        share(target, small[at : at + 1])
    share(b.b_expand, jnp.concatenate([small[5 + p : 6 + p] for p in range(inner // width)], 1))
    share(b.eb_one, small[12:13, :LANES])
    share(b.eb_two, small[12:13, LANES:])
    share(b.eb_three, small[13:14, :LANES])
    share(b.e_gain, small[13:14, LANES:])
    share(b.e_shift, small[14:15, :LANES])
    for store in moves + list(stores):
        store.wait()


def finish(moved, sums, width, hidden, features, inner):
    tall = (2 * width + features) // CORES
    part = features // CORES
    grads = Grads(
        third_g=(hidden // CORES, width),
        e_first=(features, tall),
        e_second=(part, features),
        e_third=(part, features),
        second_g=(hidden // CORES, hidden),
        first_g=(tall, hidden),
    )
    sizes = Biases(hidden, hidden, width, width, width, inner, width, width, width, *[features] * 5)
    anywhere, vmem = pl.BlockSpec(memory_space=pl.ANY), pl.BlockSpec(memory_space=pltpu.VMEM)
    outs = [shape(a.shape, a.dtype) for a in moved]
    outs += [shape(dims, F32) for dims in grads]
    outs += [shape((size // CORES,), F32) for size in sizes]
    got = pl.pallas_call(
        functools.partial(finish_kernel, width, hidden, features, inner),
        out_shape=outs,
        in_specs=[anywhere] * (len(moved) + len(sums)),
        out_specs=[anywhere] * (len(moved) + len(grads)) + [vmem] * len(sizes),
        scratch_shapes=[pltpu.VMEM(a.shape, BF16) for a in sums]
        + [pltpu.VMEM(dims, F32) for dims in grads]
        + [pltpu.VMEM(a.shape, a.dtype) for a in moved]
        + [pltpu.SemaphoreType.DMA((len(moved) + len(sums) + len(grads),)), pltpu.SemaphoreType.DMA((len(moved),))],
        compiler_params=pltpu.CompilerParams(vmem_limit_bytes=VMEM),
        name="finish",
    )(*moved, *sums)
    first = len(moved) + len(grads)
    return Moved(*got[: len(moved)]), Grads(*got[len(moved) : first]), Biases(*got[first:])


def body(
    nodes, edges, neighbours, counts,
    message_first, message_first_bias, message_second, message_second_bias, message_third, message_third_bias,
    node_norm_gain, node_norm_shift, expand_weight, expand_bias, reduce_weight, reduce_bias,
    output_norm_gain, output_norm_shift,
    edge_first, edge_first_bias, edge_second, edge_second_bias, edge_third, edge_third_bias,
    edge_norm_gain, edge_norm_shift, cot_nodes, cot_edges,
):
    width, features = nodes.shape[1], edges.shape[2]
    hidden, inner = message_second.shape[0], expand_weight.shape[1]

    by_slots = lambda values: jnp.transpose(values, (1, 0, 2))
    vectors = Vectors(
        message_first_bias, message_second_bias, message_third_bias, node_norm_gain, node_norm_shift, reduce_bias,
        output_norm_gain, output_norm_shift, expand_bias, edge_first_bias, edge_second_bias, edge_third_bias,
        edge_norm_gain, edge_norm_shift, counts,
    )
    arrays = Arrays(
        nodes, by_slots(edges), neighbours.T, message_first, message_second, message_third, expand_weight,
        reduce_weight, edge_first.T, edge_second, edge_third, cot_nodes, by_slots(cot_edges),
    )
    state, out, fed_grad, edge_grad, g_expand, g_reduce, _, _, *sums = run(vectors, arrays)
    moved = Moved(edge_grad, g_expand, g_reduce, out, state, fed_grad)
    m, g, b = finish(moved, sums, width, hidden, features, inner)
    return (
        m.state, by_slots(m.edges), m.fed, by_slots(m.grads),
        g.first_g, b.b_one, g.second_g, b.b_two, g.third_g, b.b_three, b.gain_one, b.shift_one,
        m.expand, b.b_expand, m.reduce, b.b_reduce, b.gain_two, b.shift_two,
        g.e_first.T, b.eb_one, g.e_second, b.eb_two, g.e_third, b.eb_three, b.e_gain, b.e_shift,
    )


def solution(mesh):
    rows, slots = P("res", None), P("res", None, None)
    copied = P()
    down, vec = P("half", None), P("half")
    return jax.shard_map(
        body,
        mesh=mesh,
        in_specs=(rows, slots, rows, P("res")) + (copied,) * 22 + (rows, slots),
        out_specs=(
            P("res", "half"),
            P("res", "half", None),
            P("res", "half"),
            P("res", "half", None),
            down, vec, down, vec, down, vec, vec, vec, down, vec, down, vec, vec, vec,
            down, vec, down, vec, down, vec, vec, vec,
        ),
        check_vma=False,
    )
```

time: 139 us -> 104 us (0.75)
  Pallas kernels: 121 us -> 103 us
  local copies, waits for them, and re-layouts: 9.66 us -> 0 us
  other arithmetic: 6.99 us -> 0 us
    pallas_call x2, Pallas kernels: 121 us -> 103 us  [the longest x1 95 us: run(): pl.pallas_call(functools.partial(kernel, tuple(scratch), features), out_s...]
    unnamed x16 -> x0, local copies, waits for them, and re-layouts: 9.66 us -> none
    pad x7 -> x0, other arithmetic: 4.8 us -> none  [body(): line = jnp.pad(vector.astype(F32), (0, inner - vector.shape[0]))]
where the time goes in v3:
time: 104 us
  Pallas kernels  103 us (99%)
    pallas_call x1, Pallas kernels, run(): pl.pallas_call(functools.partial(kernel, tuple(scratch), features), out_s...  95 us
    pallas_call x1, Pallas kernels, finish(): pl.pallas_call(functools.partial(finish_kernel, width, hidden, features,...  8.36 us

profile of v3, /device:TPU:0, one launch (start us, length us, event | category | flops | bytes accessed | tf_op | source)
XLA Modules:
  0.0 104.2 jit_solution(15847590563373354148)
XLA Ops:
  0.7 95.0 %graph_layer.1 = (bf16[96,256]{1,0:T(8,128)(2,1)}, bf16[30,96,192]{2,1,0:T(8,128)(2,1)}, f32[96,256]{1,0:T(8,128)}, f32[30,96,192]{2,1,0:T(8,128)}, f32[256,2048...) custom-call(bf16[512]{0:T(512)(128)(2,1)} %refs_0_.1, ...), custom_call_target="tpu_custom_call" | custom-call | tf_op jit(solution)/shard_map/graph_layer/pallas_call | solution.py:1195
  95.7 8.4 %finish.1 = (f32[30,96,192]{2,1,0:T(8,128)}, f32[256,2048]{1,0:T(8,128)}, f32[1024,512]{1,0:T(8,128)}, bf16[30,96,192]{2,1,0:T(8,128)(2,1)}, bf16[96,256]{1,0:T(...) custom-call(f32[30,96,192]{2,1,0:T(8,128)} %get-tuple-element.63.ref, ...), custom_call_target="tpu_custom_call" | custom-call | tf_op jit(solution)/shard_map/finish/pallas_call | solution.py:1332

commit v4 on v3

--- a/solution.py
+++ b/solution.py
@@ -53,9 +53,10 @@
 
 
 def gelu(values):
+    kind = values.dtype.type
     square = values * values
-    bend = jnp.tanh(values * (NEAR + (NEAR * CUBE) * square))
-    return values * (0.5 + 0.5 * bend)
+    bend = jnp.tanh(values * (kind(NEAR) + kind(NEAR * CUBE) * square))
+    return values * (kind(0.5) + kind(0.5) * bend)
 
 
 def gelu_slope(values):
@@ -427,10 +428,15 @@
     return unit_two * r.gain_two + r.shift_two
 
 
-def fill_table(window, far, own, bias, table, rows, multiply):
-    places = window.shape[0]
-    table[pl.ds(0, places), :] = multiply(window[...], far).astype(BF16)
-    table[pl.ds(places, rows), :] = (multiply(window[pl.ds(REACH, rows), :], own) + bias).astype(BF16)
+def fill_own(window, far, own, bias, table, rows, multiply):
+    here = pl.ds(REACH, rows)
+    table[here, :] = multiply(window[here, :], far).astype(BF16)
+    table[pl.ds(window.shape[0], rows), :] = (multiply(window[here, :], own) + bias).astype(BF16)
+
+
+def fill_far(window, far, table, rows, multiply):
+    for here in (pl.ds(0, REACH), pl.ds(REACH + rows, REACH)):
+        table[here, :] = multiply(window[here, :], far).astype(BF16)
 
 
 def chain_parts(step):
@@ -494,7 +500,7 @@
             r.act[here, :] = act
             r.slope_one[here, :] = slope
         else:
-            act = gelu(values).astype(BF16)
+            act = gelu(values.astype(BF16))
         acts.append(act)
     pre = [dot(act, r.second_w[...]) + r.b_two for act in acts]
     total = r.pooled[...]
@@ -503,7 +509,7 @@
             act, slope = gelu_and_slope(values)
             r.slope_two[chain_rows(r, slot), :] = slope * live_rows(r, slot, hidden).astype(BF16)
         else:
-            act = gelu(values)
+            act = gelu(values.astype(BF16))
         used = jnp.where(r.lane_slot[0:1, :] + slot.astype(F32) < count, r.diagonal[...], 0.0)
         total = total + dot(used.astype(BF16), act.astype(BF16))
     r.pooled[...] = total
@@ -664,7 +670,12 @@
     here = step_rows(r, step)
     r.g_second[...] += t_dot(r.act[here, :], r.slope_two[here, :])
     more = dot_t(r.slope_one[here, :], r.table[pl.ds(LANES, features), :])
-    r.edge_grad[pl.ds(step * STEP, STEP)] += more.reshape(STEP, rows, features)
+    there = pl.ds(step * STEP, STEP)
+    r.edge_grad_low[there] = (r.edge_grad[there] + more.reshape(STEP, rows, features)).astype(BF16)
+
+
+def put(target, rows, cols, found, fresh):
+    target[rows, cols] = (found if fresh else target[rows, cols] + found).astype(target.dtype)
 
 
 class WideBlock:
@@ -709,13 +720,13 @@
         back = [dot_t(r.ds_all[rows, :], r.reduce[self.here, :]) for rows in self.rows]
         dqs = [(grad * slope.astype(F32)).astype(BF16) for grad, slope in zip(back, slopes)]
         found = t_dot(r.normed_all[:, self.cols], jnp.concatenate(dqs, 0))
-        r.g_expand[:, self.here] = found if fresh else r.g_expand[:, self.here] + found
+        put(r.g_expand, slice(None), self.here, found, fresh)
 
         @pl.when(self.step < self.mine)
         def _():
             out = pl.ds(pl.multiple_of(self.step * WIDE, WIDE), WIDE)
             found = t_dot(act(), r.ds_all[...])
-            r.g_reduce[out, :] = found if fresh else r.g_reduce[out, :] + found
+            put(r.g_reduce, out, slice(None), found, fresh)
 
     def from_kept(self):
         slopes = [self.place(self.step, rows)[...] for rows in self.rows]
@@ -791,6 +802,7 @@
     steps = slots // STEP
     r.nodes_width = width
     total = r.edges_raw.shape[0] * rows
+    r.edge_grad_low = r.cots_raw
     r.act, r.slope_one, r.slope_two = (r.kept.at[pl.ds(at * total, total)] for at in range(3))
     for name in Vectors._fields:
         vector = getattr(r, name)
@@ -850,8 +862,8 @@
     edges_pair = copies.group([(r.edge_out.at[its_slots], edges_target, place.partner)])
     edges_keep = pltpu.make_async_copy(r.edge_out.at[my_slots], edges_target, r.keep_sem.at[2])
     grads_target = r.grads_out.at[:, there, :]
-    grads_pair = copies.group([(r.edge_grad.at[its_slots], grads_target, place.partner)])
-    grads_keep = pltpu.make_async_copy(r.edge_grad.at[my_slots], grads_target, r.keep_sem.at[3])
+    grads_pair = copies.group([(r.edge_grad_low.at[its_slots], grads_target, place.partner)])
+    grads_keep = pltpu.make_async_copy(r.edge_grad_low.at[my_slots], grads_target, r.keep_sem.at[3])
     fed_pair = copies.group([(r.fed_grad.at[1 - half], r.fed_out.at[there], place.partner)])
     fed_keep = pltpu.make_async_copy(r.fed_grad.at[half], r.fed_out.at[there], r.keep_sem.at[4])
 
@@ -892,8 +904,9 @@
     loads.edges.wait()
     bias = r.b_one
     far_w, own_w = r.first[pl.ds(width, width), :], r.first[pl.ds(0, width), :]
+    fill_own(r.windows.at[0], far_w, own_w, bias, r.table, rows, dot)
     halos[0].wait()
-    fill_table(r.windows.at[0], far_w, own_w, bias, r.table, rows, dot)
+    fill_far(r.windows.at[0], far_w, r.table, rows, dot)
     r.pooled[...] = jnp.zeros(r.pooled.shape, F32)
     loads.second.wait()
 
@@ -910,8 +923,9 @@
     halos[1].start()
     loads.cot_edges.wait()
     loads.cot_nodes.wait()
+    fill_own(r.windows.at[1], far_w, own_w, bias, r.table, rows, dot)
     halos[1].wait()
-    fill_table(r.windows.at[1], far_w, own_w, bias, r.table, rows, dot)
+    fill_far(r.windows.at[1], far_w, r.table, rows, dot)
     r.pooled[...] = jnp.zeros(r.pooled.shape, F32)
 
     def second_pass(step, carry):
@@ -926,9 +940,10 @@
     normed_gather[0].start()
     for ref in (r.ge_norm, r.ge_first, r.ge_second, r.ge_third, r.g_second, r.g_first, r.g_bias):
         ref[...] = jnp.zeros(ref.shape, F32)
+    e_own, e_far = r.e_first_t[:, pl.ds(0, width)], r.e_first_t[:, pl.ds(width, width)]
+    fill_own(r.windows.at[2], e_far, e_own, r.eb_one, r.e_table, rows, dot_t)
     halos[2].wait()
-    e_own, e_far = r.e_first_t[:, pl.ds(0, width)], r.e_first_t[:, pl.ds(width, width)]
-    fill_table(r.windows.at[2], e_far, e_own, r.eb_one, r.e_table, rows, dot_t)
+    fill_far(r.windows.at[2], e_far, r.e_table, rows, dot_t)
     state_keep = pltpu.make_async_copy(
         r.windows.at[
             2,
@@ -1120,13 +1135,14 @@
     side, deep = chip_dims(count)
     everyone = CORES * count * rows
     chunk = everyone if everyone <= 16 * rows_dev else 8 * rows_dev
+    wide_kind = BF16 if chunk == everyone else F32
     outs = (
         shape((rows_dev, width // CORES), BF16),
         shape((each, rows_dev, features), BF16),
         shape((rows_dev, width // CORES), F32),
-        shape((each, rows_dev, features), F32),
-        shape((width // CORES, inner), F32),
-        shape((inner // CORES, width), F32),
+        shape((each, rows_dev, features), BF16),
+        shape((width // CORES, inner), wide_kind),
+        shape((inner // CORES, width), wide_kind),
         shape((everyone, width), BF16),
         shape((everyone, width), BF16),
     ) + tuple(shape((size, LANE), BF16) for size in chunks)
@@ -1184,8 +1200,8 @@
         fed_grad=((CORES, rows, width // CORES), F32),
         normed_all=((chunk, width), BF16),
         ds_all=((chunk, width), BF16),
-        g_expand=((width // CORES, inner), F32),
-        g_reduce=((inner // CORES, width), F32),
+        g_expand=((width // CORES, inner), wide_kind),
+        g_reduce=((inner // CORES, width), wide_kind),
     )
     packed = [(CORES, size, LANE) for size in chunks] + [(size, LANE) for size in chunks] * 3
     sems = dict(load_sem=13, keep_sem=15, line_send=20, line_recv=20, step_send=remote, step_recv=remote)
@@ -1246,14 +1262,16 @@
     take = lambda kind: kind(*(refs.pop(0) for _ in kind._fields))
     moved_in, packed_in = take(Moved), take(Chunks)
     moved_out, grads_out, biases = take(Moved), take(Grads), take(Biases)
-    r, g, via = take(Chunks), take(Grads), take(Moved)
+    r, g, via, ready = take(Chunks), take(Grads), take(Moved), take(Moved)
     sem, move_sem = refs
     half = lax.axis_index("half")
     wide = width // LANE
     tall = (2 * width + features) // CORES
     copy = pltpu.make_async_copy
     fetches = [copy(*pair, sem.at[at]) for at, pair in enumerate(zip(moved_in, via))]
-    moves = [copy(*pair, move_sem.at[at]) for at, pair in enumerate(zip(via, moved_out))]
+    moves = [
+        copy(a if a.dtype == c.dtype else b, c, move_sem.at[at]) for at, (a, b, c) in enumerate(zip(via, ready, moved_out))
+    ]
     first = len(fetches)
     loads = Chunks(*(copy(*pair, sem.at[first + at]) for at, pair in enumerate(zip(packed_in, r))))
     first += len(loads)
@@ -1262,6 +1280,13 @@
         load.start()
     for fetch in fetches:
         fetch.start()
+
+    def move_on(at):
+        fetches[at].wait()
+        if via[at].dtype != ready[at].dtype:
+            ready[at][...] = via[at][...].astype(ready[at].dtype)
+        moves[at].start()
+
     loads.third.wait()
     g.third_g[...], _ = take_wide(r.third, 0, hidden // CORES, wide)
     stores.third_g.start()
@@ -1277,15 +1302,13 @@
     g.e_third[...] = jnp.concatenate([left_three, right[:, rest:]], 1)
     for store in (stores.e_first, stores.e_second, stores.e_third):
         store.start()
-    for fetch, move in zip(fetches[:2], moves[:2]):
-        fetch.wait()
-        move.start()
+    for at in range(2):
+        move_on(at)
     loads.second.wait()
     g.second_g[...], _ = take_wide(r.second, 0, hidden // CORES, wide)
     stores.second_g.start()
-    for fetch, move in zip(fetches[2:], moves[2:]):
-        fetch.wait()
-        move.start()
+    for at in range(2, len(fetches)):
+        move_on(at)
     loads.first_a.wait()
     g.first_g[:, : hidden // 2], _ = take_wide(r.first_a, 0, tall, wide // 2)
     loads.first_b.wait()
@@ -1326,7 +1349,8 @@
     )
     sizes = Biases(hidden, hidden, width, width, width, inner, width, width, width, *[features] * 5)
     anywhere, vmem = pl.BlockSpec(memory_space=pl.ANY), pl.BlockSpec(memory_space=pltpu.VMEM)
-    outs = [shape(a.shape, a.dtype) for a in moved]
+    kinds = Moved(F32, F32, F32, BF16, BF16, F32)
+    outs = [shape(a.shape, kind) for a, kind in zip(moved, kinds)]
     outs += [shape(dims, F32) for dims in grads]
     outs += [shape((size // CORES,), F32) for size in sizes]
     got = pl.pallas_call(
@@ -1337,6 +1361,7 @@
         scratch_shapes=[pltpu.VMEM(a.shape, BF16) for a in sums]
         + [pltpu.VMEM(dims, F32) for dims in grads]
         + [pltpu.VMEM(a.shape, a.dtype) for a in moved]
+        + [pltpu.VMEM(a.shape if a.dtype != kind else (16, LANE), kind) for a, kind in zip(moved, kinds)]
         + [pltpu.SemaphoreType.DMA((len(moved) + len(sums) + len(grads),)), pltpu.SemaphoreType.DMA((len(moved),))],
         compiler_params=pltpu.CompilerParams(vmem_limit_bytes=VMEM),
         name="finish",

time: 104 us -> 102 us (0.981)
  Pallas kernels: 103 us -> 101 us
    pallas_call x1, Pallas kernels: 8.36 us -> 6.88 us  [finish(): pl.pallas_call(functools.partial(finish_kernel, width, hidden, features,...]
where the time goes in v4:
time: 102 us
  Pallas kernels  101 us (99%)
    pallas_call x1, Pallas kernels, run(): pl.pallas_call(functools.partial(kernel, tuple(scratch), features), out_s...  94 us
    pallas_call x1, Pallas kernels, finish(): pl.pallas_call(functools.partial(finish_kernel, width, hidden, features,...  6.88 us

profile of v4, /device:TPU:0, one launch (start us, length us, event | category | flops | bytes accessed | tf_op | source)
XLA Modules:
  0.0 101.7 jit_solution(12248203464020240698)
XLA Ops:
  0.7 94.0 %graph_layer.1 = (bf16[96,256]{1,0:T(8,128)(2,1)}, bf16[30,96,192]{2,1,0:T(8,128)(2,1)}, f32[96,256]{1,0:T(8,128)}, bf16[30,96,192]{2,1,0:T(8,128)(2,1)}, bf16[2...) custom-call(bf16[512]{0:T(512)(128)(2,1)} %refs_0_.1, ...), custom_call_target="tpu_custom_call" | custom-call | tf_op jit(solution)/shard_map/graph_layer/pallas_call | solution.py:1211
  94.7 6.9 %finish.1 = (f32[30,96,192]{2,1,0:T(8,128)}, f32[256,2048]{1,0:T(8,128)}, f32[1024,512]{1,0:T(8,128)}, bf16[30,96,192]{2,1,0:T(8,128)(2,1)}, bf16[96,256]{1,0:T(...) custom-call(bf16[30,96,192]{2,1,0:T(8,128)(2,1)} %get-tuple-element., ...), custom_call_target="tpu_custom_call" | custom-call | tf_op jit(solution)/shard_map/finish/pallas_call | solution.py:1356

commit v5 on v4

--- a/solution.py
+++ b/solution.py
@@ -298,15 +298,16 @@
 
 
 class Returns:
-    def __init__(self, place, table, landing, rows, send, recv, first):
+    def __init__(self, place, table, outgoing, landing, rows, send, recv, first):
         self.place, self.table, self.landing, self.rows = place, table, landing, rows
+        self.outgoing = outgoing
         self.send, self.recv, self.first = send, recv, first
 
     def _copy(self, at, device):
         layout = halo_layout(self.rows)
         offset, size = layout[at]
         return pltpu.make_async_remote_copy(
-            src_ref=self.table.at[pl.ds(offset, size)],
+            src_ref=self.outgoing.at[pl.ds(offset, size)],
             dst_ref=self.landing.at[pl.ds(layout[3 - at][0], size)],
             send_sem=self.send.at[self.first + at],
             recv_sem=self.recv.at[self.first + 3 - at],
@@ -315,6 +316,7 @@
         )
 
     def start(self):
+        self.outgoing[...] = self.table[pl.ds(0, self.outgoing.shape[0]), :].astype(BF16)
         for at, (exists, device) in enumerate(self.place.line()):
 
             @pl.when(exists)
@@ -331,14 +333,14 @@
             def _():
                 self._copy(at, device).wait_send()
                 pltpu.make_async_remote_copy(
-                    src_ref=self.table.at[pl.ds(offset, size)],
+                    src_ref=self.outgoing.at[pl.ds(offset, size)],
                     dst_ref=self.landing.at[pl.ds(offset, size)],
                     send_sem=self.send.at[self.first + at],
                     recv_sem=self.recv.at[self.first + at],
                     device_id=device,
                     device_id_type=MESH,
                 ).wait_recv()
-                total[pl.ds(first, size), :] += self.landing[pl.ds(offset, size), :]
+                total[pl.ds(first, size), :] += self.landing[pl.ds(offset, size), :].astype(F32)
 
 
 def gather_groups(place, copies, ref, unit, source=None, base=0):
@@ -355,7 +357,7 @@
 
 
 class ChipSum:
-    def __init__(self, place, copies, order, pack, got, landed, gathered):
+    def __init__(self, place, copies, order, pack, got, landed, gathered, out, keep_sem):
         self.place, self.pack, self.got, self.landed, self.gathered = place, pack, got, landed, gathered
         half, size = place.half, pack.shape[1]
         self.pair = copies.group([(pack.at[1 - half], got, place.partner)])
@@ -374,8 +376,11 @@
             self.steps.append(copies.group(entries))
             self.shares.append((start, share, lands))
             here = gathered.at[pl.ds(start, share)]
-            back = [(here, here, device) for _, device in place.peers(level)]
+            there = here if self.back else out.at[pl.ds(start, share)]
+            back = [(here, there, device) for _, device in place.peers(level)]
             self.back.insert(0, copies.group(back))
+            if there is not here:
+                self.keep = pltpu.make_async_copy(here, there, keep_sem)
 
     def send_pair(self):
         self.pair.start()
@@ -402,9 +407,13 @@
 
     def start_back(self, step):
         self.back[step].start()
+        if step == len(self.back) - 1:
+            self.keep.start()
 
     def finish_back(self, step):
         self.back[step].wait()
+        if step == len(self.back) - 1:
+            self.keep.wait()
 
 
 def flat(values):
@@ -633,17 +642,21 @@
     return jnp.concatenate(lines + [jnp.zeros((1, r.small.shape[1]), F32)], 0)
 
 
-def pack_first(r, packs, g_own, g_far, features, small):
-    pieces = [g_own, g_far, r.g_first[pl.ds(LANES, features), :]]
+def pack_first(r, side, pack, window, spread, own_spread, own, features, places):
+    hidden = own_spread.shape[1]
+    cols = slice(side * (hidden // 2), (side + 1) * (hidden // 2))
+    pieces = [
+        t_dot(window[own, :], own_spread[:, cols].astype(BF16)),
+        t_dot(window[...], spread[:, cols].astype(BF16)),
+        r.g_first[pl.ds(LANES, features), cols],
+    ]
     tall = sum(piece.shape[0] for piece in pieces) // CORES
-    hidden = g_own.shape[1]
-    for side, pack in enumerate(packs):
-        cols = slice(side * (hidden // 2), (side + 1) * (hidden // 2))
-        for half in range(CORES):
-            at = put_wide(pack, half, 0, cut([piece[:, cols] for piece in pieces], half * tall, (half + 1) * tall))
-            if side == 1:
-                at = put_wide(pack, half, at, small)
-        put_rest(pack, at)
+    small = small_rows(r, places) if side == 1 else None
+    for half in range(CORES):
+        at = put_wide(pack, half, 0, cut(pieces, half * tall, (half + 1) * tall))
+        if side == 1:
+            at = put_wide(pack, half, at, small)
+    put_rest(pack, at)
 
 
 def first_grad_block(r, step, features):
@@ -834,11 +847,14 @@
     halos = [
         Halo(place, r.windows.at[k], rows, r.line_send, r.line_recv, 4 * k) for k in range(3)
     ]
-    edge_returns = Returns(place, r.ge_first, r.edge_landing, rows, r.line_send, r.line_recv, 12)
-    node_returns = Returns(place, r.g_first, r.node_landing, rows, r.line_send, r.line_recv, 16)
+    edge_returns = Returns(place, r.ge_first, r.edge_outgoing, r.edge_landing, rows, r.line_send, r.line_recv, 12)
+    node_returns = Returns(place, r.g_first, r.node_outgoing, r.node_landing, rows, r.line_send, r.line_recv, 16)
     copies = Copies(r.step_send, r.step_recv)
     edge, third, first_a, first_b, second = sums = Chunks(
-        *(ChipSum(place, copies, *parts) for parts in zip(ORDERS, r.pack, r.got, r.landed, r.gathered))
+        *(
+            ChipSum(place, copies, *parts, r.keep_sem.at[10 + at])
+            for at, parts in enumerate(zip(ORDERS, r.pack, r.got, r.landed, r.gathered, r.sums_out))
+        )
     )
     span = count * rows
 
@@ -986,10 +1002,8 @@
     edges_pair.start()
     r.e_own_back[...] = dot_wide(own_spread, e_own)
 
-    outs = [(r.g_expand, r.expand_out), (r.g_reduce, r.reduce_out)] + list(zip(r.gathered, r.sums_out))
-    stores = [pltpu.make_async_copy(*pair, r.keep_sem.at[8 + at]) for at, pair in enumerate(outs)]
-    expand_store, reduce_store = stores[:2]
-    sum_stores = dict(zip(sums, stores[2:]))
+    expand_store = pltpu.make_async_copy(r.g_expand, r.expand_out, r.keep_sem.at[8])
+    reduce_store = pltpu.make_async_copy(r.g_reduce, r.reduce_out, r.keep_sem.at[9])
 
     def move(chunk, at):
         if at == 0:
@@ -1006,7 +1020,6 @@
             chunk.start_back(at - 3)
         else:
             chunk.finish_back(2)
-            sum_stores[chunk].start()
 
     def ahead(groups, at):
         groups[at].wait()
@@ -1034,11 +1047,10 @@
     node_returns.start()
     moves((normed_gather, 2))
     own_spread = r.g_first[pl.ds(places, rows), :]
-    g_own = t_dot(r.windows[1, own, :], own_spread.astype(BF16))
-    g_far = t_dot(r.windows[1], r.g_first[pl.ds(0, places), :].astype(BF16))
-    pack_first(r, (r.pack.first_a, r.pack.first_b), g_own, g_far, features, small_rows(r, places))
-    first_a.send_pair()
-    first_b.send_pair()
+    spread = r.g_first[pl.ds(0, places), :]
+    for side, chunk_sum in enumerate((first_a, first_b)):
+        pack_first(r, side, chunk_sum.pack, r.windows.at[1], spread, own_spread, own, features, places)
+        chunk_sum.send_pair()
     moves((edge, 1))
     ds_keep.wait()
     moves((ds_gather, 0))
@@ -1112,8 +1124,8 @@
     for copy in (edges_keep, grads_keep, fed_keep, state_keep):
         copy.wait()
     moves((second, 6), (first_b, 6), (first_a, 6))
-    for store in stores:
-        store.wait()
+    expand_store.wait()
+    reduce_store.wait()
 
 
 def shape(dims, kind):
@@ -1185,7 +1197,8 @@
         ge_own=((features, width), F32),
         ge_far=((features, width), F32),
         e_own_back=((rows, width), F32),
-        edge_landing=((places, features), F32),
+        edge_outgoing=((places, features), BF16),
+        edge_landing=((places, features), BF16),
         edge_total=((rows, features), F32),
         ds=((rows, width), BF16),
         du=((rows, width), F32),
@@ -1195,7 +1208,8 @@
         g_second=((hidden, hidden), F32),
         g_first=((LANES + features, hidden), F32),
         g_bias=((1, hidden), F32),
-        node_landing=((places, hidden), F32),
+        node_outgoing=((places, hidden), BF16),
+        node_landing=((places, hidden), BF16),
         node_total=((rows, hidden), F32),
         fed_grad=((CORES, rows, width // CORES), F32),
         normed_all=((chunk, width), BF16),

time: 102 us -> 101 us (level)
  Pallas kernels: 101 us -> 99.5 us
    pallas_call x1, Pallas kernels: 94 us -> 92.7 us  [run(): pl.pallas_call(functools.partial(kernel, tuple(scratch), features), out_s...]
where the time goes in v5:
time: 101 us; the launch traced here: 100 us
  Pallas kernels  99.5 us (99%)
    pallas_call x1, Pallas kernels, run(): pl.pallas_call(functools.partial(kernel, tuple(scratch), features), out_s...  92.7 us
    pallas_call x1, Pallas kernels, finish(): pl.pallas_call(functools.partial(finish_kernel, width, hidden, features,...  6.88 us

profile of v5, /device:TPU:0, one launch (start us, length us, event | category | flops | bytes accessed | tf_op | source)
XLA Modules:
  0.0 100.4 jit_solution(3275069331323894136)
XLA Ops:
  0.7 92.7 %graph_layer.1 = (bf16[96,256]{1,0:T(8,128)(2,1)}, bf16[30,96,192]{2,1,0:T(8,128)(2,1)}, f32[96,256]{1,0:T(8,128)}, bf16[30,96,192]{2,1,0:T(8,128)(2,1)}, bf16[2...) custom-call(bf16[512]{0:T(512)(128)(2,1)} %refs_0_.1, ...), custom_call_target="tpu_custom_call" | custom-call | tf_op jit(solution)/shard_map/graph_layer/pallas_call | solution.py:1225
  93.3 6.9 %finish.1 = (f32[30,96,192]{2,1,0:T(8,128)}, f32[256,2048]{1,0:T(8,128)}, f32[1024,512]{1,0:T(8,128)}, bf16[30,96,192]{2,1,0:T(8,128)(2,1)}, bf16[96,256]{1,0:T(...) custom-call(bf16[30,96,192]{2,1,0:T(8,128)(2,1)} %get-tuple-element., ...), custom_call_target="tpu_custom_call" | custom-call | tf_op jit(solution)/shard_map/finish/pallas_call | solution.py:1370

commit v6 on v5

--- a/solution.py
+++ b/solution.py
@@ -16,7 +16,7 @@
 CUBE = 0.044715
 STEP = 30
 CHAIN = 5
-BACK_CHAIN = 15
+BACK_CHAIN = 30
 EDGE_CHAIN = 15
 EARLY_WIDE = 6
 PARTS = 2
@@ -114,7 +114,7 @@
     second: Any
 
 
-ORDERS = Chunks((0, 2, 1), (0, 1, 2), (2, 0, 1), (0, 1, 2), (0, 2, 1))
+ORDERS = Chunks((0, 2, 1), (0, 1, 2), (2, 0, 1), (0, 1, 2), (0, 1, 2))
 
 
 def chunk_rows(count, width, hidden, features):

time: 101 us -> 99.7 us (0.987)
  no operation moved by 1% of the time
where the time goes in v6:
time: 99.7 us; the launch traced here: 99.5 us
  Pallas kernels  98.6 us (99%)
    pallas_call x1, Pallas kernels, run(): pl.pallas_call(functools.partial(kernel, tuple(scratch), features), out_s...  91.8 us
    pallas_call x1, Pallas kernels, finish(): pl.pallas_call(functools.partial(finish_kernel, width, hidden, features,...  6.88 us

profile of v6, /device:TPU:0, one launch (start us, length us, event | category | flops | bytes accessed | tf_op | source)
XLA Modules:
  0.0 99.5 jit_solution(18149045882461637659)
XLA Ops:
  0.7 91.8 %graph_layer.1 = (bf16[96,256]{1,0:T(8,128)(2,1)}, bf16[30,96,192]{2,1,0:T(8,128)(2,1)}, f32[96,256]{1,0:T(8,128)}, bf16[30,96,192]{2,1,0:T(8,128)(2,1)}, bf16[2...) custom-call(bf16[512]{0:T(512)(128)(2,1)} %refs_0_.1, ...), custom_call_target="tpu_custom_call" | custom-call | tf_op jit(solution)/shard_map/graph_layer/pallas_call | solution.py:1225
  92.5 6.9 %finish.1 = (f32[30,96,192]{2,1,0:T(8,128)}, f32[256,2048]{1,0:T(8,128)}, f32[1024,512]{1,0:T(8,128)}, bf16[30,96,192]{2,1,0:T(8,128)(2,1)}, bf16[96,256]{1,0:T(...) custom-call(bf16[30,96,192]{2,1,0:T(8,128)(2,1)} %get-tuple-element., ...), custom_call_target="tpu_custom_call" | custom-call | tf_op jit(solution)/shard_map/finish/pallas_call | solution.py:1370
